TPU v7x, 32 devices: a whole 2x2x4 slice. The times are simulated.
32 devices in a mesh: rows: 8 (over z, x), seg: 4 (over y, core).
Axes of the slice: x: 2, y: 2, z: 4, core: 2. Of those that a mesh axis runs over, the one named last changes fastest.
Arguments:
- tokens: bfloat16 [24576, 1152], P(('rows', 'seg')), may hold values from -4 to 4
- condition: bfloat16 [32, 4, 1152], P(('rows', 'seg')), may hold values from -4 to 4
- segment_ids: int32 [32, 768], P(('rows', 'seg')), may hold values from 0 to 3, never falling along the last dimension, each value on 1 to 256 neighbouring positions
- cotangent: bfloat16 [24576, 1152], P(('rows', 'seg')), may hold values from -4 to 4
- modulation_master: float32 [1152, 6912], P('rows'), may hold values from -0.1875 to 0.1875
- modulation_first: float32 [1152, 6912], P('rows'), may hold values from -31.353468 to 31.353468
- modulation_second: float32 [1152, 6912], P('rows'), may hold values from 1.96608 to 31.45728
- attention_master: float32 [1152, 3456], P('rows'), may hold values from -0.1875 to 0.1875
- attention_first: float32 [1152, 3456], P('rows'), may hold values from -31.353468 to 31.353468
- attention_second: float32 [1152, 3456], P('rows'), may hold values from 1.96608 to 31.45728
- projection_master: float32 [1152, 1152], P('rows'), may hold values from -0.5 to 0.5
- projection_first: float32 [1152, 1152], P('rows'), may hold values from -31.353468 to 31.353468
- projection_second: float32 [1152, 1152], P('rows'), may hold values from 1.96608 to 31.45728
- expand_master: float32 [1152, 4608], P('rows'), may hold values from -0.1875 to 0.1875
- expand_first: float32 [1152, 4608], P('rows'), may hold values from -31.353468 to 31.353468
- expand_second: float32 [1152, 4608], P('rows'), may hold values from 1.96608 to 31.45728
- contract_master: float32 [4608, 1152], P('rows'), may hold values from -0.09375 to 0.09375
- contract_first: float32 [4608, 1152], P('rows'), may hold values from -31.353468 to 31.353468
- contract_second: float32 [4608, 1152], P('rows'), may hold values from 1.96608 to 31.45728
- bias_master: float32 [16128], P('rows'), may hold values from -0.6 to 0.6
- bias_first: float32 [16128], P('rows'), may hold values from -31.353468 to 31.353468
- bias_second: float32 [16128], P('rows'), may hold values from 1.96608 to 31.45728
Outputs:
- output: bfloat16 [24576, 1152], P(('rows', 'seg'))
- back_tokens: bfloat16 [24576, 1152], P(('rows', 'seg'))
- modulation_new: float32 [1152, 6912], P('rows')
- modulation_first_new: float32 [1152, 6912], P('rows')
- modulation_second_new: float32 [1152, 6912], P('rows')
- attention_new: float32 [1152, 3456], P('rows')
- attention_first_new: float32 [1152, 3456], P('rows')
- attention_second_new: float32 [1152, 3456], P('rows')
- projection_new: float32 [1152, 1152], P('rows')
- projection_first_new: float32 [1152, 1152], P('rows')
- projection_second_new: float32 [1152, 1152], P('rows')
- expand_new: float32 [1152, 4608], P('rows')
- expand_first_new: float32 [1152, 4608], P('rows')
- expand_second_new: float32 [1152, 4608], P('rows')
- contract_new: float32 [4608, 1152], P('rows')
- contract_first_new: float32 [4608, 1152], P('rows')
- contract_second_new: float32 [4608, 1152], P('rows')
- bias_new: float32 [16128], P('rows')
- bias_first_new: float32 [16128], P('rows')
- bias_second_new: float32 [16128], P('rows')
Inputs may be any that keep to these rules, and one draw needn't show every extreme that they name: `segment_ids`: within each row part the ids never fall and every id occurs; a segment holds 1 to 256 tokens, and one segment of each part exactly 256.
All inputs are finite; a program needn't handle non-finite values.
Results may differ from a plain program's by a relative error of at most 0.013.
The roundings to bfloat16 on the way count: a program that leaves them out, or rounds other values in their place, can miss the bound.
Values may be sent and summed in bfloat16 or wider, within the bound.
A program may use at most 248 MiB of HBM per device.

v0:
```python
from functools import partial

import jax
import jax.numpy as jnp
from jax import lax
from jax.sharding import PartitionSpec as P

HEAD_DIM = 72
STEP = 10


highest = lax.Precision.HIGHEST
beta_first = 0.9
beta_second = 0.999
learning = 0.06
weight_decay = 0.1
adam_epsilon = 1e-08
norm_epsilon = 1e-06


def layer_norm(values):
    center = values - jnp.mean(values, axis=-1, keepdims=True)
    inverse = lax.rsqrt(jnp.mean(center * center, axis=-1, keepdims=True) + norm_epsilon)
    return (center * inverse, inverse)


def norm_back(upstream, normed, inverse):
    return inverse * (
        upstream
        - jnp.mean(upstream, axis=-1, keepdims=True)
        - normed * jnp.mean(upstream * normed, axis=-1, keepdims=True)
    )


def split_bias(biases, width, hidden):
    edges = [
        0,
        width,
        2 * width,
        3 * width,
        3 * width + hidden,
        4 * width + hidden,
        10 * width + hidden,
    ]
    return [biases[edges[number] : edges[number + 1]] for number in range(6)]


def outer(left, right, precision=None):
    return lax.dot_general(
        left,
        right,
        (((0,), (0,)), ((), ())),
        precision=precision,
        preferred_element_type=jnp.float32,
    )


def back_dot(left, right):
    return lax.dot_general(
        left, right, (((1,), (1,)), ((), ())), preferred_element_type=jnp.float32
    )


def to_heads(values):
    return values.reshape(values.shape[0], -1, HEAD_DIM).transpose(1, 0, 2)


def from_heads(values):
    return values.transpose(1, 0, 2).reshape(values.shape[1], -1)


def soft_weights(same, query, key):
    scores = back_dot(query, key) * HEAD_DIM ** (-0.5)
    scores = jnp.where(same, scores, -1e30)
    powers = jnp.exp(scores - jnp.max(scores, axis=-1, keepdims=True))
    return powers / jnp.sum(powers, axis=-1, keepdims=True)


def attend_head(same, operands):
    query, key, value = operands
    softened = soft_weights(same, query, key).astype(jnp.bfloat16)
    return jnp.dot(softened, value, preferred_element_type=jnp.float32).astype(jnp.bfloat16)


def head_back(same, operands):
    query, key, value, upstream = operands
    softened = soft_weights(same, query, key)
    back_value = outer(softened.astype(jnp.bfloat16), upstream)
    back_soft = back_dot(upstream, value)
    back_score = (
        softened * (back_soft - jnp.sum(back_soft * softened, axis=-1, keepdims=True))
    ).astype(jnp.bfloat16)
    scale = HEAD_DIM ** (-0.5)
    back_query = jnp.dot(back_score, key, preferred_element_type=jnp.float32) * scale
    back_key = outer(back_score, query) * scale
    return (
        back_query.astype(jnp.bfloat16),
        back_key.astype(jnp.bfloat16),
        back_value.astype(jnp.bfloat16),
    )


def forward(tokens_wide, cond_silu, onehot, same, weights):
    (
        modulation_weight,
        attention_weight,
        projection_weight,
        expand_weight,
        contract_weight,
        biases,
    ) = weights
    width = attention_weight.shape[0]
    query_bias, value_bias, projection_bias, expand_bias, contract_bias, modulation_bias = (
        split_bias(biases.astype(jnp.float32), width, expand_weight.shape[1])
    )
    modulation = (
        jnp.dot(cond_silu, modulation_weight, preferred_element_type=jnp.float32) + modulation_bias
    )
    per_token = jnp.dot(onehot, modulation, precision=highest)
    shift_one, scale_one, gate_one, shift_two, scale_two, gate_two = jnp.split(per_token, 6, axis=1)
    normed_one, inverse_one = layer_norm(tokens_wide)
    hidden_one = (normed_one * (1.0 + scale_one) + shift_one).astype(jnp.bfloat16)
    triple = jnp.dot(hidden_one, attention_weight, preferred_element_type=jnp.float32)
    query = (triple[:, :width] + query_bias).astype(jnp.bfloat16)
    key = triple[:, width : 2 * width].astype(jnp.bfloat16)
    value = (triple[:, 2 * width :] + value_bias).astype(jnp.bfloat16)
    heads = (to_heads(query), to_heads(key), to_heads(value))
    attended = from_heads(lax.map(partial(attend_head, same), heads))
    projected = (
        jnp.dot(attended, projection_weight, preferred_element_type=jnp.float32) + projection_bias
    )
    middle = tokens_wide + gate_one * projected
    normed_two, inverse_two = layer_norm(middle)
    hidden_two = (normed_two * (1.0 + scale_two) + shift_two).astype(jnp.bfloat16)
    before = jnp.dot(hidden_two, expand_weight, preferred_element_type=jnp.float32) + expand_bias
    activated = jax.nn.gelu(before, approximate=True).astype(jnp.bfloat16)
    feedforward = (
        jnp.dot(activated, contract_weight, preferred_element_type=jnp.float32) + contract_bias
    )
    output = middle + gate_two * feedforward
    saved = (
        per_token,
        normed_one,
        inverse_one,
        hidden_one,
        heads,
        attended,
        projected,
        normed_two,
        inverse_two,
        hidden_two,
        before,
        activated,
        feedforward,
    )
    return (output, saved)


def backward(saved, weights, upstream, cond_silu, onehot, same):
    (
        modulation_weight,
        attention_weight,
        projection_weight,
        expand_weight,
        contract_weight,
        biases,
    ) = weights
    (
        per_token,
        normed_one,
        inverse_one,
        hidden_one,
        heads,
        attended,
        projected,
        normed_two,
        inverse_two,
        hidden_two,
        before,
        activated,
        feedforward,
    ) = saved
    width = attention_weight.shape[0]
    shift_one, scale_one, gate_one, shift_two, scale_two, gate_two = jnp.split(per_token, 6, axis=1)
    back_gate_two = upstream * feedforward
    back_feed = (upstream * gate_two).astype(jnp.bfloat16)
    back_active = back_dot(back_feed, contract_weight)
    gelu_pull = jax.vjp(partial(jax.nn.gelu, approximate=True), before)[1]
    back_before = gelu_pull(back_active)[0].astype(jnp.bfloat16)
    back_hidden_two = back_dot(back_before, expand_weight)
    back_middle = upstream + norm_back(back_hidden_two * (1.0 + scale_two), normed_two, inverse_two)
    back_gate_one = back_middle * projected
    back_project = (back_middle * gate_one).astype(jnp.bfloat16)
    back_attend = back_dot(back_project, projection_weight).astype(jnp.bfloat16)
    back_heads = lax.map(partial(head_back, same), heads + (to_heads(back_attend),))
    back_triple = jnp.concatenate([from_heads(part) for part in back_heads], axis=1)
    back_hidden_one = back_dot(back_triple, attention_weight)
    back_tokens = back_middle + norm_back(
        back_hidden_one * (1.0 + scale_one), normed_one, inverse_one
    )
    back_per_token = jnp.concatenate(
        [
            back_hidden_one,
            back_hidden_one * normed_one,
            back_gate_one,
            back_hidden_two,
            back_hidden_two * normed_two,
            back_gate_two,
        ],
        axis=1,
    )
    back_modulation = outer(onehot, back_per_token, highest)
    wide_triple = back_triple.astype(jnp.float32)
    bias_gradient = jnp.concatenate(
        [
            jnp.sum(wide_triple[:, :width], axis=0),
            jnp.sum(wide_triple[:, 2 * width :], axis=0),
            jnp.sum(back_project.astype(jnp.float32), axis=0),
            jnp.sum(back_before.astype(jnp.float32), axis=0),
            jnp.sum(back_feed.astype(jnp.float32), axis=0),
            jnp.sum(back_modulation, axis=0),
        ]
    )
    gradients = (
        outer(cond_silu.astype(jnp.float32), back_modulation, highest),
        outer(hidden_one, back_triple),
        outer(attended, back_project),
        outer(hidden_two, back_before),
        outer(activated, back_feed),
        bias_gradient,
    )
    return (back_tokens, gradients)


def adam_update(gradient, master, first, second):
    first_new = beta_first * first + (1.0 - beta_first) * gradient
    second_new = beta_second * second + (1.0 - beta_second) * gradient * gradient
    first_hat = first_new / (1.0 - beta_first**STEP)
    second_hat = second_new / (1.0 - beta_second**STEP)
    master_new = master - learning * (
        first_hat / (jnp.sqrt(second_hat) + adam_epsilon) + weight_decay * master
    )
    return (master_new, first_new, second_new)


def on_device(
    tokens,
    condition,
    segment_ids,
    cotangent,
    modulation_master,
    modulation_first,
    modulation_second,
    attention_master,
    attention_first,
    attention_second,
    projection_master,
    projection_first,
    projection_second,
    expand_master,
    expand_first,
    expand_second,
    contract_master,
    contract_first,
    contract_second,
    bias_master,
    bias_first,
    bias_second,
):
    segments = segment_ids[0]
    onehot = (segments[:, None] == jnp.arange(condition.shape[1], dtype=jnp.int32)[None, :]).astype(
        jnp.float32
    )
    same = segments[:, None] == segments[None, :]
    cond_silu = jax.nn.silu(condition[0].astype(jnp.float32)).astype(jnp.bfloat16)
    tokens_wide = tokens.astype(jnp.float32)
    weights = (
        lax.all_gather(modulation_master.astype(jnp.bfloat16), "rows", axis=0, tiled=True),
        lax.all_gather(attention_master.astype(jnp.bfloat16), "rows", axis=0, tiled=True),
        lax.all_gather(projection_master.astype(jnp.bfloat16), "rows", axis=0, tiled=True),
        lax.all_gather(expand_master.astype(jnp.bfloat16), "rows", axis=0, tiled=True),
        lax.all_gather(contract_master.astype(jnp.bfloat16), "rows", axis=0, tiled=True),
        lax.all_gather(bias_master.astype(jnp.bfloat16), "rows", axis=0, tiled=True),
    )
    output, saved = forward(tokens_wide, cond_silu, onehot, same, weights)
    weights_back = (
        lax.all_gather(modulation_master.astype(jnp.bfloat16), "rows", axis=0, tiled=True),
        lax.all_gather(attention_master.astype(jnp.bfloat16), "rows", axis=0, tiled=True),
        lax.all_gather(projection_master.astype(jnp.bfloat16), "rows", axis=0, tiled=True),
        lax.all_gather(expand_master.astype(jnp.bfloat16), "rows", axis=0, tiled=True),
        lax.all_gather(contract_master.astype(jnp.bfloat16), "rows", axis=0, tiled=True),
        lax.all_gather(bias_master.astype(jnp.bfloat16), "rows", axis=0, tiled=True),
    )
    unused, saved = forward(tokens_wide, cond_silu, onehot, same, weights_back)
    back_tokens, gradients = backward(
        saved, weights_back, cotangent.astype(jnp.float32), cond_silu, onehot, same
    )
    masters = (
        modulation_master,
        attention_master,
        projection_master,
        expand_master,
        contract_master,
        bias_master,
    )
    firsts = (
        modulation_first,
        attention_first,
        projection_first,
        expand_first,
        contract_first,
        bias_first,
    )
    seconds = (
        modulation_second,
        attention_second,
        projection_second,
        expand_second,
        contract_second,
        bias_second,
    )
    shares = (
        lax.psum_scatter(gradients[0], "rows", scatter_dimension=0, tiled=True),
        lax.psum_scatter(gradients[1], "rows", scatter_dimension=0, tiled=True),
        lax.psum_scatter(gradients[2], "rows", scatter_dimension=0, tiled=True),
        lax.psum_scatter(gradients[3], "rows", scatter_dimension=0, tiled=True),
        lax.psum_scatter(gradients[4], "rows", scatter_dimension=0, tiled=True),
        lax.psum_scatter(gradients[5], "rows", scatter_dimension=0, tiled=True),
    )
    totals = lax.psum((shares[0], shares[1], shares[2], shares[3], shares[4], shares[5]), "seg")
    results = [
        adam_update(totals[number], masters[number], firsts[number], seconds[number])
        for number in range(6)
    ]
    flat = tuple((item for result in results for item in result))
    return (output.astype(jnp.bfloat16), back_tokens.astype(jnp.bfloat16)) + flat


def solution(mesh):
    in_specs = (
        P(("rows", "seg"), None),
        P(("rows", "seg"), None, None),
        P(("rows", "seg"), None),
        P(("rows", "seg"), None),
        P("rows", None),
        P("rows", None),
        P("rows", None),
        P("rows", None),
        P("rows", None),
        P("rows", None),
        P("rows", None),
        P("rows", None),
        P("rows", None),
        P("rows", None),
        P("rows", None),
        P("rows", None),
        P("rows", None),
        P("rows", None),
        P("rows", None),
        P("rows"),
        P("rows"),
        P("rows"),
    )
    out_specs = (
        P(("rows", "seg"), None),
        P(("rows", "seg"), None),
        P("rows", None),
        P("rows", None),
        P("rows", None),
        P("rows", None),
        P("rows", None),
        P("rows", None),
        P("rows", None),
        P("rows", None),
        P("rows", None),
        P("rows", None),
        P("rows", None),
        P("rows", None),
        P("rows", None),
        P("rows", None),
        P("rows", None),
        P("rows"),
        P("rows"),
        P("rows"),
    )
    return jax.shard_map(
        on_device, mesh=mesh, in_specs=in_specs, out_specs=out_specs, check_vma=False
    )
```

profile of v0, /device:TPU:1, one launch (start us, length us, event | category | flops | bytes accessed | tf_op | source)
XLA Modules:
  0.0 2715.6 jit_solution(14234331451383321452)
XLA Ops:
  20.7 32.3 %all-reduce = bf16[16128]{0:T(1024)(128)(2,1)S(1)} all-reduce(bf16[16128]{0:T(1024)(128)(2,1)S(1)} %dynamic-update-slice), channel_id=1, replica_groups=mesh['rows'=8,'seg'=4] {'rows'}, use_global_device_ids=true, to_apply=%add | all-reduce | flops 16128 | bytes 64512
  55.2 175.2 %all-gather.6.cloned.1.call-done = bf16[1152,6912]{1,0:T(8,128)(2,1)} async-done(((bf16[144,6912]{1,0:T(8,128)(2,1)}), bf16[1152,6912]{1,0:T(8,128)(2,1)}) %all-gather.6.cloned.1.call-update) | async-done | bytes 15925264 | tf_op jit(solution)/shard_map/all_gather | solution.py:278
  255.0 96.0 %all-gather.8.cloned.1.call-done = bf16[1152,3456]{1,0:T(8,128)(2,1)} async-done(((bf16[144,3456]{1,0:T(8,128)(2,1)}), bf16[1152,3456]{1,0:T(8,128)(2,1)}) %all-gather.8.cloned.1.call-update) | async-done | bytes 7962640 | tf_op jit(solution)/shard_map/all_gather | solution.py:279
  381.5 54.5 %while.30 = (s32[]{:T(128)}, bf16[16,768,72]{1,2,0:T(8,128)(2,1)S(1)}, bf16[16,768,72]{2,1,0:T(8,128)(2,1)}, bf16[16,768,72]{2,1,0:T(8,128)(2,1)}, bf16[16,768,7...) while((s32[]{:T(128)}, bf16[16,768,72]{1,2,0:T(8,128)(2,1)S(1)}, ...), condition=%wide.region_5.6_spmd.clone, body=%wide.region_2.5_spmd.clone.sunk | while | flops 175231488 | bytes 7806037 | solution.py:128
  453.8 106.9 %all-gather.12.cloned.1.call-done = bf16[1152,4608]{1,0:T(8,128)(2,1)} async-done(((bf16[144,4608]{1,0:T(8,128)(2,1)}), bf16[1152,4608]{1,0:T(8,128)(2,1)}) %all-gather.12.cloned.1.call-update) | async-done | bytes 10616848 | tf_op jit(solution)/shard_map/all_gather | solution.py:281
  560.7 15.8 fusion.123
  576.5 137.4 %all-gather.14.cloned.1.call-done = bf16[4608,1152]{1,0:T(8,128)(2,1)} async-done(((bf16[576,1152]{1,0:T(8,128)(2,1)}), bf16[4608,1152]{1,0:T(8,128)(2,1)}) %all-gather.14.cloned.1.call-update) | async-done | bytes 10616848 | tf_op jit(solution)/shard_map/all_gather | solution.py:282
  714.0 24.6 convert_reduce_fusion
  738.6 16.8 fusion.105
  756.0 23.3 convert_reduce_fusion.3
  800.2 163.1 %while.31 = (s32[]{:T(128)}, bf16[16,768,72]{1,2,0:T(8,128)(2,1)}, bf16[16,768,72]{1,2,0:T(8,128)(2,1)}, bf16[16,768,72]{1,2,0:T(8,128)(2,1)}, bf16[16,768,72]{2...) while((s32[]{:T(128)}, bf16[16,768,72]{1,2,0:T(8,128)(2,1)}, ...), condition=%wide.region_14.15_spmd.clone, body=%wide.region_10.14_spmd.clone.sunk | while | flops 435564288 | bytes 21637228 | solution.py:195
  963.3 15.3 fusion.103
  978.7 19.9 fusion.107
  998.7 15.4 fusion.125
  1014.8 15.3 fusion.106
  1049.7 11.9 fusion.121
  1061.6 17.2 fusion.99
  1078.9 167.8 %reduce-scatter.8.cloned.1.call-done = f32[144,3456]{1,0:T(8,128)} async-done(((f32[1152,3456]{1,0:T(8,128)}), f32[144,3456]{1,0:T(8,128)}) %reduce-scatter.8.cloned.1.call-update) | async-done | bytes 1990672 | tf_op jit(solution)/shard_map/reduce_scatter | solution.py:324
  1246.7 350.7 %reduce-scatter.14.cloned.1.call-done = f32[576,1152]{1,0:T(8,128)} async-done(((f32[4608,1152]{1,0:T(8,128)}), f32[576,1152]{1,0:T(8,128)}) %reduce-scatter.14.cloned.1.call-update) | async-done | bytes 2654224 | tf_op jit(solution)/shard_map/reduce_scatter | solution.py:327
  1597.4 350.3 %reduce-scatter.12.cloned.1.call-done = f32[144,4608]{1,0:T(8,128)} async-done(((f32[1152,4608]{1,0:T(8,128)}), f32[144,4608]{1,0:T(8,128)}) %reduce-scatter.12.cloned.1.call-update) | async-done | bytes 2654224 | tf_op jit(solution)/shard_map/reduce_scatter | solution.py:326
  1947.7 515.8 %reduce-scatter.6.cloned.1.call-done = f32[144,6912]{1,0:T(8,128)} async-done(((f32[1152,6912]{1,0:T(8,128)}), f32[144,6912]{1,0:T(8,128)}) %reduce-scatter.6.cloned.1.call-update) | async-done | bytes 3981328 | tf_op jit(solution)/shard_map/reduce_scatter | solution.py:323
  2469.2 28.8 %all-reduce.1 = f32[16128]{0:T(1024)S(1)} all-reduce(f32[16128]{0:T(1024)S(1)} %constant_dynamic-update-slice_fusion.6), channel_id=7, replica_groups=mesh['rows'=8,'seg'=4] {'rows'}, use_global_device_ids=true, to_apply=%region_33.34.clone | all-reduce | flops 16128 | bytes 129024
  2498.0 13.1 psum.47
  2511.8 166.7 %all-reduce.5.cloned.1.call-done = (f32[144,6912]{1,0:T(8,128)}, f32[144,3456]{1,0:T(8,128)}, f32[144,1152]{1,0:T(8,128)}, f32[144,4608]{1,0:T(8,128)}, f32[576,1152]{1,0:T(8,128)}) async-done(((f32[144,6912]{1,0:T(8,128)}, f32[144,3456]{1,0:T(8,128)}, f32[144,1152]{1,0:T(8,128)}, f32[144,4608]{1,0:T(8,128)}, f32[576,1152]{1,0:T(8,128)}), (f32[144,6912]{1,0:T(8,128)}, f32[144,3456]{1,0:T(8,128)}, ...) | async-done | bytes 11943952 | tf_op jit(solution)/shard_map/psum | solution.py:330
  (351 shorter events, 382.0 us)
Async XLA Ops:
  7.2 223.2 %all-gather.6.cloned.1.call-start = ((), (), s32[]{:S(2)}) async-start(), calls=%async_computation.5 | async-start | bytes 17915904 | tf_op jit(solution)/shard_map/all_gather | solution.py:278
  10.9 340.1 %all-gather.8.cloned.1.call-start = ((), (), s32[]{:S(2)}) async-start(), calls=%async_computation.6 | async-start | bytes 8957952 | tf_op jit(solution)/shard_map/all_gather | solution.py:279
  13.7 422.2 %all-gather.10.cloned.1.call-start = ((), (), s32[]{:S(2)}) async-start(), calls=%async_computation.7 | async-start | bytes 2985984 | tf_op jit(solution)/shard_map/all_gather | solution.py:280
  14.6 546.1 %all-gather.12.cloned.1.call-start = ((), (), s32[]{:S(2)}) async-start(), calls=%async_computation.8 | async-start | bytes 11943936 | tf_op jit(solution)/shard_map/all_gather | solution.py:281
  15.8 38.4 %copy-start.1 = (bf16[768,1152]{1,0:T(8,128)(2,1)S(1)}, bf16[768,1152]{1,0:T(8,128)(2,1)}, u32[]{:S(2)}) copy-start(bf16[768,1152]{1,0:T(8,128)(2,1)} %param.26) | copy-start | bytes 5308420
  15.8 698.1 %all-gather.14.cloned.1.call-start = ((), (), s32[]{:S(2)}) async-start(), calls=%async_computation.9 | async-start | bytes 11943936 | tf_op jit(solution)/shard_map/all_gather | solution.py:282
  19.0 211.5 %copy-start.33 = (bf16[1,4,1152]{2,1,0:T(4,128)(2,1)S(1)}, bf16[1,4,1152]{2,1,0:T(4,128)(2,1)}, u32[]{:S(2)}) copy-start(bf16[1,4,1152]{2,1,0:T(4,128)(2,1)} %param.27) | copy-start | bytes 27652
  19.0 1059.9 %reduce-scatter.10.cloned.1.call-start = ((), (), s32[]{:S(2)}) async-start(), calls=%async_computation.12 | async-start | bytes 5971968 | tf_op jit(solution)/shard_map/reduce_scatter | solution.py:325
  54.6 192.2 %copy-start.30 = (f32[768]{0:T(1024)}, f32[768]{0:T(1024)S(1)}, u32[]{:S(2)}) copy-start(f32[768]{0:T(1024)S(1)} %broadcast_multiply_fusion.5) | copy-start | bytes 9220
  55.2 191.5 %copy-start.35 = (f32[768]{0:T(1024)}, f32[768]{0:T(1024)S(1)}, u32[]{:S(2)}) copy-start(f32[768]{0:T(1024)S(1)} %add_rsqrt_fusion.1) | copy-start | bytes 9220
  255.0 105.8 %copy-start.27 = (bf16[768,1152]{1,0:T(8,128)(2,1)}, bf16[768,1152]{1,0:T(8,128)(2,1)S(1)}, u32[]{:S(2)}) copy-start(bf16[768,1152]{1,0:T(8,128)(2,1)S(1)} %fusion.72) | copy-start | bytes 5308420
  381.5 55.7 %copy-start.48 = (f32[1152]{0:T(1024)S(1)}, f32[1152]{0:T(1024)}, u32[]{:S(2)}) copy-start(f32[1152]{0:T(1024)} %get-tuple-element.265) | copy-start | bytes 13828
  447.3 308.7 %copy-start.37 = (f32[768]{0:T(1024)}, f32[768]{0:T(1024)S(1)}, u32[]{:S(2)}) copy-start(f32[768]{0:T(1024)S(1)} %add_rsqrt_fusion) | copy-start | bytes 9220
  796.2 450.6 %reduce-scatter.8.cloned.1.call-start = ((), (), s32[]{:S(2)}) async-start(), calls=%async_computation.11 | async-start | bytes 17915904 | tf_op jit(solution)/shard_map/reduce_scatter | solution.py:324
  978.6 618.8 %reduce-scatter.14.cloned.1.call-start = ((), (), s32[]{:S(2)}) async-start(), calls=%async_computation.14 | async-start | bytes 23887872 | tf_op jit(solution)/shard_map/reduce_scatter | solution.py:327
  998.6 949.1 %reduce-scatter.12.cloned.1.call-start = ((), (), s32[]{:S(2)}) async-start(), calls=%async_computation.13 | async-start | bytes 23887872 | tf_op jit(solution)/shard_map/reduce_scatter | solution.py:326
  1014.1 1449.4 %reduce-scatter.6.cloned.1.call-start = ((), (), s32[]{:S(2)}) async-start(), calls=%async_computation.10 | async-start | bytes 35831808 | tf_op jit(solution)/shard_map/reduce_scatter | solution.py:323
  1078.8 1599.6 %all-reduce.5.cloned.1.call-start = ((), (), s32[]{:S(2)}) async-start(), calls=%async_computation.15 | async-start | bytes 23887872 | tf_op jit(solution)/shard_map/psum | solution.py:330
  2468.3 42.9 %copy-start.41 = (f32[2016]{0:T(1024)S(1)}, f32[2016]{0:T(1024)}, u32[]{:S(2)}) copy-start(f32[2016]{0:T(1024)} %param.45) | copy-start | bytes 24196
  2468.3 42.9 %copy-start.45 = (f32[2016]{0:T(1024)S(1)}, f32[2016]{0:T(1024)}, u32[]{:S(2)}) copy-start(f32[2016]{0:T(1024)} %param.46) | copy-start | bytes 24196
  2468.3 42.9 %copy-start.46 = (f32[2016]{0:T(1024)S(1)}, f32[2016]{0:T(1024)}, u32[]{:S(2)}) copy-start(f32[2016]{0:T(1024)} %param.47) | copy-start | bytes 24196
  2468.3 210.2 %copy-start.25 = (f32[144,1152]{1,0:T(8,128)S(1)}, f32[144,1152]{1,0:T(8,128)}, u32[]{:S(2)}) copy-start(f32[144,1152]{1,0:T(8,128)} %param.36) | copy-start | bytes 1990660
  2468.3 210.2 %copy-start.28 = (f32[144,1152]{1,0:T(8,128)S(1)}, f32[144,1152]{1,0:T(8,128)}, u32[]{:S(2)}) copy-start(f32[144,1152]{1,0:T(8,128)} %param.37) | copy-start | bytes 1990660
  2468.7 212.8 %copy-start.9 = (f32[144,3456]{1,0:T(8,128)S(1)}, f32[144,3456]{1,0:T(8,128)}, u32[]{:S(2)}) copy-start(f32[144,3456]{1,0:T(8,128)} %param.33) | copy-start | bytes 5971972
  (38 other events, 204.2 us)
Sparse Core Ops, SparseCore 0:
  11.0 219.3 all-gather.5
  233.2 117.7 all-gather.7
  353.7 52.3 all-gather.9
  408.7 151.9 all-gather.11
  563.3 150.6 all-gather.13
  796.3 102.5 reduce-scatter.9
  978.8 267.9 reduce-scatter.7
  1251.1 346.2 reduce-scatter.13
  1601.3 346.3 reduce-scatter.11
  1951.9 511.4 reduce-scatter.5
  2466.7 211.6 all-reduce.4
where the time goes:
time: 2730 us; the launch traced here: 2720 us
  waiting for transfers between devices  2070 us (76%)
  matrix products  420 us (15%)
  other arithmetic  88 us (3%)
  blocking collectives  74.2 us (3%)
  local copies, waits for them, and re-layouts  49.2 us (2%)
    reduce_scatter x1, waiting for transfers between devices, on_device(): lax.psum_scatter(gradients[0], 'rows', scatter_dimension=0, tiled=True)  516 us
    reduce_scatter x1, waiting for transfers between devices, on_device(): lax.psum_scatter(gradients[4], 'rows', scatter_dimension=0, tiled=True)  351 us
    reduce_scatter x1, waiting for transfers between devices, on_device(): lax.psum_scatter(gradients[3], 'rows', scatter_dimension=0, tiled=True)  350 us
    all_gather x1, waiting for transfers between devices, on_device(): lax.all_gather(modulation_master.astype(jnp.bfloat16), 'rows', axis=0, ti...  175 us
    reduce_scatter x1, waiting for transfers between devices, on_device(): lax.psum_scatter(gradients[1], 'rows', scatter_dimension=0, tiled=True)  168 us
    psum x1, waiting for transfers between devices, on_device(): lax.psum((shares[0], shares[1], shares[2], shares[3], shares[4], shares[5...  167 us
    dot_general x38, matrix products, outer(): lax.dot_general(left, right, (((0,), (0,)), ((), ())), precision=precisio...  154 us
    all_gather x1, waiting for transfers between devices, on_device(): lax.all_gather(contract_master.astype(jnp.bfloat16), 'rows', axis=0, tile...  137 us
  transfers between devices with their start and end apart: 11, of which 9 were waited for; matrix products, arithmetic and copies ran while one was open for 16% of the time, Pallas kernels for 0%

commit v1 on v0

v1 whole, which is shorter than its diff:
```python
from functools import partial

import jax
import jax.numpy as jnp
from jax import lax
from jax.experimental import pallas as pl
from jax.experimental.pallas import tpu as pltpu
from jax.sharding import PartitionSpec as P

HEAD_DIM = 72
STEP = 10

bf16 = jnp.bfloat16
f32 = jnp.float32
highest = lax.Precision.HIGHEST
beta_first = 0.9
beta_second = 0.999
learning = 0.06
weight_decay = 0.1
adam_epsilon = 1e-08
norm_epsilon = 1e-06

ROW_X = [(z * 2 + x, z * 2 + 1 - x) for z in range(4) for x in range(2)]
ROW_Z = [
    [(z * 2 + x, (z + k) % 4 * 2 + x) for z in range(4) for x in range(2)] for k in range(4)
]
SEG_Y = [(y * 2 + c, (1 - y) * 2 + c) for y in range(2) for c in range(2)]
SEG_C = [(y * 2 + c, y * 2 + 1 - c) for y in range(2) for c in range(2)]


def over_x(v):
    return lax.ppermute(v, "rows", ROW_X)


def over_z(v, k):
    return lax.ppermute(v, "rows", ROW_Z[k])


def over_y(v):
    return lax.ppermute(v, "seg", SEG_Y)


def over_core(v):
    return lax.ppermute(v, "seg", SEG_C)


def place():
    row = lax.axis_index("rows")
    seg = lax.axis_index("seg")
    return row % 2, seg // 2, row // 2, seg % 2


def layer_norm(values):
    center = values - jnp.mean(values, axis=-1, keepdims=True)
    inverse = lax.rsqrt(jnp.mean(center * center, axis=-1, keepdims=True) + norm_epsilon)
    return (center * inverse, inverse)


def norm_back(upstream, normed, inverse):
    return inverse * (
        upstream
        - jnp.mean(upstream, axis=-1, keepdims=True)
        - normed * jnp.mean(upstream * normed, axis=-1, keepdims=True)
    )


def outer(left, right, precision=None):
    return lax.dot_general(
        left,
        right,
        (((0,), (0,)), ((), ())),
        precision=precision,
        preferred_element_type=f32,
    )


def dot(left, right):
    return jnp.dot(left, right, preferred_element_type=f32)


def back_dot(left, right):
    return lax.dot_general(left, right, (((1,), (1,)), ((), ())), preferred_element_type=f32)


def to_heads(values):
    return values.reshape(values.shape[0], -1, HEAD_DIM).transpose(1, 0, 2)


def from_heads(values):
    return values.transpose(1, 0, 2).reshape(values.shape[1], -1)


def soft_weights(same, query, key):
    scores = back_dot(query, key) * HEAD_DIM ** (-0.5)
    scores = jnp.where(same, scores, -1e30)
    powers = jnp.exp(scores - jnp.max(scores, axis=-1, keepdims=True))
    return powers / jnp.sum(powers, axis=-1, keepdims=True)


def attend_head(same, operands):
    query, key, value = operands
    softened = soft_weights(same, query, key).astype(bf16)
    return dot(softened, value).astype(bf16)


def head_back(same, operands):
    query, key, value, upstream = operands
    softened = soft_weights(same, query, key)
    back_value = outer(softened.astype(bf16), upstream)
    back_soft = back_dot(upstream, value)
    back_score = (
        softened * (back_soft - jnp.sum(back_soft * softened, axis=-1, keepdims=True))
    ).astype(bf16)
    scale = HEAD_DIM ** (-0.5)
    back_query = dot(back_score, key) * scale
    back_key = outer(back_score, query) * scale
    return (back_query.astype(bf16), back_key.astype(bf16), back_value.astype(bf16))


def adam_update(gradient, master, first, second):
    first_new = beta_first * first + (1.0 - beta_first) * gradient
    second_new = beta_second * second + (1.0 - beta_second) * gradient * gradient
    first_hat = first_new / (1.0 - beta_first**STEP)
    second_hat = second_new / (1.0 - beta_second**STEP)
    master_new = master - learning * (
        first_hat / (jnp.sqrt(second_hat) + adam_epsilon) + weight_decay * master
    )
    return (master_new, first_new, second_new)


def remote(src, dst, send, recv, device):
    return pltpu.make_async_remote_copy(
        src_ref=src,
        dst_ref=dst,
        send_sem=send,
        recv_sem=recv,
        device_id=device,
        device_id_type=pl.DeviceIdType.MESH,
    )


def greet(peers):
    barrier = pltpu.get_barrier_semaphore()
    for peer in peers:
        pl.semaphore_signal(
            barrier, inc=1, device_id=peer, device_id_type=pl.DeviceIdType.MESH
        )
    pl.semaphore_wait(barrier, len(peers))


def gather_kernel(own, w_nat, w_con, w, z_s, z_r, x_s, x_r, y_s, y_r, c_s, c_r, load_sem, out_sem):
    row, seg = lax.axis_index("rows"), lax.axis_index("seg")
    x, z = row % 2, row // 2
    y, c = seg // 2, seg % 2
    n = own.shape[1]
    units = own.shape[0] // 2
    piece = n // 3
    part = pl.multiple_of(y * piece, piece)
    third = pl.multiple_of(y * 2 * piece, piece)
    far = [lax.rem(z + 4 - k, 4) for k in range(4)]
    loads = []
    for u in range(units):
        copy = pltpu.make_async_copy(
            own.at[2 * u + c, pl.ds(part, 2 * piece)],
            w.at[2 * u + c, row, pl.ds(part, 2 * piece)],
            load_sem.at[u],
        )
        copy.start()
        loads.append(copy)
    z_peers = [(lax.rem(z + k, 4) * 2 + x, seg) for k in (1, 2, 3)]
    x_peer, y_peer, c_peer = (row + 1 - 2 * x, seg), (row, seg + 2 - 4 * y), (row, seg + 1 - 2 * c)
    greet(z_peers + [x_peer, y_peer, c_peer])
    sent = []

    def along_z(u, k):
        ref = w.at[2 * u + c, row, pl.ds(part, 2 * piece)]
        return remote(ref, ref, z_s.at[u, k - 1], z_r.at[u, k - 1], z_peers[k - 1])

    def along_x(u, k):
        ref = w.at[2 * u + c, far[k] * 2 + x, pl.ds(part, 2 * piece)]
        return remote(ref, ref, x_s.at[u, k], x_r.at[u, k], x_peer)

    def along_y(u, k):
        ref = w.at[2 * u + c, pl.ds(far[k] * 2, 2), pl.ds(third, piece)]
        return remote(ref, ref, y_s.at[u, k], y_r.at[u, k], y_peer)

    def across(u, k):
        ref = w.at[2 * u + c, pl.ds(far[k] * 2, 2)]
        return remote(ref, ref, c_s.at[u, k], c_r.at[u, k], c_peer)

    def go(copy):
        copy.start()
        sent.append(copy)

    steps = [(u, k) for u in range(units) for k in (0, 1, 3, 2)]
    outs = []
    for j in range(len(steps) + 3):
        if j < len(steps):
            u, k = steps[j]
            if k == 0:
                for later in [0, 1] if u == 0 else [u + 1]:
                    if later < units:
                        loads[later].wait()
                        for hop in (1, 3, 2):
                            go(along_z(later, hop))
            else:
                along_z(u, k).wait_recv()
            go(along_x(u, k))
        if 0 <= j - 1 < len(steps):
            along_x(*steps[j - 1]).wait_recv()
            go(along_y(*steps[j - 1]))
        if 0 <= j - 2 < len(steps):
            along_y(*steps[j - 2]).wait_recv()
            go(across(*steps[j - 2]))
        if 0 <= j - 3 < len(steps):
            u, k = steps[j - 3]
            across(u, k).wait_recv()
            if k == 2:
                for b in (2 * u, 2 * u + 1):
                    dst = w_nat.at[b] if u < 4 else w_con.at[:, b - 8]
                    copy = pltpu.make_async_copy(w.at[b], dst, out_sem.at[b])
                    copy.start()
                    outs.append(copy)
    for copy in sent:
        copy.wait_send()
    for copy in outs:
        copy.wait()


def gather_fast(attention, projection, expand, contract):
    width = projection.shape[1]
    n = attention.shape[0]
    blocks = [attention[:, j * width : (j + 1) * width] for j in range(3)] + [projection]
    blocks += [expand[:, j * width : (j + 1) * width] for j in range(4)]
    blocks += [contract[j * n : (j + 1) * n] for j in range(4)]
    own = jnp.stack([block.astype(bf16) for block in blocks])
    sems = pltpu.SemaphoreType.DMA
    w_nat, w_con = pl.pallas_call(
        gather_kernel,
        out_shape=(
            jax.ShapeDtypeStruct((8, 8, n, width), bf16),
            jax.ShapeDtypeStruct((8, 4, n, width), bf16),
        ),
        in_specs=[pl.BlockSpec(memory_space=pl.ANY)],
        out_specs=(pl.BlockSpec(memory_space=pl.ANY),) * 2,
        scratch_shapes=[pltpu.VMEM((12, 8, n, width), bf16)]
        + [sems((6, 3))] * 2
        + [sems((6, 4))] * 6
        + [sems((6,)), sems((12,))],
        compiler_params=pltpu.CompilerParams(
            collective_id=0, has_side_effects=True, vmem_limit_bytes=48 << 20
        ),
        name="gather_weights",
    )(own)
    w_nat = w_nat.reshape(8, 8 * n, width)
    return (
        (w_nat[0], w_nat[1], w_nat[2]),
        w_nat[3],
        (w_nat[4], w_nat[5], w_nat[6], w_nat[7]),
        w_con.reshape(32 * n, width),
    )


def gather_plain(attention, projection, expand, contract):
    def whole(part):
        return lax.all_gather(part.astype(bf16), "rows", axis=0, tiled=True)

    width = projection.shape[1]
    att, proj, exp, con = map(whole, (attention, projection, expand, contract))
    return (
        tuple(att[:, j * width : (j + 1) * width] for j in range(3)),
        proj,
        tuple(exp[:, j * width : (j + 1) * width] for j in range(4)),
        con,
    )


def reduce_unit(part):
    x, y, z, c = place()
    part = part.reshape(8, 3, part.shape[0] // 24, part.shape[1])
    there = lax.dynamic_index_in_dim(part, 1 - y, 1, False)
    here = lax.dynamic_index_in_dim(part, y, 1, False)
    here = here.astype(f32) + over_y(there).astype(f32)
    pair = jnp.stack([here.astype(bf16), part[:, 2]], axis=1)
    pair = pair.reshape((4, 2) + pair.shape[1:])
    there = lax.dynamic_index_in_dim(pair, 1 - x, 1, False)
    here = lax.dynamic_index_in_dim(pair, x, 1, False)
    quad = (here.astype(f32) + over_x(there).astype(f32)).astype(bf16)

    def level(k):
        return lax.dynamic_index_in_dim(quad, lax.rem(z + k, 4), 0, False)

    total = level(0).astype(f32)
    for k in (1, 2, 3):
        total = total + over_z(level(k), k).astype(f32)
    total = total.astype(bf16)
    back = over_y(total)
    last = (total[1].astype(f32) + back[1].astype(f32)).astype(bf16)
    first = jnp.where(y == 0, total[0], back[0])
    second = jnp.where(y == 0, back[0], total[0])
    mine = jnp.concatenate([first, second, last])
    other = over_core(mine)
    return (
        jnp.where(c == 0, mine, other).astype(f32),
        jnp.where(c == 0, other, mine).astype(f32),
    )


def reduce_fast(early, hidden_one, attended, hidden_two, activated, back_feed, back_before):
    x, y, z, c = place()
    width = hidden_one.shape[1]

    def pick(first, second, which):
        return jnp.where(which == 0, first, second)

    act = activated.T.reshape(8, 4, width // 8, activated.shape[0])
    feed_far = over_core(back_feed)
    results = {}
    for unit in range(2):
        mine, there = (
            lax.dynamic_index_in_dim(act, 2 * unit + which, 1, False).reshape(width, -1)
            for which in (c, 1 - c)
        )
        far = over_core(there)
        results["con", unit] = reduce_unit((dot(mine, back_feed) + dot(far, feed_far)).astype(bf16))
    two_far = over_core(hidden_two)
    for unit in range(2):
        first, second = (
            back_before[:, (2 * unit + j) * width : (2 * unit + j + 1) * width] for j in range(2)
        )
        far = over_core(pick(second, first, c))
        results["exp", unit] = reduce_unit(
            (outer(hidden_two, pick(first, second, c)) + outer(two_far, far)).astype(bf16)
        )
    one_far, att_far = over_core(hidden_one), over_core(attended)

    def late(back_query, back_key, back_value, back_project):
        far = over_core(pick(back_project, back_key, c))
        left, left_far = pick(hidden_one, attended, c), pick(one_far, att_far, c)
        first = reduce_unit(
            (outer(left, pick(back_key, back_project, c)) + outer(left_far, far)).astype(bf16)
        )
        far = over_core(pick(back_value, back_query, c))
        second = reduce_unit(
            (outer(hidden_one, pick(back_query, back_value, c)) + outer(one_far, far)).astype(bf16)
        )
        con = jnp.concatenate(results["con", 0] + results["con", 1], axis=0)
        exp = jnp.concatenate(results["exp", 0] + results["exp", 1], axis=1)
        att = jnp.concatenate([second[0], first[0], second[1]], axis=1)
        return att, first[1], exp, con

    return late


def reduce_plain(early, hidden_one, attended, hidden_two, activated, back_feed, back_before):
    def total(left, right):
        part = lax.psum_scatter(
            outer(left, right).astype(bf16), "rows", scatter_dimension=0, tiled=True
        )
        return lax.psum(part.astype(f32), "seg")

    con = total(activated, back_feed)
    exp = total(hidden_two, back_before)

    def late(back_query, back_key, back_value, back_project):
        att = total(hidden_one, jnp.concatenate([back_query, back_key, back_value], axis=1))
        return att, total(attended, back_project), exp, con

    return late


def on_device(
    fast,
    tokens,
    condition,
    segment_ids,
    cotangent,
    modulation_master,
    modulation_first,
    modulation_second,
    attention_master,
    attention_first,
    attention_second,
    projection_master,
    projection_first,
    projection_second,
    expand_master,
    expand_first,
    expand_second,
    contract_master,
    contract_first,
    contract_second,
    bias_master,
    bias_first,
    bias_second,
):
    width = tokens.shape[1]
    hidden = expand_master.shape[1]
    shard = modulation_master.shape[0]
    n_seg = condition.shape[1]
    row = lax.axis_index("rows")
    segments = segment_ids[0]
    onehot = (segments[:, None] == jnp.arange(n_seg, dtype=jnp.int32)[None, :]).astype(f32)
    same = segments[:, None] == segments[None, :]
    tokens_wide = tokens.astype(f32)
    upstream = cotangent.astype(f32)

    cond_silu = jax.nn.silu(condition[0].astype(f32)).astype(bf16)
    cond_seg = lax.all_gather(cond_silu, "rows", axis=0, tiled=True)
    cond_mine = lax.dynamic_slice_in_dim(cond_seg, row * shard, shard, axis=1)
    partial_mod = dot(cond_mine, modulation_master.astype(bf16))
    modulation = lax.psum_scatter(partial_mod, "rows", scatter_dimension=0, tiled=True)
    biases = lax.all_gather(bias_master.astype(bf16), "rows", axis=0, tiled=True).astype(f32)
    query_bias, value_bias, projection_bias = (
        biases[j * width : (j + 1) * width] for j in range(3)
    )
    expand_bias = biases[3 * width : 3 * width + hidden]
    contract_bias = biases[3 * width + hidden : 4 * width + hidden]
    modulation = modulation + biases[4 * width + hidden :]

    gather = gather_fast if fast else gather_plain
    w_att, w_proj, w_exp, w_con = gather(
        attention_master, projection_master, expand_master, contract_master
    )

    per_token = jnp.dot(onehot, modulation, precision=highest)
    shift_one, scale_one, gate_one, shift_two, scale_two, gate_two = jnp.split(per_token, 6, axis=1)
    normed_one, inverse_one = layer_norm(tokens_wide)
    hidden_one = (normed_one * (1.0 + scale_one) + shift_one).astype(bf16)
    query = (dot(hidden_one, w_att[0]) + query_bias).astype(bf16)
    key = dot(hidden_one, w_att[1]).astype(bf16)
    value = (dot(hidden_one, w_att[2]) + value_bias).astype(bf16)
    heads = (to_heads(query), to_heads(key), to_heads(value))
    attended = from_heads(lax.map(partial(attend_head, same), heads))
    projected = dot(attended, w_proj) + projection_bias
    middle = tokens_wide + gate_one * projected
    normed_two, inverse_two = layer_norm(middle)
    hidden_two = (normed_two * (1.0 + scale_two) + shift_two).astype(bf16)
    before = (
        jnp.concatenate([dot(hidden_two, part) for part in w_exp], axis=1) + expand_bias
    )
    activated = jax.nn.gelu(before, approximate=True).astype(bf16)
    feedforward = dot(activated, w_con) + contract_bias
    output = middle + gate_two * feedforward

    back_gate_two = upstream * feedforward
    back_feed = (upstream * gate_two).astype(bf16)
    back_active = back_dot(back_feed, w_con)
    gelu_pull = jax.vjp(partial(jax.nn.gelu, approximate=True), before)[1]
    back_before = gelu_pull(back_active)[0].astype(bf16)
    reduce = reduce_fast if fast else reduce_plain
    late = reduce(None, hidden_one, attended, hidden_two, activated, back_feed, back_before)
    back_hidden_two = sum(
        back_dot(back_before[:, j * width : (j + 1) * width], w_exp[j]) for j in range(4)
    )
    back_middle = upstream + norm_back(back_hidden_two * (1.0 + scale_two), normed_two, inverse_two)
    back_gate_one = back_middle * projected
    back_project = (back_middle * gate_one).astype(bf16)
    back_attend = back_dot(back_project, w_proj).astype(bf16)
    back_heads = lax.map(partial(head_back, same), heads + (to_heads(back_attend),))
    back_query, back_key, back_value = (from_heads(part) for part in back_heads)
    grad_att, grad_proj, grad_exp, grad_con = late(back_query, back_key, back_value, back_project)
    back_hidden_one = (
        back_dot(back_query, w_att[0]) + back_dot(back_key, w_att[1]) + back_dot(back_value, w_att[2])
    )
    back_tokens = back_middle + norm_back(
        back_hidden_one * (1.0 + scale_one), normed_one, inverse_one
    )
    back_modulation = jnp.concatenate(
        [
            outer(onehot, part, highest)
            for part in (
                back_hidden_one,
                back_hidden_one * normed_one,
                back_gate_one,
                back_hidden_two,
                back_hidden_two * normed_two,
                back_gate_two,
            )
        ],
        axis=1,
    )
    columns = jnp.concatenate(
        [
            jnp.sum(part.astype(f32), axis=0)
            for part in (back_query, back_value, back_project, back_before, back_feed)
        ]
    )
    payload = jnp.concatenate([back_modulation, columns.reshape(n_seg, -1)], axis=1)
    everyone = lax.all_gather(payload, ("rows", "seg"), axis=0, tiled=True)
    cond_all = lax.all_gather(cond_silu, ("rows", "seg"), axis=0, tiled=True)
    mod_all = everyone[:, : 6 * width]
    cond_rows = lax.dynamic_slice_in_dim(cond_all, row * shard, shard, axis=1)
    grad_mod = outer(cond_rows.astype(f32), mod_all, highest)
    devices = everyone.shape[0] // n_seg
    rest = jnp.sum(everyone[:, 6 * width :].reshape(devices, -1), axis=0)
    grad_bias = lax.dynamic_slice_in_dim(
        jnp.concatenate([rest, jnp.sum(mod_all, axis=0)]),
        row * bias_master.shape[0],
        bias_master.shape[0],
    )
    results = [
        adam_update(*operands)
        for operands in (
            (grad_mod, modulation_master, modulation_first, modulation_second),
            (grad_att, attention_master, attention_first, attention_second),
            (grad_proj, projection_master, projection_first, projection_second),
            (grad_exp, expand_master, expand_first, expand_second),
            (grad_con, contract_master, contract_first, contract_second),
            (grad_bias, bias_master, bias_first, bias_second),
        )
    ]
    flat = tuple((item for result in results for item in result))
    return (output.astype(bf16), back_tokens.astype(bf16)) + flat


def solution(mesh):
    both = ("rows", "seg")
    fast = mesh.shape["rows"] == 8 and mesh.shape["seg"] == 4
    token, matrix, vector = P(both, None), P("rows", None), P("rows")
    in_specs = (token, P(both, None, None), token, token) + (matrix,) * 15 + (vector,) * 3
    out_specs = (token, token) + (matrix,) * 15 + (vector,) * 3
    return jax.shard_map(
        partial(on_device, fast),
        mesh=mesh,
        in_specs=in_specs,
        out_specs=out_specs,
        check_vma=False,
    )
```

time: 2730 us -> 1160 us (0.42)
  waiting for transfers between devices: 2070 us -> 173 us
  Pallas kernels: 0 us -> 146 us
  starting transfers between devices: 0.46 us -> 74.8 us
  local copies, waits for them, and re-layouts: 49.2 us -> 108 us
  matrix products: 420 us -> 455 us
  blocking collectives: 74.2 us -> 108 us
    reduce_scatter x5 -> x0, waiting for transfers between devices: 1380 us -> none  [the longest x1 516 us: on_device(): lax.psum_scatter(gradients[0], 'rows', scatter_dimension=0, tiled=True)]
    all_gather x5 -> x1, waiting for transfers between devices: 516 us -> 0.01 us  [on_device(): everyone = lax.all_gather(payload, ('rows', 'seg'), axis=0, tiled=True)]
    ppermute x0 -> x52, waiting for transfers between devices: none -> 173 us  [the longest x12 90 us: over_y(): return lax.ppermute(v, 'seg', SEG_Y)]
    psum x1 -> x0, waiting for transfers between devices: 167 us -> none  [on_device(): lax.psum((shares[0], shares[1], shares[2], shares[3], shares[4], shares[5...]
    pallas_call x0 -> x1, Pallas kernels: none -> 146 us  [gather_fast(): pl.pallas_call(gather_kernel, out_shape=(jax.ShapeDtypeStruct((8, 8, n, w...]
    all_gather x0 -> x2, blocking collectives: none -> 78.2 us  [the longest x1 52.6 us: on_device(): cond_all = lax.all_gather(cond_silu, ('rows', 'seg'), axis=0, tiled=True)]
    ppermute x0 -> x52, starting transfers between devices: none -> 74.7 us  [the longest x18 39.6 us: over_z(): return lax.ppermute(v, 'rows', ROW_Z[k])]
    unnamed x2 -> x1, blocking collectives: 61 us -> 29.9 us
  transfers between devices with their start and end apart: 11 -> 54, of which waited for: 9 -> 19; matrix products, arithmetic and copies ran while one was open for 16% -> 39% of each run, Pallas kernels for 0% -> 13%
where the time goes in v1:
time: 1160 us; the launch traced here: 1150 us
  matrix products  455 us (39%)
  waiting for transfers between devices  173 us (15%)
  Pallas kernels  146 us (13%)
  blocking collectives  108 us (9%)
  local copies, waits for them, and re-layouts  108 us (9%)
  starting transfers between devices  74.8 us (6%)
  other arithmetic  69.3 us (6%)
  between operations  17 us (1%)
    dot_general x57, matrix products, back_dot(): lax.dot_general(left, right, (((1,), (1,)), ((), ())), preferred_element_...  156 us
    pallas_call x1, Pallas kernels, gather_fast(): pl.pallas_call(gather_kernel, out_shape=(jax.ShapeDtypeStruct((8, 8, n, w...  146 us
    dot_general x46, matrix products, dot(): return jnp.dot(left, right, preferred_element_type=f32)  146 us
    dot_general x47, matrix products, outer(): lax.dot_general(left, right, (((0,), (0,)), ((), ())), precision=precisio...  143 us
    ppermute x12, waiting for transfers between devices, over_y(): return lax.ppermute(v, 'seg', SEG_Y)  90 us
    all_gather x1, blocking collectives, on_device(): cond_all = lax.all_gather(cond_silu, ('rows', 'seg'), axis=0, tiled=True)  52.6 us
    ppermute x18, waiting for transfers between devices, over_z(): return lax.ppermute(v, 'rows', ROW_Z[k])  47.8 us
    unnamed x160, local copies, waits for them, and re-layouts  43.4 us
  transfers between devices with their start and end apart: 54, of which 19 were waited for; matrix products, arithmetic and copies ran while one was open for 39% of the time, Pallas kernels for 13%

profile of v1, /device:TPU:1, one launch (start us, length us, event | category | flops | bytes accessed | tf_op | source)
XLA Modules:
  0.0 1151.6 jit_solution(2126272295750363571)
XLA Ops:
  8.0 25.6 %all-gather = bf16[8,4,1152]{2,1,0:T(4,128)(2,1)S(1)} all-gather(bf16[1,4,1152]{2,1,0:T(4,128)(2,1)S(1)} %fusion.223), channel_id=1, replica_groups=mesh['rows'=8,'seg'=4] {'rows'}, dimensions={0}, use_global_device_ids=true | all-gather | bytes 82944 | tf_op jit(solution)/shard_map/all_gather | solution.py:409
  39.0 29.9 %all-reduce = bf16[16128]{0:T(1024)(128)(2,1)S(1)} all-reduce(bf16[16128]{0:T(1024)(128)(2,1)S(1)} %dynamic-update-slice), channel_id=1, replica_groups=mesh['rows'=8,'seg'=4] {'rows'}, use_global_device_ids=true, to_apply=%add | all-reduce | flops 16128 | bytes 64512
  70.1 52.6 %all-gather.1 = bf16[32,4,1152]{2,1,0:T(4,128)(2,1)S(1)} all-gather(bf16[1,4,1152]{2,1,0:T(4,128)(2,1)S(1)} %fusion.223), channel_id=1, replica_groups=mesh['rows'=8,'seg'=4] {'rows','seg'}, dimensions={0}, use_global_device_ids=true | all-gather | bytes 304128 | tf_op jit(solution)/shard_map/all_gather | solution.py:491
  127.8 146.2 %gather_weights.1 = (bf16[8,8,144,1152]{3,2,1,0:T(8,128)(2,1)}, bf16[8,4,144,1152]{3,2,1,0:T(8,128)(2,1)}) custom-call(bf16[12,144,1152]{2,1,0:T(8,128)(2,1)S(1)} %fusion.193.own), custom_call_target="tpu_custom_call" | custom-call | tf_op jit(solution)/shard_map/gather_weights/pallas_call | solution.py:238
  275.6 15.1 %fusion.244 = (bf16[1,8,144,1152]{3,2,1,0:T(8,128)(2,1)}, bf16[1,8,144,1152]{3,2,1,0:T(8,128)(2,1)}, bf16[1,8,144,1152]{3,2,1,0:T(8,128)(2,1)}, bf16[1,8,144,115...) fusion(bf16[8,8,144,1152]{3,2,1,0:T(8,128)(2,1)} %get-tuple-ele, ...), kind=kLoop, calls=%fused_computation.442 | loop fusion | bytes 42467328 | tf_op jit(solution)/shard_map/slice | solution.py:259
  290.7 9.5 fusion.192
  333.7 54.2 %while.26 = (s32[]{:T(128)}, bf16[16,768,72]{1,2,0:T(8,128)(2,1)S(1)}, bf16[16,768,72]{2,1,0:T(8,128)(2,1)}, bf16[16,768,72]{2,1,0:T(8,128)(2,1)}, bf16[16,768,7...) while((s32[]{:T(128)}, bf16[16,768,72]{1,2,0:T(8,128)(2,1)S(1)}, ...), condition=%wide.region_6.7_spmd.clone, body=%wide.region_3.6_spmd.clone.sunk | while | flops 175231488 | bytes 7806029 | solution.py:434
  430.2 28.1 %convert_reduce_fusion = (f32[4608]{0:T(1024)}, bf16[768,4608]{1,0:T(8,128)(2,1)}, bf16[768,4608]{1,0:T(8,128)(2,1)}) fusion(f32[4608]{0:T(1024)} %slice.294, f32[768,1152]{1,0:T(8,128)} %fusion.256, f32[768,1152]{1,0:T(8,128)} %fusion.255, f32[768,1152]{1,0:T(8,128)} %fusion.254, f32[768,1152]{1,0:T(8,128)} %fusion.253, ...), kind=kOutput, calls=%fused_computation.67 | convolution fusion | flops 8252812800 | bytes 40734720 | tf_op jit(solution)/shard_map/dot_general | solution.py:82
  496.5 22.4 %convert_reduce_fusion.3 = (f32[1152]{0:T(1024)}, bf16[768,1152]{1,0:T(8,128)(2,1)}, f32[768,1152]{1,0:T(8,128)}, bf16[768,1152]{1,0:T(8,128)(2,1)}, f32[768,1152]{1,0:T(8,128)}) fusion(f32[768,6912]{1,0:T(8,128)} %copy-done, f32[768]{0:T(1024)S(1)} %get-tuple-element.331, f32[768,1152]{1,0:T(8,128)S(1)} %get-tuple-element.235, ...), kind=kOutput, calls=%fused_computation.124 | convolution fusion | flops 8169651200 | bytes 47797248 | tf_op jit(solution)/shard_map/dot_general | solution.py:78
  532.8 162.8 %while.27 = (s32[]{:T(128)}, bf16[16,768,72]{1,2,0:T(8,128)(2,1)}, bf16[16,768,72]{1,2,0:T(8,128)(2,1)}, bf16[16,768,72]{1,2,0:T(8,128)(2,1)}, bf16[16,768,72]{2...) while((s32[]{:T(128)}, bf16[16,768,72]{1,2,0:T(8,128)(2,1)}, ...), condition=%wide.region_15.16_spmd.clone, body=%wide.region_11.15_spmd.clone.sunk | while | flops 435564288 | bytes 21637220 | solution.py:460
  747.3 9.1 fusion.228
  771.1 10.3 copy.125
  854.9 18.5 %collective-permute-done.45 = bf16[8,48,1152]{2,1,0:T(8,128)(2,1)S(1)} collective-permute-done((bf16[8,48,1152]{2,1,0:T(8,128)(2,1)S(1)}, bf16[8,48,1152]{2,1,0:T(8,128)(2,1)S(1)}, u32[]{:S(2)}, u32[]{:S(2)}) %collective-permute-start.45) | collective-permute-done | bytes 884768 | tf_op jit(solution)/shard_map/ppermute | solution.py:40
  876.7 15.7 %collective-permute-done.20 = bf16[8,48,1152]{2,1,0:T(8,128)(2,1)S(1)} collective-permute-done((bf16[8,48,1152]{2,1,0:T(8,128)(2,1)S(1)}, bf16[8,48,1152]{2,1,0:T(8,128)(2,1)S(1)}, u32[]{:S(2)}, u32[]{:S(2)}) %collective-permute-start.20) | collective-permute-done | bytes 884768 | tf_op jit(solution)/shard_map/ppermute | solution.py:40
  895.0 16.4 %collective-permute-done.28 = bf16[8,48,1152]{2,1,0:T(8,128)(2,1)S(1)} collective-permute-done((bf16[8,48,1152]{2,1,0:T(8,128)(2,1)S(1)}, bf16[8,48,1152]{2,1,0:T(8,128)(2,1)S(1)}, u32[]{:S(2)}, u32[]{:S(2)}) %collective-permute-start.28) | collective-permute-done | bytes 884768 | tf_op jit(solution)/shard_map/ppermute | solution.py:40
  914.8 15.6 %collective-permute-done.11 = bf16[8,48,1152]{2,1,0:T(8,128)(2,1)S(1)} collective-permute-done((bf16[8,48,1152]{2,1,0:T(8,128)(2,1)S(1)}, bf16[8,48,1152]{2,1,0:T(8,128)(2,1)S(1)}, u32[]{:S(2)}, u32[]{:S(2)}) %collective-permute-start.11) | collective-permute-done | bytes 884768 | tf_op jit(solution)/shard_map/ppermute | solution.py:40
  933.2 16.1 %collective-permute-done.2 = bf16[8,48,1152]{2,1,0:T(8,128)(2,1)S(1)} collective-permute-done((bf16[8,48,1152]{2,1,0:T(8,128)(2,1)S(1)}, bf16[8,48,1152]{2,1,0:T(8,128)(2,1)S(1)}, u32[]{:S(2)}, u32[]{:S(2)}) %collective-permute-start.2) | collective-permute-done | bytes 884768 | tf_op jit(solution)/shard_map/ppermute | solution.py:40
  956.7 15.2 %collective-permute-done.12 = bf16[4,2,48,1152]{3,2,1,0:T(8,128)(2,1)S(1)} collective-permute-done((bf16[4,2,48,1152]{3,2,1,0:T(8,128)(2,1)S(1)}, bf16[4,2,48,1152]{3,2,1,0:T(8,128)(2,1)S(1)}, u32[]{:S(2)}, u32[]{:S(2)}) %collective-permute-start.12) | collective-permute-done | bytes 884768 | tf_op jit(solution)/shard_map/ppermute | solution.py:32
  972.2 18.7 %collective-permute-done.3 = bf16[4,2,48,1152]{3,2,0,1:T(8,128)(2,1)S(1)} collective-permute-done((bf16[4,2,48,1152]{3,2,0,1:T(8,128)(2,1)S(1)}, bf16[4,2,48,1152]{3,2,0,1:T(8,128)(2,1)S(1)}, u32[]{:S(2)}, u32[]{:S(2)}) %collective-permute-start.3) | collective-permute-done | bytes 884768 | tf_op jit(solution)/shard_map/ppermute | solution.py:32
  1005.8 10.6 collective-permute-start.31
  1020.2 10.4 collective-permute-done.23
  1037.9 11.4 collective-permute-done.31
  1056.9 11.4 collective-permute-done.14
  1128.7 15.1 %multiply_subtract_fusion = (f32[144,6912]{1,0:T(8,128)}, f32[144,6912]{1,0:T(8,128)}, f32[144,6912]{1,0:T(8,128)}) fusion(f32[144,6912]{1,0:T(8,128)} %param.30, f32[144,6912]{1,0:T(8,128)} %param.31, f32[144,6912]{1,0:T(8,128)} %param.32, f32[128,9216]{1,0:T(8,128)} %reshape.340, bf16[128,1152]{1,0:T(8,128)(2,1)} %reshape.338, s32[]{:T(128)S(6)} %select_n.328), kind=kOutput, calls=%fused_computation.98 | convolution fusion | flops 1543753728 | bytes 27492356 | tf_op jit(solution)/shard_map/dot_general | solution.py:68
  (569 shorter events, 610.2 us)
Async XLA Ops:
  7.2 283.5 %all-reduce.4.cloned.1.call-start = ((), (), s32[]{:S(2)}) async-start(), calls=%async_computation.1 | async-start | bytes 1769472
  37.3 1082.9 %all-gather.5.cloned.1.call-start = ((), (), s32[]{:S(2)}) async-start(), calls=%async_computation | async-start | bytes 4866048 | tf_op jit(solution)/shard_map/all_gather | solution.py:490
  430.2 383.3 %collective-permute-start.36 = (bf16[768,1152]{1,0:T(8,128)(2,1)}, bf16[768,1152]{1,0:T(8,128)(2,1)}, u32[]{:S(2)}, u32[]{:S(2)}) collective-permute-start(bf16[768,1152]{1,0:T(8,128)(2,1)} %get-tuple-element.228), channel_id=1, source_target_pairs={{0,1},{1,0},{2,3},{3,2},{4,5},{5,4},{6,7},{7,6},{8,9},{9,8},{10,11... | collective-permute-start | bytes 5308424 | tf_op jit(solution)/shard_map/ppermute | solution.py:44
  473.8 352.7 %collective-permute-start.18 = (bf16[768,1152]{1,0:T(8,128)(2,1)}, bf16[768,1152]{1,0:T(8,128)(2,1)}, u32[]{:S(2)}, u32[]{:S(2)}) collective-permute-start(bf16[768,1152]{1,0:T(8,128)(2,1)} %get-tuple-element.243), channel_id=1, source_target_pairs={{0,1},{1,0},{2,3},{3,2},{4,5},{5,4},{6,7},{7,6},{8,9},{9,8},{10,11... | collective-permute-start | bytes 5308424 | tf_op jit(solution)/shard_map/ppermute | solution.py:44
  709.7 130.8 %collective-permute-start.9 = (bf16[768,1152]{1,0:T(8,128)(2,1)}, bf16[768,1152]{1,0:T(8,128)(2,1)}, u32[]{:S(2)}, u32[]{:S(2)}) collective-permute-start(bf16[768,1152]{1,0:T(8,128)(2,1)} %copy.109), channel_id=1, source_target_pairs={{0,1},{1,0},{2,3},{3,2},{4,5},{5,4},{6,7},{7,6},{8,9},{9,8},{10,11... | collective-permute-start | bytes 5308424 | tf_op jit(solution)/shard_map/ppermute | solution.py:44
  785.7 32.0 %collective-permute-start.44 = (bf16[1152,768]{1,0:T(8,128)(2,1)S(1)}, bf16[1152,768]{1,0:T(8,128)(2,1)S(1)}, u32[]{:S(2)}, u32[]{:S(2)}) collective-permute-start(bf16[1152,768]{1,0:T(8,128)(2,1)S(1)} %bitcast.499), channel_id=1, source_target_pairs={{0,1},{1,0},{2,3},{3,2},{4,5},{5,4},{6,7},{7,6},{8,9},{9,8},{10,11... | collective-permute-start | bytes 5308424 | tf_op jit(solution)/shard_map/ppermute | solution.py:44
  839.2 34.2 %collective-permute-start.45 = (bf16[8,48,1152]{2,1,0:T(8,128)(2,1)S(1)}, bf16[8,48,1152]{2,1,0:T(8,128)(2,1)S(1)}, u32[]{:S(2)}, u32[]{:S(2)}) collective-permute-start(bf16[8,48,1152]{2,1,0:T(8,128)(2,1)S(1)} %get-tuple-element.262), channel_id=1, source_target_pairs={{0,2},{1,3},{2,0},{3,1},{4,6},{5,7},{6,4},{7,5},{8,10},{9,11},{10,... | collective-permute-start | bytes 2654216 | tf_op jit(solution)/shard_map/ppermute | solution.py:40
  840.5 51.8 %collective-permute-start.20 = (bf16[8,48,1152]{2,1,0:T(8,128)(2,1)S(1)}, bf16[8,48,1152]{2,1,0:T(8,128)(2,1)S(1)}, u32[]{:S(2)}, u32[]{:S(2)}) collective-permute-start(bf16[8,48,1152]{2,1,0:T(8,128)(2,1)S(1)} %get-tuple-element.264), channel_id=1, source_target_pairs={{0,2},{1,3},{2,0},{3,1},{4,6},{5,7},{6,4},{7,5},{8,10},{9,11},{10,... | collective-permute-start | bytes 2654216 | tf_op jit(solution)/shard_map/ppermute | solution.py:40
  840.8 70.6 %collective-permute-start.28 = (bf16[8,48,1152]{2,1,0:T(8,128)(2,1)S(1)}, bf16[8,48,1152]{2,1,0:T(8,128)(2,1)S(1)}, u32[]{:S(2)}, u32[]{:S(2)}) collective-permute-start(bf16[8,48,1152]{2,1,0:T(8,128)(2,1)S(1)} %get-tuple-element.266), channel_id=1, source_target_pairs={{0,2},{1,3},{2,0},{3,1},{4,6},{5,7},{6,4},{7,5},{8,10},{9,11},{10,... | collective-permute-start | bytes 2654216 | tf_op jit(solution)/shard_map/ppermute | solution.py:40
  847.8 82.5 %collective-permute-start.11 = (bf16[8,48,1152]{2,1,0:T(8,128)(2,1)S(1)}, bf16[8,48,1152]{2,1,0:T(8,128)(2,1)S(1)}, u32[]{:S(2)}, u32[]{:S(2)}) collective-permute-start(bf16[8,48,1152]{2,1,0:T(8,128)(2,1)S(1)} %get-tuple-element.268), channel_id=1, source_target_pairs={{0,2},{1,3},{2,0},{3,1},{4,6},{5,7},{6,4},{7,5},{8,10},{9,11},{10,... | collective-permute-start | bytes 2654216 | tf_op jit(solution)/shard_map/ppermute | solution.py:40
  854.5 94.8 %collective-permute-start.2 = (bf16[8,48,1152]{2,1,0:T(8,128)(2,1)S(1)}, bf16[8,48,1152]{2,1,0:T(8,128)(2,1)S(1)}, u32[]{:S(2)}, u32[]{:S(2)}) collective-permute-start(bf16[8,48,1152]{2,1,0:T(8,128)(2,1)S(1)} %get-tuple-element.270), channel_id=1, source_target_pairs={{0,2},{1,3},{2,0},{3,1},{4,6},{5,7},{6,4},{7,5},{8,10},{9,11},{10,... | collective-permute-start | bytes 2654216 | tf_op jit(solution)/shard_map/ppermute | solution.py:40
  874.2 77.8 %collective-permute-start.38 = (bf16[4,2,48,1152]{3,2,1,0:T(8,128)(2,1)S(1)}, bf16[4,2,48,1152]{3,2,1,0:T(8,128)(2,1)S(1)}, u32[]{:S(2)}, u32[]{:S(2)}) collective-permute-start(bf16[4,2,48,1152]{3,2,1,0:T(8,128)(2,1)S(1)} %bitcast.506), channel_id=1, source_target_pairs={{0,4},{4,0},{8,12},{12,8},{16,20},{20,16},{24,28},{28,24},{1,5},{5... | collective-permute-start | bytes 2654216 | tf_op jit(solution)/shard_map/ppermute | solution.py:32
  892.4 59.9 %collective-permute-start.46 = (bf16[4,2,48,1152]{3,2,1,0:T(8,128)(2,1)S(1)}, bf16[4,2,48,1152]{3,2,1,0:T(8,128)(2,1)S(1)}, u32[]{:S(2)}, u32[]{:S(2)}) collective-permute-start(bf16[4,2,48,1152]{3,2,1,0:T(8,128)(2,1)S(1)} %bitcast.503), channel_id=1, source_target_pairs={{0,4},{4,0},{8,12},{12,8},{16,20},{20,16},{24,28},{28,24},{1,5},{5... | collective-permute-start | bytes 2654216 | tf_op jit(solution)/shard_map/ppermute | solution.py:32
  912.3 40.4 %collective-permute-start.21 = (bf16[4,2,48,1152]{3,2,1,0:T(8,128)(2,1)S(1)}, bf16[4,2,48,1152]{3,2,1,0:T(8,128)(2,1)S(1)}, u32[]{:S(2)}, u32[]{:S(2)}) collective-permute-start(bf16[4,2,48,1152]{3,2,1,0:T(8,128)(2,1)S(1)} %bitcast.507), channel_id=1, source_target_pairs={{0,4},{4,0},{8,12},{12,8},{16,20},{20,16},{24,28},{28,24},{1,5},{5... | collective-permute-start | bytes 2654216 | tf_op jit(solution)/shard_map/ppermute | solution.py:32
  952.0 38.9 %collective-permute-start.3 = (bf16[4,2,48,1152]{3,2,0,1:T(8,128)(2,1)S(1)}, bf16[4,2,48,1152]{3,2,0,1:T(8,128)(2,1)S(1)}, u32[]{:S(2)}, u32[]{:S(2)}) collective-permute-start(bf16[4,2,48,1152]{3,2,0,1:T(8,128)(2,1)S(1)} %fusion.169), channel_id=1, source_target_pairs={{0,4},{4,0},{8,12},{12,8},{16,20},{20,16},{24,28},{28,24},{1,5},{5... | collective-permute-start | bytes 2654216 | tf_op jit(solution)/shard_map/ppermute | solution.py:32
  952.3 39.1 %collective-permute-start.39 = (bf16[2,48,1152]{2,1,0:T(8,128)(2,1)S(1)}, bf16[2,48,1152]{2,1,0:T(8,128)(2,1)S(1)}, u32[]{:S(2)}, u32[]{:S(2)}) collective-permute-start(bf16[2,48,1152]{2,1,0:T(8,128)(2,1)S(1)} %get-tuple-element.281), channel_id=1, source_target_pairs={{0,8},{4,12},{8,16},{12,20},{16,24},{20,28},{24,0},{28,4},{1,9},{5... | collective-permute-start | bytes 663560 | tf_op jit(solution)/shard_map/ppermute | solution.py:36
  952.7 39.1 %collective-permute-start.40 = (bf16[2,48,1152]{2,1,0:T(8,128)(2,1)S(1)}, bf16[2,48,1152]{2,1,0:T(8,128)(2,1)S(1)}, u32[]{:S(2)}, u32[]{:S(2)}) collective-permute-start(bf16[2,48,1152]{2,1,0:T(8,128)(2,1)S(1)} %get-tuple-element.283), channel_id=1, source_target_pairs={{0,16},{4,20},{8,24},{12,28},{16,0},{20,4},{24,8},{28,12},{1,17},{... | collective-permute-start | bytes 663560 | tf_op jit(solution)/shard_map/ppermute | solution.py:36
  954.0 39.0 %collective-permute-start.41 = (bf16[2,48,1152]{2,1,0:T(8,128)(2,1)S(1)}, bf16[2,48,1152]{2,1,0:T(8,128)(2,1)S(1)}, u32[]{:S(2)}, u32[]{:S(2)}) collective-permute-start(bf16[2,48,1152]{2,1,0:T(8,128)(2,1)S(1)} %get-tuple-element.282), channel_id=1, source_target_pairs={{0,24},{4,28},{8,0},{12,4},{16,8},{20,12},{24,16},{28,20},{1,25},{... | collective-permute-start | bytes 663560 | tf_op jit(solution)/shard_map/ppermute | solution.py:36
  993.0 37.6 %collective-permute-start.23 = (bf16[2,48,1152]{2,1,0:T(8,128)(2,1)S(1)}, bf16[2,48,1152]{2,1,0:T(8,128)(2,1)S(1)}, u32[]{:S(2)}, u32[]{:S(2)}) collective-permute-start(bf16[2,48,1152]{2,1,0:T(8,128)(2,1)S(1)} %get-tuple-element.289), channel_id=1, source_target_pairs={{0,16},{4,20},{8,24},{12,28},{16,0},{20,4},{24,8},{28,12},{1,17},{... | collective-permute-start | bytes 663560 | tf_op jit(solution)/shard_map/ppermute | solution.py:36
  995.2 39.0 %collective-permute-start.24 = (bf16[2,48,1152]{2,1,0:T(8,128)(2,1)S(1)}, bf16[2,48,1152]{2,1,0:T(8,128)(2,1)S(1)}, u32[]{:S(2)}, u32[]{:S(2)}) collective-permute-start(bf16[2,48,1152]{2,1,0:T(8,128)(2,1)S(1)} %get-tuple-element.288), channel_id=1, source_target_pairs={{0,24},{4,28},{8,0},{12,4},{16,8},{20,12},{24,16},{28,20},{1,25},{... | collective-permute-start | bytes 663560 | tf_op jit(solution)/shard_map/ppermute | solution.py:36
  1003.5 34.0 %collective-permute-start.30 = (bf16[2,48,1152]{2,1,0:T(8,128)(2,1)S(1)}, bf16[2,48,1152]{2,1,0:T(8,128)(2,1)S(1)}, u32[]{:S(2)}, u32[]{:S(2)}) collective-permute-start(bf16[2,48,1152]{2,1,0:T(8,128)(2,1)S(1)} %get-tuple-element.290), channel_id=1, source_target_pairs={{0,8},{4,12},{8,16},{12,20},{16,24},{20,28},{24,0},{28,4},{1,9},{5... | collective-permute-start | bytes 663560 | tf_op jit(solution)/shard_map/ppermute | solution.py:36
  1005.8 43.5 %collective-permute-start.31 = (bf16[2,48,1152]{2,1,0:T(8,128)(2,1)S(1)}, bf16[2,48,1152]{2,1,0:T(8,128)(2,1)S(1)}, u32[]{:S(2)}, u32[]{:S(2)}) collective-permute-start(bf16[2,48,1152]{2,1,0:T(8,128)(2,1)S(1)} %get-tuple-element.292), channel_id=1, source_target_pairs={{0,16},{4,20},{8,24},{12,28},{16,0},{20,4},{24,8},{28,12},{1,17},{... | collective-permute-start | bytes 663560 | tf_op jit(solution)/shard_map/ppermute | solution.py:36
  1016.5 36.6 %collective-permute-start.32 = (bf16[2,48,1152]{2,1,0:T(8,128)(2,1)S(1)}, bf16[2,48,1152]{2,1,0:T(8,128)(2,1)S(1)}, u32[]{:S(2)}, u32[]{:S(2)}) collective-permute-start(bf16[2,48,1152]{2,1,0:T(8,128)(2,1)S(1)} %get-tuple-element.291), channel_id=1, source_target_pairs={{0,24},{4,28},{8,0},{12,4},{16,8},{20,12},{24,16},{28,20},{1,25},{... | collective-permute-start | bytes 663560 | tf_op jit(solution)/shard_map/ppermute | solution.py:36
  1034.2 34.0 %collective-permute-start.14 = (bf16[2,48,1152]{2,1,0:T(8,128)(2,1)S(1)}, bf16[2,48,1152]{2,1,0:T(8,128)(2,1)S(1)}, u32[]{:S(2)}, u32[]{:S(2)}) collective-permute-start(bf16[2,48,1152]{2,1,0:T(8,128)(2,1)S(1)} %get-tuple-element.295), channel_id=1, source_target_pairs={{0,16},{4,20},{8,24},{12,28},{16,0},{20,4},{24,8},{28,12},{1,17},{... | collective-permute-start | bytes 663560 | tf_op jit(solution)/shard_map/ppermute | solution.py:36
  (97 other events, 1424.1 us)
Sparse Core Ops, SparseCore 0:
  37.5 82.5 all-reduce.3
  771.2 63.4 all-gather.4

commit v2 on v1

--- a/solution.py
+++ b/solution.py
@@ -9,6 +9,8 @@
 
 HEAD_DIM = 72
 STEP = 10
+SPAN = 256
+EXP_SCALE = HEAD_DIM**-0.5 * 1.4426950408889634
 
 bf16 = jnp.bfloat16
 f32 = jnp.float32
@@ -82,39 +84,89 @@
     return lax.dot_general(left, right, (((1,), (1,)), ((), ())), preferred_element_type=f32)
 
 
-def to_heads(values):
-    return values.reshape(values.shape[0], -1, HEAD_DIM).transpose(1, 0, 2)
-
-
-def from_heads(values):
-    return values.transpose(1, 0, 2).reshape(values.shape[1], -1)
-
-
-def soft_weights(same, query, key):
-    scores = back_dot(query, key) * HEAD_DIM ** (-0.5)
-    scores = jnp.where(same, scores, -1e30)
-    powers = jnp.exp(scores - jnp.max(scores, axis=-1, keepdims=True))
-    return powers / jnp.sum(powers, axis=-1, keepdims=True)
-
-
-def attend_head(same, operands):
-    query, key, value = operands
-    softened = soft_weights(same, query, key).astype(bf16)
-    return dot(softened, value).astype(bf16)
-
-
-def head_back(same, operands):
-    query, key, value, upstream = operands
-    softened = soft_weights(same, query, key)
-    back_value = outer(softened.astype(bf16), upstream)
-    back_soft = back_dot(upstream, value)
-    back_score = (
-        softened * (back_soft - jnp.sum(back_soft * softened, axis=-1, keepdims=True))
-    ).astype(bf16)
-    scale = HEAD_DIM ** (-0.5)
-    back_query = dot(back_score, key) * scale
-    back_key = outer(back_score, query) * scale
-    return (back_query.astype(bf16), back_key.astype(bf16), back_value.astype(bf16))
+def spread(starts, source, padded, out):
+    rows=source.shape[0]
+    padded[0:rows,:]=source[...]
+    padded[rows:,:]=jnp.zeros((padded.shape[0]-rows,padded.shape[1]),bf16)
+    def one(s,_):
+        start=starts[s]
+        base=pl.multiple_of(start//128*128,128)
+        row=lax.broadcasted_iota(jnp.int32,(SPAN,SPAN+128),0)
+        col=lax.broadcasted_iota(jnp.int32,(SPAN,SPAN+128),1)
+        pick=(col==row+(start-base))&(row<starts[s+1]-start)
+        out[s]=dot(pick.astype(bf16),padded[pl.ds(base,SPAN+128),:]).astype(bf16)
+        return 0
+    lax.fori_loop(0,out.shape[0],one,0)
+
+def unspread(starts, slabs, out):
+    n=slabs.shape[0]; rows=out.shape[0]
+    def one(i,_):
+        row=lax.broadcasted_iota(jnp.int32,(SPAN,1),0)+i*SPAN
+        home=row
+        for s in range(1,n):
+            home=home+jnp.where(row>=starts[s],SPAN-(starts[s]-starts[s-1]),0)
+        pick=(lax.broadcasted_iota(jnp.int32,(SPAN,n*SPAN),1)==home).astype(bf16)
+        out[pl.ds(pl.multiple_of(i*SPAN,SPAN),SPAN),:]=dot(pick,slabs[...].reshape(n*SPAN,slabs.shape[2])).astype(bf16)
+        return 0
+    lax.fori_loop(0,rows//SPAN,one,0)
+
+def attend_kernel(starts, q, k, v, out, qs, ks, vs, wide, os):
+    for src,dst in ((q,qs),(k,ks),(v,vs)): spread(starts,src,wide,dst)
+    n=qs.shape[0]
+    def seg(s,_):
+        length=starts[s+1]-starts[s]
+        outside=jnp.where(lax.broadcasted_iota(jnp.int32,(SPAN,1),0)<length,0.0,-1e30)
+        for h in range(qs.shape[2]//HEAD_DIM):
+            cols=slice(h*HEAD_DIM,(h+1)*HEAD_DIM)
+            score=back_dot(ks[s,:,cols],qs[s,:,cols])+outside
+            power=jnp.exp2((score-jnp.max(score,axis=0,keepdims=True))*EXP_SCALE)
+            soft=(power*(1.0/jnp.sum(power,axis=0,keepdims=True))).astype(bf16)
+            os[s,:,cols]=outer(soft,vs[s,:,cols]).astype(bf16)
+        return 0
+    lax.fori_loop(0,n,seg,0)
+    unspread(starts,os,out)
+
+def back_kernel(starts, qs, ks, vs, up, dq, dk, dv, wide, ups, dqs, dks, dvs):
+    spread(starts,up,wide,ups)
+    n=qs.shape[0]; scale=HEAD_DIM**-0.5
+    def seg(s,_):
+        length=starts[s+1]-starts[s]
+        outside=jnp.where(lax.broadcasted_iota(jnp.int32,(SPAN,1),0)<length,0.0,-1e30)
+        for h in range(qs.shape[2]//HEAD_DIM):
+            cols=slice(h*HEAD_DIM,(h+1)*HEAD_DIM)
+            query,key,value,upstream=qs[s,:,cols],ks[s,:,cols],vs[s,:,cols],ups[s,:,cols]
+            score=back_dot(key,query)+outside
+            power=jnp.exp2((score-jnp.max(score,axis=0,keepdims=True))*EXP_SCALE)
+            soft=power*(1.0/jnp.sum(power,axis=0,keepdims=True))
+            back_soft=back_dot(value,upstream)
+            mean=jnp.sum(back_soft*soft,axis=0,keepdims=True)
+            back_score=(soft*(back_soft-mean)).astype(bf16)
+            dvs[s,:,cols]=dot(soft.astype(bf16),upstream).astype(bf16)
+            dks[s,:,cols]=(dot(back_score,query)*scale).astype(bf16)
+            dqs[s,:,cols]=(outer(back_score,key)*scale).astype(bf16)
+        return 0
+    lax.fori_loop(0,n,seg,0)
+    for slabs,out in ((dqs,dq),(dks,dk),(dvs,dv)): unspread(starts,slabs,out)
+
+VM = pl.BlockSpec(memory_space=pltpu.VMEM)
+SM = pl.BlockSpec(memory_space=pltpu.SMEM)
+ANY = pl.BlockSpec(memory_space=pl.ANY)
+def attend(starts,q,k,v):
+    n=starts.shape[0]-1; rows,width=q.shape
+    slab=jax.ShapeDtypeStruct((n,SPAN,width),bf16)
+    return pl.pallas_call(attend_kernel,out_shape=(jax.ShapeDtypeStruct(q.shape,bf16),slab,slab,slab),
+        in_specs=[SM,VM,VM,VM],out_specs=(VM,)*4,
+        scratch_shapes=[pltpu.VMEM((rows+SPAN,width),bf16),pltpu.VMEM((n,SPAN,width),bf16)],
+        compiler_params=pltpu.CompilerParams(vmem_limit_bytes=56<<20),
+        cost_estimate=pl.CostEstimate(flops=2*2*16*n*SPAN*SPAN*128,bytes_accessed=rows*width*14,transcendentals=16*n*SPAN*SPAN),name="attend")(starts,q,k,v)
+def attend_back(starts,qs,ks,vs,up):
+    n=starts.shape[0]-1; rows,width=up.shape
+    slab=pltpu.VMEM((n,SPAN,width),bf16); o=jax.ShapeDtypeStruct(up.shape,bf16)
+    return pl.pallas_call(back_kernel,out_shape=(o,o,o),
+        in_specs=[SM,VM,VM,VM,VM],out_specs=(VM,)*3,
+        scratch_shapes=[pltpu.VMEM((rows+SPAN,width),bf16)]+[slab]*4,
+        compiler_params=pltpu.CompilerParams(vmem_limit_bytes=56<<20),
+        cost_estimate=pl.CostEstimate(flops=5*2*16*n*SPAN*SPAN*128,bytes_accessed=rows*width*14,transcendentals=16*n*SPAN*SPAN),name="attend_back")(starts,qs,ks,vs,up)
 
 
 def adam_update(gradient, master, first, second):
@@ -148,11 +200,17 @@
     pl.semaphore_wait(barrier, len(peers))
 
 
-def gather_kernel(own, w_nat, w_con, w, z_s, z_r, x_s, x_r, y_s, y_r, c_s, c_r, load_sem, out_sem):
+def gather_kernel(
+    own, cond, bias, w_mod, *refs
+):
+    w_out, (w_con, modulation, biases), rest = refs[:8], refs[8:11], refs[11:]
+    w, conds, parts, x_parts, z_parts, small_s, small_r, part_s, part_r = rest[:9]
+    z_s, z_r, x_s, x_r, y_s, y_r, c_s, c_r, load_sem, out_sem = rest[9:]
     row, seg = lax.axis_index("rows"), lax.axis_index("seg")
     x, z = row % 2, row // 2
     y, c = seg // 2, seg % 2
     n = own.shape[1]
+    width = own.shape[2]
     units = own.shape[0] // 2
     piece = n // 3
     part = pl.multiple_of(y * piece, piece)
@@ -169,8 +227,54 @@
         loads.append(copy)
     z_peers = [(lax.rem(z + k, 4) * 2 + x, seg) for k in (1, 2, 3)]
     x_peer, y_peer, c_peer = (row + 1 - 2 * x, seg), (row, seg + 2 - 4 * y), (row, seg + 1 - 2 * c)
-    greet(z_peers + [x_peer, y_peer, c_peer])
+    cross_peers = [(lax.rem(z + k, 4) * 2 + 1 - x, seg) for k in (1, 2, 3)]
+    row_peers = z_peers + cross_peers + [x_peer]
+    greet(row_peers + [y_peer, c_peer])
     sent = []
+
+    small = []
+    for i, peer in enumerate(row_peers):
+        small.append(remote(cond.at[peer[0]], conds.at[row], small_s.at[i], small_r.at[i], peer))
+        small.append(remote(bias, biases.at[row], small_s.at[7 + i], small_r.at[7 + i], peer))
+    for copy in small:
+        copy.start()
+        sent.append(copy)
+    conds[row] = cond[row]
+    biases[row] = bias[...]
+
+    def to_x():
+        return remote(parts.at[:, 1 - x], x_parts, part_s.at[0], part_r.at[0], x_peer)
+
+    def to_z(k):
+        src = parts.at[lax.rem(z + k, 4), x]
+        return remote(src, z_parts.at[k - 1], part_s.at[k], part_r.at[k], z_peers[k - 1])
+
+    def multiply():
+        for copy in small:
+            copy.wait_recv()
+        left = conds[...].reshape(-1, conds.shape[2])[:, : w_mod.shape[0]].astype(bf16)
+        half = w_mod.shape[1] // 2
+        upper = lax.broadcasted_iota(jnp.int32, (left.shape[0], 1), 0) % 8 < 4
+        for start in range(0, half, width):
+            both = jnp.where(
+                upper,
+                dot(left, w_mod[:, start : start + width]),
+                dot(left, w_mod[:, half + start : half + start + width]),
+            )
+            parts[:, :, :, start : start + width] = both.reshape(4, 2, 8, width)
+        go(to_x())
+
+    def sum_x():
+        to_x().wait_recv()
+        for level in range(4):
+            parts[level, x] = parts[level, x] + x_parts[level]
+        for k in (1, 3, 2):
+            go(to_z(k))
+
+    def sum_z():
+        for k in (1, 3, 2):
+            to_z(k).wait_recv()
+        modulation[...] = parts[z, x] + z_parts[0] + z_parts[1] + z_parts[2]
 
     def along_z(u, k):
         ref = w.at[2 * u + c, row, pl.ds(part, 2 * piece)]
@@ -206,6 +310,12 @@
             else:
                 along_z(u, k).wait_recv()
             go(along_x(u, k))
+            if j == 0:
+                multiply()
+            if j == 2:
+                sum_x()
+            if j == 6:
+                sum_z()
         if 0 <= j - 1 < len(steps):
             along_x(*steps[j - 1]).wait_recv()
             go(along_y(*steps[j - 1]))
@@ -217,7 +327,7 @@
             across(u, k).wait_recv()
             if k == 2:
                 for b in (2 * u, 2 * u + 1):
-                    dst = w_nat.at[b] if u < 4 else w_con.at[:, b - 8]
+                    dst = w_out[b] if u < 4 else w_con.at[:, b - 8]
                     copy = pltpu.make_async_copy(w.at[b], dst, out_sem.at[b])
                     copy.start()
                     outs.append(copy)
@@ -227,83 +337,215 @@
         copy.wait()
 
 
-def gather_fast(attention, projection, expand, contract):
+def gather_fast(attention, projection, expand, contract, cond_silu, bias_low, mod_low):
     width = projection.shape[1]
     n = attention.shape[0]
     blocks = [attention[:, j * width : (j + 1) * width] for j in range(3)] + [projection]
     blocks += [expand[:, j * width : (j + 1) * width] for j in range(4)]
     blocks += [contract[j * n : (j + 1) * n] for j in range(4)]
     own = jnp.stack([block.astype(bf16) for block in blocks])
+    n_seg = cond_silu.shape[0]
+    cond = cond_silu.astype(f32).reshape(n_seg, 8, n).transpose(1, 0, 2)
+    cond = jnp.pad(jnp.concatenate([cond, cond], axis=1), ((0, 0), (0, 0), (0, 256 - n)))
+    n_bias = bias_low.shape[0]
+    bias = jnp.pad(bias_low, (0, 2048 - n_bias)).reshape(16, 128)
     sems = pltpu.SemaphoreType.DMA
-    w_nat, w_con = pl.pallas_call(
+    outs = pl.pallas_call(
         gather_kernel,
-        out_shape=(
-            jax.ShapeDtypeStruct((8, 8, n, width), bf16),
+        out_shape=(jax.ShapeDtypeStruct((8, n, width), bf16),) * 8
+        + (
             jax.ShapeDtypeStruct((8, 4, n, width), bf16),
+            jax.ShapeDtypeStruct((8, 3 * width), f32),
+            jax.ShapeDtypeStruct((8, 16, 128), bf16),
         ),
-        in_specs=[pl.BlockSpec(memory_space=pl.ANY)],
-        out_specs=(pl.BlockSpec(memory_space=pl.ANY),) * 2,
-        scratch_shapes=[pltpu.VMEM((12, 8, n, width), bf16)]
+        in_specs=[ANY, VM, VM, VM],
+        out_specs=(ANY,) * 9 + (VM, VM),
+        scratch_shapes=[
+            pltpu.VMEM((12, 8, n, width), bf16),
+            pltpu.VMEM((8, 8, 256), f32),
+            pltpu.VMEM((4, 2, 8, 3 * width), f32),
+            pltpu.VMEM((4, 8, 3 * width), f32),
+            pltpu.VMEM((3, 8, 3 * width), f32),
+            sems((14,)),
+            sems((14,)),
+            sems((4,)),
+            sems((4,)),
+        ]
         + [sems((6, 3))] * 2
         + [sems((6, 4))] * 6
         + [sems((6,)), sems((12,))],
         compiler_params=pltpu.CompilerParams(
-            collective_id=0, has_side_effects=True, vmem_limit_bytes=48 << 20
+            collective_id=0, has_side_effects=True, vmem_limit_bytes=50 << 20
         ),
         name="gather_weights",
-    )(own)
-    w_nat = w_nat.reshape(8, 8 * n, width)
-    return (
-        (w_nat[0], w_nat[1], w_nat[2]),
-        w_nat[3],
-        (w_nat[4], w_nat[5], w_nat[6], w_nat[7]),
-        w_con.reshape(32 * n, width),
-    )
-
-
-def gather_plain(attention, projection, expand, contract):
+    )(own, cond, bias, mod_low)
+    w = [block.reshape(8 * n, width) for block in outs[:8]]
+    modulation = jnp.concatenate([outs[9][:n_seg], outs[9][n_seg:]], axis=1)
+    biases = outs[10].reshape(8, 2048)[:, :n_bias].reshape(-1)
+    return tuple(w[:3]), w[3], tuple(w[4:]), outs[8].reshape(32 * n, width), modulation, biases
+
+
+def gather_plain(attention, projection, expand, contract, cond_silu, bias_low, mod_low):
     def whole(part):
         return lax.all_gather(part.astype(bf16), "rows", axis=0, tiled=True)
 
     width = projection.shape[1]
     att, proj, exp, con = map(whole, (attention, projection, expand, contract))
+    shard = mod_low.shape[0]
+    cond = lax.all_gather(cond_silu, "rows", axis=0, tiled=True)
+    cond = lax.dynamic_slice_in_dim(cond, lax.axis_index("rows") * shard, shard, axis=1)
+    modulation = lax.psum_scatter(dot(cond, mod_low), "rows", scatter_dimension=0, tiled=True)
     return (
         tuple(att[:, j * width : (j + 1) * width] for j in range(3)),
         proj,
         tuple(exp[:, j * width : (j + 1) * width] for j in range(4)),
         con,
-    )
-
-
-def reduce_unit(part):
-    x, y, z, c = place()
-    part = part.reshape(8, 3, part.shape[0] // 24, part.shape[1])
-    there = lax.dynamic_index_in_dim(part, 1 - y, 1, False)
-    here = lax.dynamic_index_in_dim(part, y, 1, False)
-    here = here.astype(f32) + over_y(there).astype(f32)
-    pair = jnp.stack([here.astype(bf16), part[:, 2]], axis=1)
-    pair = pair.reshape((4, 2) + pair.shape[1:])
-    there = lax.dynamic_index_in_dim(pair, 1 - x, 1, False)
-    here = lax.dynamic_index_in_dim(pair, x, 1, False)
-    quad = (here.astype(f32) + over_x(there).astype(f32)).astype(bf16)
-
-    def level(k):
-        return lax.dynamic_index_in_dim(quad, lax.rem(z + k, 4), 0, False)
-
-    total = level(0).astype(f32)
-    for k in (1, 2, 3):
-        total = total + over_z(level(k), k).astype(f32)
-    total = total.astype(bf16)
-    back = over_y(total)
-    last = (total[1].astype(f32) + back[1].astype(f32)).astype(bf16)
-    first = jnp.where(y == 0, total[0], back[0])
-    second = jnp.where(y == 0, back[0], total[0])
-    mine = jnp.concatenate([first, second, last])
-    other = over_core(mine)
-    return (
-        jnp.where(c == 0, mine, other).astype(f32),
-        jnp.where(c == 0, other, mine).astype(f32),
-    )
+        modulation,
+        whole(bias_low),
+    )
+
+
+def reduce_kernel(
+    blocks, out, d, y_in, x_in, z_in, total, y2_in, grad, load, y_s, y_r, x_s, x_r, z_s, z_r, y2_s, y2_r, c_s, c_r, store
+):
+    row, seg = lax.axis_index("rows"), lax.axis_index("seg")
+    x, z = row % 2, row // 2
+    y, c = seg // 2, seg % 2
+    units, _, n, width = blocks.shape
+    piece = n // 3
+    part = pl.multiple_of(y * piece, piece)
+    mine = pl.multiple_of(y * 2 * piece, piece)
+    theirs = pl.multiple_of((1 - y) * 2 * piece, piece)
+    level = [lax.rem(z + k, 4) for k in range(4)]
+    z_peers = [(level[k] * 2 + x, seg) for k in range(4)]
+    x_peer, y_peer, c_peer = (row + 1 - 2 * x, seg), (row, seg + 2 - 4 * y), (row, seg + 1 - 2 * c)
+    loads = []
+    for u in range(units):
+        copy = pltpu.make_async_copy(blocks.at[u], d.at[u], load.at[u])
+        copy.start()
+        loads.append(copy)
+    greet(z_peers[1:] + [x_peer, y_peer, c_peer])
+    sent = []
+
+    def add(*terms):
+        result = terms[0].astype(f32)
+        for term in terms[1:]:
+            result = result + term.astype(f32)
+        return result.astype(bf16)
+
+    def to_y(u, k):
+        src = d.at[u, pl.ds(level[k] * 2, 2), pl.ds(theirs, piece)]
+        return remote(src, y_in.at[u, k], y_s.at[u, k], y_r.at[u, k], y_peer)
+
+    def to_x(u, k):
+        src = d.at[u, level[k] * 2 + 1 - x, pl.ds(part, 2 * piece)]
+        return remote(src, x_in.at[u, k], x_s.at[u, k], x_r.at[u, k], x_peer)
+
+    def to_z(u, k):
+        src = d.at[u, level[k] * 2 + x, pl.ds(part, 2 * piece)]
+        return remote(src, z_in.at[u, k - 1], z_s.at[u, k - 1], z_r.at[u, k - 1], z_peers[k])
+
+    def to_y_again(u):
+        return remote(total.at[u], y2_in.at[u], y2_s.at[u], y2_r.at[u], y_peer)
+
+    def to_core(u):
+        ref = grad.at[u, c]
+        return remote(ref, ref, c_s.at[u], c_r.at[u], c_peer)
+
+    def go(copy):
+        copy.start()
+        sent.append(copy)
+
+    steps = [(u, k) for u in range(units) for k in (1, 3, 2, 0)]
+    ahead = 5
+    outs = []
+
+    def first(j):
+        u, k = steps[j]
+        if k == 1:
+            loads[u].wait()
+        go(to_y(u, k))
+
+    for j in range(ahead):
+        first(j)
+    for j in range(len(steps) + 8):
+        if j + ahead < len(steps):
+            first(j + ahead)
+        if j < len(steps):
+            u, k = steps[j]
+            to_y(u, k).wait_recv()
+            for side in range(2):
+                r = level[k] * 2 + side
+                d[u, r, pl.ds(mine, piece)] = add(d[u, r, pl.ds(mine, piece)], y_in[u, k, side])
+            go(to_x(u, k))
+        if 0 <= j - 1 < len(steps):
+            u, k = steps[j - 1]
+            to_x(u, k).wait_recv()
+            r = level[k] * 2 + x
+            d[u, r, pl.ds(part, 2 * piece)] = add(d[u, r, pl.ds(part, 2 * piece)], x_in[u, k])
+            if k:
+                go(to_z(u, k))
+        if j >= 3 and (j - 3) % 4 == 2 and (j - 3) // 4 < units:
+            u = (j - 3) // 4
+            for k in (1, 3, 2):
+                to_z(u, k).wait_recv()
+            total[u] = add(d[u, row, pl.ds(part, 2 * piece)], z_in[u, 0], z_in[u, 1], z_in[u, 2])
+            go(to_y_again(u))
+        if j >= 4 and (j - 4) % 4 == 2 and (j - 4) // 4 < units:
+            u = (j - 4) // 4
+            to_y_again(u).wait_recv()
+            here, there = y * piece, (1 - y) * piece
+            here, there = pl.multiple_of(here, piece), pl.multiple_of(there, piece)
+            grad[u, c, pl.ds(mine, piece)] = total[u, pl.ds(here, piece)]
+            grad[u, c, pl.ds(theirs, piece)] = y2_in[u, pl.ds(there, piece)]
+            grad[u, c, pl.ds(piece, piece)] = add(
+                total[u, pl.ds(there, piece)], y2_in[u, pl.ds(here, piece)]
+            )
+            go(to_core(u))
+        if j >= 5 and (j - 5) % 4 == 2 and (j - 5) // 4 < units:
+            u = (j - 5) // 4
+            to_core(u).wait_recv()
+            copy = pltpu.make_async_copy(grad.at[u], out.at[u], store.at[u])
+            copy.start()
+            outs.append(copy)
+    for copy in sent:
+        copy.wait_send()
+    for copy in outs:
+        copy.wait()
+
+
+def reduce_units(blocks, number):
+    units = len(blocks)
+    rows, width = blocks[0].shape
+    n = rows // 8
+    sems = pltpu.SemaphoreType.DMA
+
+    def space(*shape):
+        return pltpu.VMEM(shape + (width,), bf16)
+
+    return pl.pallas_call(
+        reduce_kernel,
+        out_shape=jax.ShapeDtypeStruct((units, 2, n, width), bf16),
+        in_specs=[ANY],
+        out_specs=ANY,
+        scratch_shapes=[
+            space(units, 8, n),
+            space(units, 4, 2, n // 3),
+            space(units, 4, 2 * n // 3),
+            space(units, 3, 2 * n // 3),
+            space(units, 2 * n // 3),
+            space(units, 2 * n // 3),
+            space(units, 2, n),
+            sems((units,)),
+        ]
+        + [sems((units, 4))] * 4
+        + [sems((units, 3))] * 2
+        + [sems((units,))] * 5,
+        compiler_params=pltpu.CompilerParams(
+            collective_id=number, has_side_effects=True, vmem_limit_bytes=48 << 20
+        ),
+        name=f"reduce_{number}",
+    )(jnp.stack(blocks).reshape(units, 8, n, width))
 
 
 def reduce_fast(early, hidden_one, attended, hidden_two, activated, back_feed, back_before):
@@ -315,39 +557,39 @@
 
     act = activated.T.reshape(8, 4, width // 8, activated.shape[0])
     feed_far = over_core(back_feed)
-    results = {}
+    blocks = []
     for unit in range(2):
         mine, there = (
             lax.dynamic_index_in_dim(act, 2 * unit + which, 1, False).reshape(width, -1)
             for which in (c, 1 - c)
         )
         far = over_core(there)
-        results["con", unit] = reduce_unit((dot(mine, back_feed) + dot(far, feed_far)).astype(bf16))
+        blocks.append((dot(mine, back_feed) + dot(far, feed_far)).astype(bf16))
     two_far = over_core(hidden_two)
     for unit in range(2):
         first, second = (
             back_before[:, (2 * unit + j) * width : (2 * unit + j + 1) * width] for j in range(2)
         )
         far = over_core(pick(second, first, c))
-        results["exp", unit] = reduce_unit(
+        blocks.append(
             (outer(hidden_two, pick(first, second, c)) + outer(two_far, far)).astype(bf16)
         )
+    big = reduce_units(blocks, 1).astype(f32)
     one_far, att_far = over_core(hidden_one), over_core(attended)
 
     def late(back_query, back_key, back_value, back_project):
         far = over_core(pick(back_project, back_key, c))
         left, left_far = pick(hidden_one, attended, c), pick(one_far, att_far, c)
-        first = reduce_unit(
-            (outer(left, pick(back_key, back_project, c)) + outer(left_far, far)).astype(bf16)
-        )
+        first = (outer(left, pick(back_key, back_project, c)) + outer(left_far, far)).astype(bf16)
         far = over_core(pick(back_value, back_query, c))
-        second = reduce_unit(
-            (outer(hidden_one, pick(back_query, back_value, c)) + outer(one_far, far)).astype(bf16)
-        )
-        con = jnp.concatenate(results["con", 0] + results["con", 1], axis=0)
-        exp = jnp.concatenate(results["exp", 0] + results["exp", 1], axis=1)
-        att = jnp.concatenate([second[0], first[0], second[1]], axis=1)
-        return att, first[1], exp, con
+        second = (
+            outer(hidden_one, pick(back_query, back_value, c)) + outer(one_far, far)
+        ).astype(bf16)
+        small = reduce_units([first, second], 2).astype(f32)
+        con = big[0:2].reshape(-1, width)
+        exp = jnp.concatenate([big[2, 0], big[2, 1], big[3, 0], big[3, 1]], axis=1)
+        att = jnp.concatenate([small[1, 0], small[0, 0], small[1, 1]], axis=1)
+        return att, small[0, 1], exp, con
 
     return late
 
@@ -401,27 +643,30 @@
     row = lax.axis_index("rows")
     segments = segment_ids[0]
     onehot = (segments[:, None] == jnp.arange(n_seg, dtype=jnp.int32)[None, :]).astype(f32)
-    same = segments[:, None] == segments[None, :]
+    starts = jnp.sum(
+        segments[:, None] < jnp.arange(n_seg + 1, dtype=jnp.int32)[None, :], axis=0, dtype=jnp.int32
+    )
     tokens_wide = tokens.astype(f32)
     upstream = cotangent.astype(f32)
 
     cond_silu = jax.nn.silu(condition[0].astype(f32)).astype(bf16)
-    cond_seg = lax.all_gather(cond_silu, "rows", axis=0, tiled=True)
-    cond_mine = lax.dynamic_slice_in_dim(cond_seg, row * shard, shard, axis=1)
-    partial_mod = dot(cond_mine, modulation_master.astype(bf16))
-    modulation = lax.psum_scatter(partial_mod, "rows", scatter_dimension=0, tiled=True)
-    biases = lax.all_gather(bias_master.astype(bf16), "rows", axis=0, tiled=True).astype(f32)
+    gather = gather_fast if fast else gather_plain
+    w_att, w_proj, w_exp, w_con, modulation, biases = gather(
+        attention_master,
+        projection_master,
+        expand_master,
+        contract_master,
+        cond_silu,
+        bias_master.astype(bf16),
+        modulation_master.astype(bf16),
+    )
+    biases = biases.astype(f32)
     query_bias, value_bias, projection_bias = (
         biases[j * width : (j + 1) * width] for j in range(3)
     )
     expand_bias = biases[3 * width : 3 * width + hidden]
     contract_bias = biases[3 * width + hidden : 4 * width + hidden]
     modulation = modulation + biases[4 * width + hidden :]
-
-    gather = gather_fast if fast else gather_plain
-    w_att, w_proj, w_exp, w_con = gather(
-        attention_master, projection_master, expand_master, contract_master
-    )
 
     per_token = jnp.dot(onehot, modulation, precision=highest)
     shift_one, scale_one, gate_one, shift_two, scale_two, gate_two = jnp.split(per_token, 6, axis=1)
@@ -430,8 +675,7 @@
     query = (dot(hidden_one, w_att[0]) + query_bias).astype(bf16)
     key = dot(hidden_one, w_att[1]).astype(bf16)
     value = (dot(hidden_one, w_att[2]) + value_bias).astype(bf16)
-    heads = (to_heads(query), to_heads(key), to_heads(value))
-    attended = from_heads(lax.map(partial(attend_head, same), heads))
+    attended, *slabs = attend(starts, query, key, value)
     projected = dot(attended, w_proj) + projection_bias
     middle = tokens_wide + gate_one * projected
     normed_two, inverse_two = layer_norm(middle)
@@ -457,8 +701,7 @@
     back_gate_one = back_middle * projected
     back_project = (back_middle * gate_one).astype(bf16)
     back_attend = back_dot(back_project, w_proj).astype(bf16)
-    back_heads = lax.map(partial(head_back, same), heads + (to_heads(back_attend),))
-    back_query, back_key, back_value = (from_heads(part) for part in back_heads)
+    back_query, back_key, back_value = attend_back(starts, *slabs, back_attend)
     grad_att, grad_proj, grad_exp, grad_con = late(back_query, back_key, back_value, back_project)
     back_hidden_one = (
         back_dot(back_query, w_att[0]) + back_dot(back_key, w_att[1]) + back_dot(back_value, w_att[2])

time: 1160 us -> 851 us (0.73)
  Pallas kernels: 146 us -> 432 us
  matrix products: 455 us -> 242 us
  waiting for transfers between devices: 173 us -> 0.04 us
  starting transfers between devices: 74.8 us -> 2.5 us
  blocking collectives: 108 us -> 41.7 us
  local copies, waits for them, and re-layouts: 108 us -> 56.9 us
  other arithmetic: 69.3 us -> 49.6 us
    pallas_call x1 -> x5, Pallas kernels: 146 us -> 432 us  [the longest x2 192 us: reduce_units(): pl.pallas_call(reduce_kernel, out_shape=jax.ShapeDtypeStruct((units, 2, n...]
    ppermute x36 -> x0, waiting for transfers between devices: 172 us -> none  [the longest x12 90 us: over_y(): return lax.ppermute(v, 'seg', SEG_Y)]
    dot_general x57 -> x9, matrix products: 156 us -> 70 us  [back_dot(): lax.dot_general(left, right, (((1,), (1,)), ((), ())), preferred_element_...]
    dot_general x47 -> x15, matrix products: 143 us -> 74.3 us  [outer(): lax.dot_general(left, right, (((0,), (0,)), ((), ())), precision=precisio...]
    ppermute x36 -> x0, starting transfers between devices: 60 us -> none  [the longest x18 39.6 us: over_z(): return lax.ppermute(v, 'rows', ROW_Z[k])]
    dot_general x46 -> x13, matrix products: 146 us -> 89.1 us  [dot(): return jnp.dot(left, right, preferred_element_type=f32)]
    unnamed x1 -> x0, blocking collectives: 29.9 us -> none
    all_gather x1 -> x0, blocking collectives: 25.6 us -> none  [on_device(): cond_seg = lax.all_gather(cond_silu, 'rows', axis=0, tiled=True)]
  transfers between devices with their start and end apart: 54 -> 11, of which waited for: 19 -> 0; matrix products, arithmetic and copies ran while one was open for 39% -> 31% of each run, Pallas kernels for 13% -> 28%
where the time goes in v2:
time: 851 us; the launch traced here: 841 us
  Pallas kernels  432 us (51%)
  matrix products  242 us (28%)
  local copies, waits for them, and re-layouts  56.9 us (7%)
  other arithmetic  49.6 us (6%)
  blocking collectives  41.7 us (5%)
  between operations  15.2 us (2%)
    pallas_call x2, Pallas kernels, reduce_units(): pl.pallas_call(reduce_kernel, out_shape=jax.ShapeDtypeStruct((units, 2, n...  192 us
    pallas_call x1, Pallas kernels, gather_fast(): pl.pallas_call(gather_kernel, out_shape=(jax.ShapeDtypeStruct((8, n, widt...  165 us
    dot_general x13, matrix products, dot(): return jnp.dot(left, right, preferred_element_type=f32)  89.1 us
    dot_general x15, matrix products, outer(): lax.dot_general(left, right, (((0,), (0,)), ((), ())), precision=precisio...  74.3 us
    dot_general x9, matrix products, back_dot(): lax.dot_general(left, right, (((1,), (1,)), ((), ())), preferred_element_...  70 us
    all_gather x1, blocking collectives, on_device(): cond_all = lax.all_gather(cond_silu, ('rows', 'seg'), axis=0, tiled=True)  41.7 us
    pallas_call x1, Pallas kernels, attend_back(): pl.pallas_call(back_kernel, out_shape=(o, o, o), in_specs=[SM, VM, VM, VM...  41.6 us
    pallas_call x1, Pallas kernels, attend(): pl.pallas_call(attend_kernel, out_shape=(jax.ShapeDtypeStruct(q.shape, bf...  34.5 us
  transfers between devices with their start and end apart: 11, of which 0 were waited for; matrix products, arithmetic and copies ran while one was open for 31% of the time, Pallas kernels for 28%

profile of v2, /device:TPU:1, one launch (start us, length us, event | category | flops | bytes accessed | tf_op | source)
XLA Modules:
  0.0 840.7 jit_solution(16380591225833234762)
XLA Ops:
  19.3 164.5 %gather_weights.1 = (bf16[8,144,1152]{2,1,0:T(8,128)(2,1)}, bf16[8,144,1152]{2,1,0:T(8,128)(2,1)}, bf16[8,144,1152]{2,1,0:T(8,128)(2,1)}, bf16[8,144,1152]{2,1,0...) custom-call(bf16[12,144,1152]{2,1,0:T(8,128)(2,1)} %fusion.87.own, ...), custom_call_target="tpu_custom_call" | custom-call | tf_op jit(solution)/shard_map/gather_weights/pallas_call | solution.py:353
  187.8 8.8 %fusion.86 = f32[768,6912]{1,0:T(8,128)S(1)} fusion(s32[768]{0:T(1024)S(1)} %reduce, f32[4,3456]{1,0:T(4,128)S(1)} %get-tuple-element.104, f32[4,3456]{1,0:T(4,128)S(1)} %get-tuple-element.103, f32[6912]{0:T(1024)S(1)} %slice.167), kind=kOutput, calls=%fused_computation.154 | convolution fusion | flops 254862336 | bytes 21374976 | tf_op jit(solution)/shard_map/dot_general | solution.py:671
  197.6 8.4 %convolution_convert_fusion.1.k = bf16[768,1152]{1,0:T(8,128)(2,1)} fusion(bf16[768,1152]{1,0:T(8,128)(2,1)S(1)} %fusion.21, bf16[1152,1152]{1,0:T(8,128)(2,1)} %bitcast.192), kind=kOutput, calls=%fused_computation.83 | convolution fusion | flops 2039316480 | bytes 6193152 | tf_op jit(solution)/shard_map/dot_general | solution.py:80
  213.7 34.5 %attend.1 = (bf16[768,1152]{1,0:T(8,128)(2,1)}, bf16[4,256,1152]{2,1,0:T(8,128)(2,1)}, bf16[4,256,1152]{2,1,0:T(8,128)(2,1)}, bf16[4,256,1152]{2,1,0:T(8,128)(2,1)}) custom-call(s32[5]{0:T(128)} %convert_reduce_fusion.6.starts, bf16[768,1152]{1,0:T(8,128)(2,1)} %fusion.37.q, bf16[768,1152]{1,0:T(8,128)(2,1)} %convolution_convert_fusion.1.k, ...), custom_call_target="tpu_custom_call" | custom-call | flops 2147483648 | bytes 12386304 | tf_op jit(solution)/shard_map/attend/pallas_call | solution.py:157
  248.2 8.5 %fusion.134 = (f32[768]{0:T(1024)S(1)}, f32[768,1152]{1,0:T(8,128)S(1)}, f32[768,1152]{1,0:T(8,128)}) fusion(f32[768,6912]{1,0:T(8,128)} %copy-done, bf16[768,1152]{1,0:T(8,128)(2,1)} %param.22, f32[1152]{0:T(1024)S(1)} %copy-done.56, bf16[768,1152]{1,0:T(8,128)(2,1)} %get-tuple-element.43, bf16[1152,1152]{1,0:T(8,128)(2,1)} %bitcast.196), kind=kOutput, calls=%fused_computation.238 | convolution fusion | flops 2042854656 | bytes 16817664 | tf_op jit(solution)/shard_map/dot_general | solution.py:80
  263.8 6.9 fusion.137
  288.9 28.1 %convert_reduce_fusion = (f32[4608]{0:T(1024)}, bf16[768,4608]{1,0:T(8,128)(2,1)}, bf16[768,4608]{1,0:T(8,128)(2,1)}) fusion(f32[4608]{0:T(1024)} %slice.171, f32[768,1152]{1,0:T(8,128)} %fusion.140, f32[768,1152]{1,0:T(8,128)} %fusion.139, f32[768,1152]{1,0:T(8,128)} %fusion.138, f32[768,1152]{1,0:T(8,128)} %fusion.137, ...), kind=kOutput, calls=%fused_computation.10 | convolution fusion | flops 8252812800 | bytes 40734720 | tf_op jit(solution)/shard_map/dot_general | solution.py:84
  327.8 6.4 fusion.123
  334.2 21.7 %convert_reduce_fusion.3 = (f32[1152]{0:T(1024)S(1)}, bf16[768,1152]{1,0:T(8,128)(2,1)}, f32[768,1152]{1,0:T(8,128)}, bf16[768,1152]{1,0:T(8,128)(2,1)}, f32[768,1152]{1,0:T(8,128)}) fusion(f32[768,6912]{1,0:T(8,128)} %copy-done, f32[768]{0:T(1024)S(1)} %get-tuple-element.113, f32[768,1152]{1,0:T(8,128)S(1)} %get-tuple-element.86, ...), kind=kOutput, calls=%fused_computation.69 | convolution fusion | flops 8169651200 | bytes 47797248 | tf_op jit(solution)/shard_map/dot_general | solution.py:80
  355.9 6.2 convolution_convert_fusion.up
  362.1 41.6 %attend_back.1 = (bf16[768,1152]{1,0:T(8,128)(2,1)}, bf16[768,1152]{1,0:T(8,128)(2,1)}, bf16[768,1152]{1,0:T(8,128)(2,1)}) custom-call(s32[5]{0:T(128)} %convert_reduce_fusion.6.starts, bf16[4,256,1152]{2,1,0:T(8,128)(2,1)} %get-tuple-element.50.qs, bf16[4,256,1152]{2,1,0:T(8,128)(2,1)} %get-tuple-element.51.ks, bf16[4,256,1152]{2,1,0:T(8,128)(2,1)} %get-tuple-element.52.vs, ...), custom_call_target="tpu_custom_call" | custom-call | flops 5368709120 | bytes 12386304 | tf_op jit(solution)/shard_map/attend_back/pallas_call | solution.py:165
  405.5 6.1 fusion.141
  419.9 6.2 convolution_add_fusion.8
  426.1 6.3 fusion.124
  446.4 10.6 %copy.55 = bf16[4608,768]{1,0:T(8,128)(2,1)} copy(bf16[4608,768]{0,1:T(8,128)(2,1)} %bitcast.176) | data formatting | bytes 14155776 | tf_op jit(solution)/shard_map/transpose | solution.py:558
  457.0 6.2 constant_dynamic-slice_fusion.2
  468.9 7.5 fusion.59
  476.4 7.5 fusion.57
  485.5 6.6 fusion.64
  503.5 41.7 %all-gather = bf16[32,4,1152]{2,1,0:T(4,128)(2,1)} all-gather(bf16[1,4,1152]{2,1,0:T(4,128)(2,1)S(1)} %fusion.118), channel_id=1, replica_groups=mesh['rows'=8,'seg'=4] {'rows','seg'}, dimensions={0}, use_global_device_ids=true | all-gather | bytes 304128 | tf_op jit(solution)/shard_map/all_gather | solution.py:734
  580.5 122.7 %reduce_1.1 = bf16[4,2,144,1152]{3,2,1,0:T(8,128)(2,1)S(1)} custom-call(bf16[4,8,144,1152]{3,2,1,0:T(8,128)(2,1)} %pad_maximum_fusion.blocks), custom_call_target="tpu_custom_call" | custom-call | tf_op jit(solution)/shard_map/reduce_1/pallas_call | solution.py:526
  703.7 6.2 fusion.8
  717.6 69.1 %reduce_2.1 = bf16[2,2,144,1152]{3,2,1,0:T(8,128)(2,1)S(1)} custom-call(bf16[2,8,144,1152]{3,2,1,0:T(8,128)(2,1)} %pad_maximum_fusion.1.blocks), custom_call_target="tpu_custom_call" | custom-call | tf_op jit(solution)/shard_map/reduce_2/pallas_call | solution.py:526
  817.8 15.1 %multiply_subtract_fusion = (f32[144,6912]{1,0:T(8,128)}, f32[144,6912]{1,0:T(8,128)}, f32[144,6912]{1,0:T(8,128)}) fusion(f32[144,6912]{1,0:T(8,128)} %param.26, f32[144,6912]{1,0:T(8,128)} %param.27, f32[144,6912]{1,0:T(8,128)} %param.28, f32[128,9216]{1,0:T(8,128)} %reshape.196, bf16[128,1152]{1,0:T(8,128)(2,1)} %reshape.194, s32[]{:T(128)S(6)} %select_n.70), kind=kOutput, calls=%fused_computation.43 | convolution fusion | flops 1543753728 | bytes 27492356 | tf_op jit(solution)/shard_map/dot_general | solution.py:70
  (285 shorter events, 178.0 us)
Async XLA Ops:
  7.2 801.9 %all-gather.4.cloned.1.call-start = ((), (), s32[]{:S(2)}) async-start(), calls=%async_computation | async-start | bytes 4866048 | tf_op jit(solution)/shard_map/all_gather | solution.py:733
  184.0 12.6 %copy-start.45 = (f32[16128]{0:T(1024)}, f32[16128]{0:T(1024)S(1)}, u32[]{:S(2)}) copy-start(f32[16128]{0:T(1024)S(1)} %reshape.191) | copy-start | bytes 193540
  197.5 12.4 %copy-start.36 = (bf16[768,1152]{1,0:T(8,128)(2,1)}, bf16[768,1152]{1,0:T(8,128)(2,1)S(1)}, u32[]{:S(2)}) copy-start(bf16[768,1152]{1,0:T(8,128)(2,1)S(1)} %fusion.21) | copy-start | bytes 5308420
  213.7 34.5 %copy-start.56 = (f32[1152]{0:T(1024)S(1)}, f32[1152]{0:T(1024)}, u32[]{:S(2)}) copy-start(f32[1152]{0:T(1024)} %get-tuple-element.106) | copy-start | bytes 13828
  213.7 43.5 %slice-start = ((s8[21233664]{0:T(1024)(128)(4,1)}), s8[4194304]{0:T(1024)(128)(4,1)S(1)}, s32[]{:S(2)}) async-start(s8[21233664]{0:T(1024)(128)(4,1)} %bitcast.173), calls=%async_computation.1 | async-start | bytes 8388608
  213.7 43.5 %slice-start.1 = ((s8[21233664]{0:T(1024)(128)(4,1)}), s8[262144]{0:T(1024)(128)(4,1)S(1)}, s32[]{:S(2)}) async-start(s8[21233664]{0:T(1024)(128)(4,1)} %bitcast.173), calls=%async_computation.2 | async-start | bytes 524288
  248.2 9.9 %slice-start.5 = ((s8[21233664]{0:T(1024)(128)(4,1)}), s8[4194304]{0:T(1024)(128)(4,1)S(1)}, s32[]{:S(2)}) async-start(s8[21233664]{0:T(1024)(128)(4,1)} %bitcast.173), calls=%async_computation.6 | async-start | bytes 8388608
  262.0 293.9 %collective-permute-start.5 = (bf16[768,1152]{1,0:T(8,128)(2,1)}, bf16[768,1152]{1,0:T(8,128)(2,1)}, u32[]{:S(2)}, u32[]{:S(2)}) collective-permute-start(bf16[768,1152]{1,0:T(8,128)(2,1)} %get-tuple-element.79), channel_id=1, source_target_pairs={{0,1},{1,0},{2,3},{3,2},{4,5},{5,4},{6,7},{7,6},{8,9},{9,8},{10,11... | collective-permute-start | bytes 5308424 | tf_op jit(solution)/shard_map/ppermute | solution.py:46
  262.0 304.2 %collective-permute-start.7 = (bf16[768,1152]{1,0:T(8,128)(2,1)}, bf16[768,1152]{1,0:T(8,128)(2,1)}, u32[]{:S(2)}, u32[]{:S(2)}) collective-permute-start(bf16[768,1152]{1,0:T(8,128)(2,1)} %get-tuple-element.88), channel_id=1, source_target_pairs={{0,1},{1,0},{2,3},{3,2},{4,5},{5,4},{6,7},{7,6},{8,9},{9,8},{10,11... | collective-permute-start | bytes 5308424 | tf_op jit(solution)/shard_map/ppermute | solution.py:46
  362.1 43.4 %copy-start.63 = (bf16[8,144,1152]{2,1,0:T(8,128)(2,1)S(1)}, bf16[8,144,1152]{2,1,0:T(8,128)(2,1)}, u32[]{:S(2)}) copy-start(bf16[8,144,1152]{2,1,0:T(8,128)(2,1)} %get-tuple-element.40) | copy-start | bytes 7962628
  405.5 10.4 %copy-start.52 = (f32[4608]{0:T(1024)S(1)}, f32[4608]{0:T(1024)}, u32[]{:S(2)}) copy-start(f32[4608]{0:T(1024)} %get-tuple-element.80) | copy-start | bytes 55300
  405.5 11.7 %copy-start.49 = (f32[1152]{0:T(1024)S(1)}, f32[1152]{0:T(1024)}, u32[]{:S(2)}) copy-start(f32[1152]{0:T(1024)} %get-tuple-element.78) | copy-start | bytes 13828
  463.2 92.5 %collective-permute-start.4 = (bf16[1152,768]{1,0:T(8,128)(2,1)}, bf16[1152,768]{1,0:T(8,128)(2,1)}, u32[]{:S(2)}, u32[]{:S(2)}) collective-permute-start(bf16[1152,768]{1,0:T(8,128)(2,1)} %bitcast.35), channel_id=1, source_target_pairs={{0,1},{1,0},{2,3},{3,2},{4,5},{5,4},{6,7},{7,6},{8,9},{9,8},{10,11... | collective-permute-start | bytes 5308424 | tf_op jit(solution)/shard_map/ppermute | solution.py:46
  463.2 97.8 %collective-permute-start.6 = (bf16[1152,768]{1,0:T(8,128)(2,1)}, bf16[1152,768]{1,0:T(8,128)(2,1)}, u32[]{:S(2)}, u32[]{:S(2)}) collective-permute-start(bf16[1152,768]{1,0:T(8,128)(2,1)} %bitcast.38), channel_id=1, source_target_pairs={{0,1},{1,0},{2,3},{3,2},{4,5},{5,4},{6,7},{7,6},{8,9},{9,8},{10,11... | collective-permute-start | bytes 5308424 | tf_op jit(solution)/shard_map/ppermute | solution.py:46
  468.9 96.9 %collective-permute-start.8 = (bf16[768,1152]{1,0:T(8,128)(2,1)}, bf16[768,1152]{1,0:T(8,128)(2,1)}, u32[]{:S(2)}, u32[]{:S(2)}) collective-permute-start(bf16[768,1152]{1,0:T(8,128)(2,1)} %get-tuple-element.94), channel_id=1, source_target_pairs={{0,1},{1,0},{2,3},{3,2},{4,5},{5,4},{6,7},{7,6},{8,9},{9,8},{10,11... | collective-permute-start | bytes 5308424 | tf_op jit(solution)/shard_map/ppermute | solution.py:46
  555.6 154.3 %collective-permute-start.1 = (bf16[768,1152]{1,0:T(8,128)(2,1)}, bf16[768,1152]{1,0:T(8,128)(2,1)}, u32[]{:S(2)}, u32[]{:S(2)}) collective-permute-start(bf16[768,1152]{1,0:T(8,128)(2,1)} %get-tuple-element.43), channel_id=1, source_target_pairs={{0,1},{1,0},{2,3},{3,2},{4,5},{5,4},{6,7},{7,6},{8,9},{9,8},{10,11... | collective-permute-start | bytes 5308424 | tf_op jit(solution)/shard_map/ppermute | solution.py:46
  555.9 15.1 %collective-permute-start.9 = (bf16[768,1152]{1,0:T(8,128)(2,1)S(1)}, bf16[768,1152]{1,0:T(8,128)(2,1)S(1)}, u32[]{:S(2)}, u32[]{:S(2)}) collective-permute-start(bf16[768,1152]{1,0:T(8,128)(2,1)S(1)} %copy-done.39), channel_id=1, source_target_pairs={{0,1},{1,0},{2,3},{3,2},{4,5},{5,4},{6,7},{7,6},{8,9},{9,8},{10,11... | collective-permute-start | bytes 5308424 | tf_op jit(solution)/shard_map/ppermute | solution.py:46
  556.3 10.1 %slice-start.11 = ((s8[5308416]{0:T(1024)(128)(4,1)}), s8[4194304]{0:T(1024)(128)(4,1)S(1)}, s32[]{:S(2)}) async-start(s8[5308416]{0:T(1024)(128)(4,1)} %bitcast.208), calls=%async_computation.12 | async-start | bytes 8388608
  560.9 142.8 %collective-permute-start = (bf16[768,1152]{1,0:T(8,128)(2,1)S(1)}, bf16[768,1152]{1,0:T(8,128)(2,1)}, u32[]{:S(2)}, u32[]{:S(2)}) collective-permute-start(bf16[768,1152]{1,0:T(8,128)(2,1)S(1)} %copy-done.38), channel_id=1, source_target_pairs={{0,1},{1,0},{2,3},{3,2},{4,5},{5,4},{6,7},{7,6},{8,9},{9,8},{10,11... | collective-permute-start | bytes 5308424 | tf_op jit(solution)/shard_map/ppermute | solution.py:46
  565.8 144.1 %collective-permute-start.2 = (bf16[768,1152]{1,0:T(8,128)(2,1)S(1)}, bf16[768,1152]{1,0:T(8,128)(2,1)}, u32[]{:S(2)}, u32[]{:S(2)}) collective-permute-start(bf16[768,1152]{1,0:T(8,128)(2,1)S(1)} %broadcast_select_fusion.2), channel_id=1, source_target_pairs={{0,1},{1,0},{2,3},{3,2},{4,5},{5,4},{6,7},{7,6},{8,9},{9,8},{10,11... | collective-permute-start | bytes 5308424 | tf_op jit(solution)/shard_map/ppermute | solution.py:46
  566.2 137.5 %collective-permute-start.3 = (bf16[768,1152]{1,0:T(8,128)(2,1)S(1)}, bf16[768,1152]{1,0:T(8,128)(2,1)}, u32[]{:S(2)}, u32[]{:S(2)}) collective-permute-start(bf16[768,1152]{1,0:T(8,128)(2,1)S(1)} %broadcast_select_fusion.1), channel_id=1, source_target_pairs={{0,1},{1,0},{2,3},{3,2},{4,5},{5,4},{6,7},{7,6},{8,9},{9,8},{10,11... | collective-permute-start | bytes 5308424 | tf_op jit(solution)/shard_map/ppermute | solution.py:46
  817.7 15.2 %copy-start.51 = (f32[2016]{0:T(1024)S(1)}, f32[2016]{0:T(1024)}, u32[]{:S(2)}) copy-start(f32[2016]{0:T(1024)} %param.41) | copy-start | bytes 24196
  817.7 15.2 %copy-start.53 = (f32[2016]{0:T(1024)S(1)}, f32[2016]{0:T(1024)}, u32[]{:S(2)}) copy-start(f32[2016]{0:T(1024)} %param.42) | copy-start | bytes 24196
  817.8 15.1 %copy-start.54 = (f32[2016]{0:T(1024)S(1)}, f32[2016]{0:T(1024)}, u32[]{:S(2)}) copy-start(f32[2016]{0:T(1024)} %param.43) | copy-start | bytes 24196
  (68 other events, 321.1 us)
Sparse Core Ops, SparseCore 0:
  446.5 62.3 all-gather.3

commit v3 on v2

--- a/solution.py
+++ b/solution.py
@@ -84,17 +84,16 @@
     return lax.dot_general(left, right, (((1,), (1,)), ((), ())), preferred_element_type=f32)
 
 
-def spread(starts, source, padded, out):
-    rows=source.shape[0]
-    padded[0:rows,:]=source[...]
-    padded[rows:,:]=jnp.zeros((padded.shape[0]-rows,padded.shape[1]),bf16)
+def spread_rows(starts, source, s):
+    rows = source.shape[0]
+    row = lax.broadcasted_iota(jnp.int32, (SPAN, rows), 0) + starts[s]
+    col = lax.broadcasted_iota(jnp.int32, (SPAN, rows), 1)
+    pick = jnp.where((col == row) & (row < starts[s + 1]), 1.0, 0.0).astype(bf16)
+    return dot(pick, source[...])
+
+def spread(starts, source, out):
     def one(s,_):
-        start=starts[s]
-        base=pl.multiple_of(start//128*128,128)
-        row=lax.broadcasted_iota(jnp.int32,(SPAN,SPAN+128),0)
-        col=lax.broadcasted_iota(jnp.int32,(SPAN,SPAN+128),1)
-        pick=(col==row+(start-base))&(row<starts[s+1]-start)
-        out[s]=dot(pick.astype(bf16),padded[pl.ds(base,SPAN+128),:]).astype(bf16)
+        out[s]=spread_rows(starts,source,s).astype(bf16)
         return 0
     lax.fori_loop(0,out.shape[0],one,0)
 
@@ -110,24 +109,30 @@
         return 0
     lax.fori_loop(0,rows//SPAN,one,0)
 
-def attend_kernel(starts, q, k, v, out, qs, ks, vs, wide, os):
-    for src,dst in ((q,qs),(k,ks),(v,vs)): spread(starts,src,wide,dst)
-    n=qs.shape[0]
-    def seg(s,_):
-        length=starts[s+1]-starts[s]
-        outside=jnp.where(lax.broadcasted_iota(jnp.int32,(SPAN,1),0)<length,0.0,-1e30)
-        for h in range(qs.shape[2]//HEAD_DIM):
-            cols=slice(h*HEAD_DIM,(h+1)*HEAD_DIM)
-            score=back_dot(ks[s,:,cols],qs[s,:,cols])+outside
-            power=jnp.exp2((score-jnp.max(score,axis=0,keepdims=True))*EXP_SCALE)
-            soft=(power*(1.0/jnp.sum(power,axis=0,keepdims=True))).astype(bf16)
-            os[s,:,cols]=outer(soft,vs[s,:,cols]).astype(bf16)
-        return 0
-    lax.fori_loop(0,n,seg,0)
-    unspread(starts,os,out)
-
-def back_kernel(starts, qs, ks, vs, up, dq, dk, dv, wide, ups, dqs, dks, dvs):
-    spread(starts,up,wide,ups)
+def attend_slab(starts, s, qs, ks, vs, os, heads):
+    length = starts[s + 1] - starts[s]
+    outside = jnp.where(lax.broadcasted_iota(jnp.int32, (SPAN, 1), 0) < length, 0.0, -1e30)
+    for h in heads:
+        cols = slice(h * HEAD_DIM, (h + 1) * HEAD_DIM)
+        score = back_dot(ks[s, :, cols], qs[s, :, cols]) + outside
+        power = jnp.exp2((score - jnp.max(score, axis=0, keepdims=True)) * EXP_SCALE)
+        soft = (power * (1.0 / jnp.sum(power, axis=0, keepdims=True))).astype(bf16)
+        os[s, :, cols] = outer(soft, vs[s, :, cols]).astype(bf16)
+
+
+def attend_kernel(starts, q, k, v, out, qs, ks, vs, os):
+    for src, dst in ((q, qs), (k, ks), (v, vs)):
+        spread(starts, src, dst)
+
+    def seg(s, carry):
+        attend_slab(starts, s, qs, ks, vs, os, range(qs.shape[2] // HEAD_DIM))
+        return carry
+
+    lax.fori_loop(0, qs.shape[0], seg, 0)
+    unspread(starts, os, out)
+
+def back_kernel(starts, qs, ks, vs, up, dq, dk, dv, ups, dqs, dks, dvs):
+    spread(starts,up,ups)
     n=qs.shape[0]; scale=HEAD_DIM**-0.5
     def seg(s,_):
         length=starts[s+1]-starts[s]
@@ -156,7 +161,7 @@
     slab=jax.ShapeDtypeStruct((n,SPAN,width),bf16)
     return pl.pallas_call(attend_kernel,out_shape=(jax.ShapeDtypeStruct(q.shape,bf16),slab,slab,slab),
         in_specs=[SM,VM,VM,VM],out_specs=(VM,)*4,
-        scratch_shapes=[pltpu.VMEM((rows+SPAN,width),bf16),pltpu.VMEM((n,SPAN,width),bf16)],
+        scratch_shapes=[pltpu.VMEM((n,SPAN,width),bf16)],
         compiler_params=pltpu.CompilerParams(vmem_limit_bytes=56<<20),
         cost_estimate=pl.CostEstimate(flops=2*2*16*n*SPAN*SPAN*128,bytes_accessed=rows*width*14,transcendentals=16*n*SPAN*SPAN),name="attend")(starts,q,k,v)
 def attend_back(starts,qs,ks,vs,up):
@@ -164,7 +169,7 @@
     slab=pltpu.VMEM((n,SPAN,width),bf16); o=jax.ShapeDtypeStruct(up.shape,bf16)
     return pl.pallas_call(back_kernel,out_shape=(o,o,o),
         in_specs=[SM,VM,VM,VM,VM],out_specs=(VM,)*3,
-        scratch_shapes=[pltpu.VMEM((rows+SPAN,width),bf16)]+[slab]*4,
+        scratch_shapes=[slab]*4,
         compiler_params=pltpu.CompilerParams(vmem_limit_bytes=56<<20),
         cost_estimate=pl.CostEstimate(flops=5*2*16*n*SPAN*SPAN*128,bytes_accessed=rows*width*14,transcendentals=16*n*SPAN*SPAN),name="attend_back")(starts,qs,ks,vs,up)
 
@@ -178,6 +183,10 @@
         first_hat / (jnp.sqrt(second_hat) + adam_epsilon) + weight_decay * master
     )
     return (master_new, first_new, second_new)
+
+
+def gelu(v):
+    return 0.5 * v * (1.0 + jnp.tanh(0.7978845608028654 * (v + 0.044715 * (v * v * v))))
 
 
 def remote(src, dst, send, recv, device):
@@ -200,27 +209,45 @@
     pl.semaphore_wait(barrier, len(peers))
 
 
-def gather_kernel(
-    own, cond, bias, w_mod, *refs
+def layer_rows(values):
+    center = values - jnp.mean(values, axis=-1, keepdims=True)
+    return center * lax.rsqrt(jnp.mean(center * center, axis=-1, keepdims=True) + norm_epsilon)
+
+
+def forward_kernel(
+    own, cond, bias, w_mod, starts, seg_ids, tokens, *refs
 ):
-    w_out, (w_con, modulation, biases), rest = refs[:8], refs[8:11], refs[11:]
-    w, conds, parts, x_parts, z_parts, small_s, small_r, part_s, part_r = rest[:9]
-    z_s, z_r, x_s, x_r, y_s, y_r, c_s, c_r, load_sem, out_sem = rest[9:]
+    w_out, rest = refs[:8], refs[8:]
+    w_con_out, modulation, h1_out, slab_out, att_out, proj_out, mid_out, h2_out = rest[:8]
+    before_out, act_out, ff_out, y_out = rest[8:12]
+    w, w_con, conds, bias_in, bias_all, parts, x_parts, z_parts = rest[12:20]
+    slabs, padded, wide, hidden = rest[20:24]
+    small_s, small_r, part_s, part_r = rest[24:28]
+    z_s, z_r, x_s, x_r, y_s, y_r, c_s, c_r, load_sem, out_sem, save_sem = rest[28:]
     row, seg = lax.axis_index("rows"), lax.axis_index("seg")
     x, z = row % 2, row // 2
     y, c = seg // 2, seg % 2
-    n = own.shape[1]
-    width = own.shape[2]
-    units = own.shape[0] // 2
+    n, width = own.shape[1:]
+    count = tokens.shape[0]
+    units = ((0, 2), (1, 3), (4, 5), (6, 7), (8, 9), (10, 11))
     piece = n // 3
     part = pl.multiple_of(y * piece, piece)
     third = pl.multiple_of(y * 2 * piece, piece)
     far = [lax.rem(z + 4 - k, 4) for k in range(4)]
+
+    def block_of(u):
+        return units[u][0] + c * (units[u][1] - units[u][0])
+
+    def slot(u, r, rows):
+        if u < 4:
+            return w.at[block_of(u), r, rows]
+        return w_con.at[r, block_of(u) - 8, rows]
+
     loads = []
-    for u in range(units):
+    for u in range(6):
         copy = pltpu.make_async_copy(
-            own.at[2 * u + c, pl.ds(part, 2 * piece)],
-            w.at[2 * u + c, row, pl.ds(part, 2 * piece)],
+            own.at[block_of(u), pl.ds(part, 2 * piece)],
+            slot(u, row, pl.ds(part, 2 * piece)),
             load_sem.at[u],
         )
         copy.start()
@@ -232,15 +259,18 @@
     greet(row_peers + [y_peer, c_peer])
     sent = []
 
+    def go(copy):
+        copy.start()
+        sent.append(copy)
+
     small = []
     for i, peer in enumerate(row_peers):
         small.append(remote(cond.at[peer[0]], conds.at[row], small_s.at[i], small_r.at[i], peer))
-        small.append(remote(bias, biases.at[row], small_s.at[7 + i], small_r.at[7 + i], peer))
+        small.append(remote(bias, bias_in.at[row], small_s.at[7 + i], small_r.at[7 + i], peer))
     for copy in small:
-        copy.start()
-        sent.append(copy)
+        go(copy)
     conds[row] = cond[row]
-    biases[row] = bias[...]
+    bias_in[row] = bias[...]
 
     def to_x():
         return remote(parts.at[:, 1 - x], x_parts, part_s.at[0], part_r.at[0], x_peer)
@@ -252,7 +282,7 @@
     def multiply():
         for copy in small:
             copy.wait_recv()
-        left = conds[...].reshape(-1, conds.shape[2])[:, : w_mod.shape[0]].astype(bf16)
+        left = conds[...].reshape(-1, conds.shape[2])[:, :n].astype(bf16)
         half = w_mod.shape[1] // 2
         upper = lax.broadcasted_iota(jnp.int32, (left.shape[0], 1), 0) % 8 < 4
         for start in range(0, half, width):
@@ -263,6 +293,10 @@
             )
             parts[:, :, :, start : start + width] = both.reshape(4, 2, 8, width)
         go(to_x())
+        bias_all[...] = jnp.zeros_like(bias_all)
+        for r in range(8):
+            rows = slice(16 * max(r - 1, 0), 16 * max(r - 1, 0) + 32)
+            bias_all[rows] = bias_all[rows] + bias_in[r].astype(f32)
 
     def sum_x():
         to_x().wait_recv()
@@ -274,48 +308,65 @@
     def sum_z():
         for k in (1, 3, 2):
             to_z(k).wait_recv()
-        modulation[...] = parts[z, x] + z_parts[0] + z_parts[1] + z_parts[2]
+        total = parts[z, x] + z_parts[0] + z_parts[1] + z_parts[2]
+        first = 3 + w_expand // width + 1
+        for part_no in range(3):
+            cols = slice(part_no * width, (part_no + 1) * width)
+            upper = lax.broadcasted_iota(jnp.int32, (8, 1), 0) < 4
+            modulation[:, cols] = total[:, cols] + jnp.where(
+                upper, bias_row(first + part_no), bias_row(first + 3 + part_no)
+            )
+
+    w_expand = 4 * width
+
+    def bias_row(number):
+        tall = width // 128
+        return jnp.concatenate(
+            [bias_all[number * tall + i : number * tall + i + 1, :] for i in range(tall)], axis=1
+        )
 
     def along_z(u, k):
-        ref = w.at[2 * u + c, row, pl.ds(part, 2 * piece)]
+        ref = slot(u, row, pl.ds(part, 2 * piece))
         return remote(ref, ref, z_s.at[u, k - 1], z_r.at[u, k - 1], z_peers[k - 1])
 
     def along_x(u, k):
-        ref = w.at[2 * u + c, far[k] * 2 + x, pl.ds(part, 2 * piece)]
+        ref = slot(u, far[k] * 2 + x, pl.ds(part, 2 * piece))
         return remote(ref, ref, x_s.at[u, k], x_r.at[u, k], x_peer)
 
     def along_y(u, k):
-        ref = w.at[2 * u + c, pl.ds(far[k] * 2, 2), pl.ds(third, piece)]
+        ref = slot(u, pl.ds(far[k] * 2, 2), pl.ds(third, piece))
         return remote(ref, ref, y_s.at[u, k], y_r.at[u, k], y_peer)
 
     def across(u, k):
-        ref = w.at[2 * u + c, pl.ds(far[k] * 2, 2)]
+        ref = slot(u, pl.ds(far[k] * 2, 2), slice(None))
         return remote(ref, ref, c_s.at[u, k], c_r.at[u, k], c_peer)
 
-    def go(copy):
+    steps = [(u, k) for u in range(6) for k in (0, 1, 3, 2)]
+    outs, kept = [], {}
+
+    def keep(name, number, src, dst, sem):
+        kept[name, number] = save(src, dst, save_sem.at[sem])
+
+    def finish(name, number=None):
+        kept.pop((name, number)).wait()
+
+    def save(src, dst, sem):
+        copy = pltpu.make_async_copy(src, dst, sem)
         copy.start()
-        sent.append(copy)
-
-    steps = [(u, k) for u in range(units) for k in (0, 1, 3, 2)]
-    outs = []
-    for j in range(len(steps) + 3):
+        return copy
+
+    def step(j):
         if j < len(steps):
             u, k = steps[j]
             if k == 0:
                 for later in [0, 1] if u == 0 else [u + 1]:
-                    if later < units:
+                    if later < 6:
                         loads[later].wait()
                         for hop in (1, 3, 2):
                             go(along_z(later, hop))
             else:
                 along_z(u, k).wait_recv()
             go(along_x(u, k))
-            if j == 0:
-                multiply()
-            if j == 2:
-                sum_x()
-            if j == 6:
-                sum_z()
         if 0 <= j - 1 < len(steps):
             along_x(*steps[j - 1]).wait_recv()
             go(along_y(*steps[j - 1]))
@@ -326,20 +377,152 @@
             u, k = steps[j - 3]
             across(u, k).wait_recv()
             if k == 2:
-                for b in (2 * u, 2 * u + 1):
-                    dst = w_out[b] if u < 4 else w_con.at[:, b - 8]
-                    copy = pltpu.make_async_copy(w.at[b], dst, out_sem.at[b])
-                    copy.start()
-                    outs.append(copy)
+                if u < 4:
+                    for b in units[u]:
+                        outs.append(save(w.at[b], w_out[b], out_sem.at[b]))
+                elif u == 5:
+                    outs.append(save(w_con, w_con_out, out_sem.at[8]))
+
+
+    def of_segment(rows, number):
+        ids = seg_ids[rows, :]
+        base, col = number // 3 * 4, number % 3 * width
+        result = jnp.zeros((ids.shape[0], width), f32)
+        for s in range(4):
+            line = modulation[base + s : base + s + 1, col : col + width]
+            result = jnp.where(ids == s, line, result)
+        return result
+
+    def tiles(size, body):
+        def one(i, carry):
+            body(pl.ds(pl.multiple_of(i * size, size), size))
+            return carry
+
+        lax.fori_loop(0, count // size, one, 0)
+
+    def matrix(b):
+        return w[b].reshape(8 * n, width)
+
+    def norm_one():
+        def body(rows):
+            normed = layer_rows(tokens[rows, :].astype(f32))
+            padded[rows, :] = (
+                normed * (1.0 + of_segment(rows, 1)) + of_segment(rows, 0)
+            ).astype(bf16)
+
+        tiles(128, body)
+        keep("h1", None, padded, h1_out, 0)
+
+    def spread_hidden():
+        def one(s, carry):
+            slabs[3, s] = spread_rows(starts, padded, s).astype(bf16)
+            return carry
+
+        lax.fori_loop(0, 4, one, 0)
+
+    def project(which):
+        def one(s, carry):
+            result = dot(slabs[3, s], matrix(which))
+            if which != 1:
+                result = result + bias_row(which // 2)
+            slabs[which, s] = result.astype(bf16)
+            return carry
+
+        lax.fori_loop(0, 4, one, 0)
+        keep("slab", which, slabs.at[which], slab_out.at[which], 1 + which)
+
+    def attend_heads(first, last):
+        def one(s, carry):
+            attend_slab(
+                starts, s, slabs.at[0], slabs.at[1], slabs.at[2], slabs.at[3], range(first, last)
+            )
+            return carry
+
+        lax.fori_loop(0, 4, one, 0)
+
+    def gather_back():
+        finish("h1")
+        unspread(starts, slabs.at[3], padded)
+        keep("attended", None, padded, att_out, 4)
+
+    def add_projected():
+        def body(rows):
+            projected = dot(padded[rows, :], matrix(3)) + bias_row(2)
+            wide[1, rows, :] = projected
+            middle = tokens[rows, :].astype(f32) + of_segment(rows, 2) * projected
+            wide[0, rows, :] = middle
+
+        tiles(256, body)
+        keep("wide", None, wide.at[1], proj_out, 5)
+        keep("middle", None, wide.at[0], mid_out, 6)
+
+    def norm_two():
+        def body(rows):
+            normed = layer_rows(wide[0, rows, :])
+            hidden[rows, :] = (
+                normed * (1.0 + of_segment(rows, 4)) + of_segment(rows, 3)
+            ).astype(bf16)
+
+        tiles(128, body)
+        keep("h2", None, hidden, h2_out, 7)
+
+    def expand_block(j):
+        finish("wide")
+        if j < 3:
+            finish("slab", j)
+
+        def body(i, carry):
+            rows = pl.ds(pl.multiple_of(i * SPAN, SPAN), SPAN)
+            before = dot(hidden[rows, :], matrix(4 + j)) + bias_row(3 + j)
+            wide[1, rows, :] = before
+            slabs[j, i] = gelu(before).astype(bf16)
+            return carry
+
+        lax.fori_loop(0, count // SPAN, body, 0)
+        keep("wide", None, wide.at[1], before_out.at[j], 8 + j)
+        keep("act", j, slabs.at[j, pl.ds(0, 3)], act_out.at[:, :, pl.ds(j * width, width)], 12 + j)
+
+    def contract():
+        finish("wide")
+        finish("attended")
+
+        def body(i, carry):
+            rows = pl.ds(pl.multiple_of(i * SPAN, SPAN), SPAN)
+            result = dot(slabs[0, i], w_con[0:2].reshape(8 * n, width))
+            for q in range(1, 4):
+                result = result + dot(slabs[q, i], w_con[2 * q : 2 * q + 2].reshape(8 * n, width))
+            result = result + bias_row(7)
+            wide[1, rows, :] = result
+            padded[rows, :] = (wide[0, rows, :] + of_segment(rows, 5) * result).astype(bf16)
+            return carry
+
+        lax.fori_loop(0, count // SPAN, body, 0)
+        keep("wide", None, wide.at[1], ff_out, 16)
+        keep("out", None, padded, y_out, 17)
+
+    plan = [0, multiply, 1, 2, sum_x, 3, 4, sum_z, 5, norm_one, 6, spread_hidden, 7]
+    plan += [partial(project, 0), 8, partial(project, 2), 9, 10, partial(project, 1), 11]
+    for first in range(0, 16, 2):
+        plan += [partial(attend_heads, first, first + 2)] + ([12 + first // 4] if first % 4 else [])
+    plan += [gather_back, 16, add_projected, norm_two, 17]
+    plan += [partial(expand_block, 0), 18, partial(expand_block, 1), 19]
+    plan += [partial(expand_block, 2), 20, partial(expand_block, 3), 21, 22, 23, 24, 25, 26]
+    for item in plan + [contract]:
+        if isinstance(item, int):
+            step(item)
+        else:
+            item()
     for copy in sent:
         copy.wait_send()
-    for copy in outs:
+    for copy in outs + list(kept.values()):
         copy.wait()
 
 
-def gather_fast(attention, projection, expand, contract, cond_silu, bias_low, mod_low):
+def forward_fast(own_parts, cond_silu, bias_low, mod_low, starts, segments, tokens):
+    attention, projection, expand, contract = own_parts
     width = projection.shape[1]
     n = attention.shape[0]
+    count = tokens.shape[0]
     blocks = [attention[:, j * width : (j + 1) * width] for j in range(3)] + [projection]
     blocks += [expand[:, j * width : (j + 1) * width] for j in range(4)]
     blocks += [contract[j * n : (j + 1) * n] for j in range(4)]
@@ -347,25 +530,48 @@
     n_seg = cond_silu.shape[0]
     cond = cond_silu.astype(f32).reshape(n_seg, 8, n).transpose(1, 0, 2)
     cond = jnp.pad(jnp.concatenate([cond, cond], axis=1), ((0, 0), (0, 0), (0, 256 - n)))
-    n_bias = bias_low.shape[0]
-    bias = jnp.pad(bias_low, (0, 2048 - n_bias)).reshape(16, 128)
+    row = lax.axis_index("rows")
+    window = 128 * 16 * jnp.maximum(row - 1, 0)
+    bias = lax.dynamic_update_slice(
+        jnp.zeros(4096, bf16), bias_low, (row * bias_low.shape[0] - window,)
+    ).reshape(32, 128)
     sems = pltpu.SemaphoreType.DMA
+
+    def shape(dtype, *dims):
+        return jax.ShapeDtypeStruct(dims, dtype)
+
     outs = pl.pallas_call(
-        gather_kernel,
-        out_shape=(jax.ShapeDtypeStruct((8, n, width), bf16),) * 8
+        forward_kernel,
+        out_shape=(shape(bf16, 8, n, width),) * 8
         + (
-            jax.ShapeDtypeStruct((8, 4, n, width), bf16),
-            jax.ShapeDtypeStruct((8, 3 * width), f32),
-            jax.ShapeDtypeStruct((8, 16, 128), bf16),
+            shape(bf16, 8, 4, n, width),
+            shape(f32, 8, 3 * width),
+            shape(bf16, count, width),
+            shape(bf16, 3, 4, SPAN, width),
+            shape(bf16, count, width),
+            shape(f32, count, width),
+            shape(f32, count, width),
+            shape(bf16, count, width),
+            shape(f32, 4, count, width),
+            shape(bf16, count // SPAN, SPAN, 4 * width),
+            shape(f32, count, width),
+            shape(bf16, count, width),
         ),
-        in_specs=[ANY, VM, VM, VM],
-        out_specs=(ANY,) * 9 + (VM, VM),
+        in_specs=[ANY, VM, VM, VM, SM, VM, VM],
+        out_specs=(ANY,) * 9 + (VM,) + (ANY,) * 10,
         scratch_shapes=[
-            pltpu.VMEM((12, 8, n, width), bf16),
+            pltpu.VMEM((8, 8, n, width), bf16),
+            pltpu.VMEM((8, 4, n, width), bf16),
             pltpu.VMEM((8, 8, 256), f32),
+            pltpu.VMEM((8, 32, 128), bf16),
+            pltpu.VMEM((128, 128), f32),
             pltpu.VMEM((4, 2, 8, 3 * width), f32),
             pltpu.VMEM((4, 8, 3 * width), f32),
             pltpu.VMEM((3, 8, 3 * width), f32),
+            pltpu.VMEM((4, 4, SPAN, width), bf16),
+            pltpu.VMEM((count, width), bf16),
+            pltpu.VMEM((2, count, width), f32),
+            pltpu.VMEM((count, width), bf16),
             sems((14,)),
             sems((14,)),
             sems((4,)),
@@ -373,36 +579,82 @@
         ]
         + [sems((6, 3))] * 2
         + [sems((6, 4))] * 6
-        + [sems((6,)), sems((12,))],
+        + [sems((6,)), sems((9,)), sems((18,))],
         compiler_params=pltpu.CompilerParams(
-            collective_id=0, has_side_effects=True, vmem_limit_bytes=50 << 20
+            collective_id=0, has_side_effects=True, vmem_limit_bytes=60 << 20
         ),
-        name="gather_weights",
-    )(own, cond, bias, mod_low)
+        name="forward",
+    )(own, cond, bias, mod_low, starts, segments[:, None], tokens)
     w = [block.reshape(8 * n, width) for block in outs[:8]]
     modulation = jnp.concatenate([outs[9][:n_seg], outs[9][n_seg:]], axis=1)
-    biases = outs[10].reshape(8, 2048)[:, :n_bias].reshape(-1)
-    return tuple(w[:3]), w[3], tuple(w[4:]), outs[8].reshape(32 * n, width), modulation, biases
-
-
-def gather_plain(attention, projection, expand, contract, cond_silu, bias_low, mod_low):
+    weights = (tuple(w[:3]), w[3], tuple(w[4:]), outs[8].reshape(32 * n, width))
+    h1, slabs, attended, projected, middle, h2, before, act, feedforward, output = outs[10:]
+    saved = (
+        modulation,
+        h1,
+        (slabs[0], slabs[1], slabs[2]),
+        attended,
+        projected,
+        middle,
+        h2,
+        [before[j] for j in range(4)],
+        act.reshape(count, 4 * width),
+        feedforward,
+    )
+    return output, saved, weights
+
+
+def of_tokens(onehot, modulation, width):
+    rows = sum(onehot[:, s : s + 1] * modulation[s] for s in range(onehot.shape[1]))
+    return [rows[:, j * width : (j + 1) * width] for j in range(6)]
+
+
+def forward_plain(own_parts, cond_silu, bias_low, mod_low, starts, segments, tokens):
     def whole(part):
         return lax.all_gather(part.astype(bf16), "rows", axis=0, tiled=True)
 
+    attention, projection, expand, contract = own_parts
     width = projection.shape[1]
-    att, proj, exp, con = map(whole, (attention, projection, expand, contract))
+    att, w_proj, exp, w_con = map(whole, own_parts)
+    w_att = tuple(att[:, j * width : (j + 1) * width] for j in range(3))
+    w_exp = tuple(exp[:, j * width : (j + 1) * width] for j in range(4))
     shard = mod_low.shape[0]
     cond = lax.all_gather(cond_silu, "rows", axis=0, tiled=True)
     cond = lax.dynamic_slice_in_dim(cond, lax.axis_index("rows") * shard, shard, axis=1)
     modulation = lax.psum_scatter(dot(cond, mod_low), "rows", scatter_dimension=0, tiled=True)
-    return (
-        tuple(att[:, j * width : (j + 1) * width] for j in range(3)),
-        proj,
-        tuple(exp[:, j * width : (j + 1) * width] for j in range(4)),
-        con,
+    biases = whole(bias_low).astype(f32)
+    bias = [biases[j * width : (j + 1) * width] for j in range(14)]
+    modulation = modulation + biases[8 * width :]
+    onehot = (segments[:, None] == jnp.arange(cond_silu.shape[0])[None, :]).astype(f32)
+    shift_one, scale_one, gate_one, shift_two, scale_two, gate_two = of_tokens(
+        onehot, modulation, width
+    )
+    wide = tokens.astype(f32)
+    hidden_one = (layer_norm(wide)[0] * (1.0 + scale_one) + shift_one).astype(bf16)
+    query = (dot(hidden_one, w_att[0]) + bias[0]).astype(bf16)
+    key = dot(hidden_one, w_att[1]).astype(bf16)
+    value = (dot(hidden_one, w_att[2]) + bias[1]).astype(bf16)
+    attended, *slabs = attend(starts, query, key, value)
+    projected = dot(attended, w_proj) + bias[2]
+    middle = wide + gate_one * projected
+    hidden_two = (layer_norm(middle)[0] * (1.0 + scale_two) + shift_two).astype(bf16)
+    before = [dot(hidden_two, part) + bias[3 + j] for j, part in enumerate(w_exp)]
+    activated = jnp.concatenate([gelu(part).astype(bf16) for part in before], axis=1)
+    feedforward = dot(activated, w_con) + bias[7]
+    output = (middle + gate_two * feedforward).astype(bf16)
+    saved = (
         modulation,
-        whole(bias_low),
-    )
+        hidden_one,
+        slabs,
+        attended,
+        projected,
+        middle,
+        hidden_two,
+        before,
+        activated,
+        feedforward,
+    )
+    return output, saved, (w_att, w_proj, w_exp, w_con)
 
 
 def reduce_kernel(
@@ -650,48 +902,41 @@
     upstream = cotangent.astype(f32)
 
     cond_silu = jax.nn.silu(condition[0].astype(f32)).astype(bf16)
-    gather = gather_fast if fast else gather_plain
-    w_att, w_proj, w_exp, w_con, modulation, biases = gather(
-        attention_master,
-        projection_master,
-        expand_master,
-        contract_master,
+    forward = forward_fast if fast else forward_plain
+    output, saved, (w_att, w_proj, w_exp, w_con) = forward(
+        (attention_master, projection_master, expand_master, contract_master),
         cond_silu,
         bias_master.astype(bf16),
         modulation_master.astype(bf16),
-    )
-    biases = biases.astype(f32)
-    query_bias, value_bias, projection_bias = (
-        biases[j * width : (j + 1) * width] for j in range(3)
-    )
-    expand_bias = biases[3 * width : 3 * width + hidden]
-    contract_bias = biases[3 * width + hidden : 4 * width + hidden]
-    modulation = modulation + biases[4 * width + hidden :]
-
-    per_token = jnp.dot(onehot, modulation, precision=highest)
-    shift_one, scale_one, gate_one, shift_two, scale_two, gate_two = jnp.split(per_token, 6, axis=1)
+        starts,
+        segments,
+        tokens,
+    )
+    (
+        modulation,
+        hidden_one,
+        slabs,
+        attended,
+        projected,
+        middle,
+        hidden_two,
+        before,
+        activated,
+        feedforward,
+    ) = saved
+    shift_one, scale_one, gate_one, shift_two, scale_two, gate_two = of_tokens(
+        onehot, modulation, width
+    )
     normed_one, inverse_one = layer_norm(tokens_wide)
-    hidden_one = (normed_one * (1.0 + scale_one) + shift_one).astype(bf16)
-    query = (dot(hidden_one, w_att[0]) + query_bias).astype(bf16)
-    key = dot(hidden_one, w_att[1]).astype(bf16)
-    value = (dot(hidden_one, w_att[2]) + value_bias).astype(bf16)
-    attended, *slabs = attend(starts, query, key, value)
-    projected = dot(attended, w_proj) + projection_bias
-    middle = tokens_wide + gate_one * projected
     normed_two, inverse_two = layer_norm(middle)
-    hidden_two = (normed_two * (1.0 + scale_two) + shift_two).astype(bf16)
-    before = (
-        jnp.concatenate([dot(hidden_two, part) for part in w_exp], axis=1) + expand_bias
-    )
-    activated = jax.nn.gelu(before, approximate=True).astype(bf16)
-    feedforward = dot(activated, w_con) + contract_bias
-    output = middle + gate_two * feedforward
 
     back_gate_two = upstream * feedforward
     back_feed = (upstream * gate_two).astype(bf16)
-    back_active = back_dot(back_feed, w_con)
-    gelu_pull = jax.vjp(partial(jax.nn.gelu, approximate=True), before)[1]
-    back_before = gelu_pull(back_active)[0].astype(bf16)
+    back_before = []
+    for j, part in enumerate(before):
+        back_active = back_dot(back_feed, w_con[j * width : (j + 1) * width])
+        back_before.append(jax.vjp(gelu, part)[1](back_active)[0].astype(bf16))
+    back_before = jnp.concatenate(back_before, axis=1)
     reduce = reduce_fast if fast else reduce_plain
     late = reduce(None, hidden_one, attended, hidden_two, activated, back_feed, back_before)
     back_hidden_two = sum(
@@ -729,14 +974,17 @@
             for part in (back_query, back_value, back_project, back_before, back_feed)
         ]
     )
-    payload = jnp.concatenate([back_modulation, columns.reshape(n_seg, -1)], axis=1)
+    payload = jnp.concatenate(
+        [back_modulation, columns.reshape(n_seg, -1), cond_silu.astype(f32)], axis=1
+    )
     everyone = lax.all_gather(payload, ("rows", "seg"), axis=0, tiled=True)
-    cond_all = lax.all_gather(cond_silu, ("rows", "seg"), axis=0, tiled=True)
     mod_all = everyone[:, : 6 * width]
-    cond_rows = lax.dynamic_slice_in_dim(cond_all, row * shard, shard, axis=1)
-    grad_mod = outer(cond_rows.astype(f32), mod_all, highest)
+    cond_rows = lax.dynamic_slice_in_dim(
+        everyone, everyone.shape[1] - width + row * shard, shard, axis=1
+    )
+    grad_mod = outer(cond_rows, mod_all, highest)
     devices = everyone.shape[0] // n_seg
-    rest = jnp.sum(everyone[:, 6 * width :].reshape(devices, -1), axis=0)
+    rest = jnp.sum(everyone[:, 6 * width : -width].reshape(devices, -1), axis=0)
     grad_bias = lax.dynamic_slice_in_dim(
         jnp.concatenate([rest, jnp.sum(mod_all, axis=0)]),
         row * bias_master.shape[0],
@@ -754,7 +1002,7 @@
         )
     ]
     flat = tuple((item for result in results for item in result))
-    return (output.astype(bf16), back_tokens.astype(bf16)) + flat
+    return (output, back_tokens.astype(bf16)) + flat
 
 
 def solution(mesh):

time: 851 us -> 778 us (0.914)
  matrix products: 242 us -> 165 us
  blocking collectives: 41.7 us -> 0 us
  local copies, waits for them, and re-layouts: 56.9 us -> 77.6 us
  Pallas kernels: 432 us -> 448 us
    dot_general x13 -> x4, matrix products: 89.1 us -> 18.3 us  [dot(): return jnp.dot(left, right, preferred_element_type=f32)]
    all_gather x1 -> x0, blocking collectives: 41.7 us -> none  [on_device(): cond_all = lax.all_gather(cond_silu, ('rows', 'seg'), axis=0, tiled=True)]
    pallas_call x2 -> x1, Pallas kernels: 199 us -> 211 us  [forward_fast(): pl.pallas_call(forward_kernel, out_shape=(shape(bf16, 8, n, width),) * 8...]
    transpose x1 -> x0, local copies, waits for them, and re-layouts: 10.6 us -> none  [reduce_fast(): act = activated.T.reshape(8, 4, width // 8, activated.shape[0])]
    reshape x2, local copies, waits for them, and re-layouts: 0.34 us -> 10.6 us  [the longest x1 10.3 us: forward_fast(): act.reshape(count, 4 * width)]
    dot_general x1 -> x0, matrix products: 8.82 us -> none  [on_device(): per_token = jnp.dot(onehot, modulation, precision=highest)]
    unnamed x177 -> x191, local copies, waits for them, and re-layouts: 31.9 us -> 40.3 us
    dot_general x9 -> x12, matrix products: 70 us -> 73.6 us  [back_dot(): lax.dot_general(left, right, (((1,), (1,)), ((), ())), preferred_element_...]
  transfers between devices with their start and end apart: 11 -> 11, of which waited for: 0 -> 0; matrix products, arithmetic and copies ran while one was open for 31% -> 30% of each run, Pallas kernels for 28% -> 31%
where the time goes in v3:
time: 778 us; the launch traced here: 768 us
  Pallas kernels  448 us (58%)
  matrix products  165 us (21%)
  local copies, waits for them, and re-layouts  77.6 us (10%)
  other arithmetic  57.9 us (7%)
  between operations  15.2 us (2%)
    pallas_call x1, Pallas kernels, forward_fast(): pl.pallas_call(forward_kernel, out_shape=(shape(bf16, 8, n, width),) * 8...  211 us
    pallas_call x2, Pallas kernels, reduce_units(): pl.pallas_call(reduce_kernel, out_shape=jax.ShapeDtypeStruct((units, 2, n...  195 us
    dot_general x12, matrix products, back_dot(): lax.dot_general(left, right, (((1,), (1,)), ((), ())), preferred_element_...  73.6 us
    dot_general x15, matrix products, outer(): lax.dot_general(left, right, (((0,), (0,)), ((), ())), precision=precisio...  73.2 us
    pallas_call x1, Pallas kernels, attend_back(): pl.pallas_call(back_kernel, out_shape=(o, o, o), in_specs=[SM, VM, VM, VM...  42.2 us
    unnamed x191, local copies, waits for them, and re-layouts  40.3 us
    dot_general x4, matrix products, dot(): return jnp.dot(left, right, preferred_element_type=f32)  18.3 us
    sub x5, other arithmetic, adam_update(): master - learning * (first_hat / (jnp.sqrt(second_hat) + adam_epsilon) +...  16.1 us
  transfers between devices with their start and end apart: 11, of which 0 were waited for; matrix products, arithmetic and copies ran while one was open for 30% of the time, Pallas kernels for 31%

profile of v3, /device:TPU:1, one launch (start us, length us, event | category | flops | bytes accessed | tf_op | source)
XLA Modules:
  0.0 768.2 jit_solution(3062926243890667750)
XLA Ops:
  24.5 210.8 %forward.1 = (bf16[8,144,1152]{2,1,0:T(8,128)(2,1)}, bf16[8,144,1152]{2,1,0:T(8,128)(2,1)}, bf16[8,144,1152]{2,1,0:T(8,128)(2,1)}, bf16[8,144,1152]{2,1,0:T(8,12...) custom-call(bf16[12,144,1152]{2,1,0:T(8,128)(2,1)} %fusion.101.own, ...), custom_call_target="tpu_custom_call" | custom-call | tf_op jit(solution)/shard_map/forward/pallas_call | solution.py:543
  236.6 6.0 multiply_add_fusion
  242.6 7.1 copy-done.1
  252.8 6.1 fusion.154
  258.9 6.0 fusion.158
  264.9 6.0 fusion.156
  270.9 6.1 fusion.159
  277.8 6.9 slice_bitcast_fusion
  286.2 16.8 %broadcast_select_fusion.3 = (bf16[768,1152]{1,0:T(8,128)(2,1)}, bf16[768,1152]{1,0:T(8,128)(2,1)S(1)}, bf16[768,1152]{1,0:T(8,128)(2,1)S(1)}, bf16[768,1152]{1,...) fusion(pred[]{:T(512)S(6)} %eq.13, f32[4,768,1152]{2,1,0:T(8,128)} %get-tuple-element.45, ...), kind=kOutput, calls=%fused_computation.167 | convolution fusion | flops 2121596928 | bytes 39813120 | tf_op jit(solution)/shard_map/dot_general | solution.py:84
  312.2 6.5 convolution_add_fusion.9
  318.7 6.9 fusion.139
  333.2 42.2 %attend_back.1 = (bf16[768,1152]{1,0:T(8,128)(2,1)}, bf16[768,1152]{1,0:T(8,128)(2,1)}, bf16[768,1152]{1,0:T(8,128)(2,1)}) custom-call(s32[5]{0:T(128)} %convert_reduce_fusion.6.starts, bf16[4,256,1152]{2,1,0:T(8,128)(2,1)} %get-tuple-element.120.qs, bf16[4,256,1152]{2,1,0:T(8,128)(2,1)} %get-tuple-element.119.ks, ...), custom_call_target="tpu_custom_call" | custom-call | flops 5368709120 | bytes 12386304 | tf_op jit(solution)/shard_map/attend_back/pallas_call | solution.py:170
  395.6 6.3 fusion.140
  416.6 10.3 %copy.59 = bf16[768,4608]{0,1:T(8,128)(2,1)} copy(bf16[768,4608]{1,0:T(8,128)(2,1)} %bitcast.224) | data formatting | bytes 14155776 | tf_op jit(solution)/shard_map/reshape | solution.py:601
  426.8 6.3 constant_dynamic-slice_fusion.2
  434.2 6.5 fusion.83
  453.5 6.3 fusion.81
  459.8 6.3 fusion.85
  496.8 5.2 pad_maximum_fusion.blocks
  502.0 126.6 %reduce_1.1 = bf16[4,2,144,1152]{3,2,1,0:T(8,128)(2,1)S(1)} custom-call(bf16[4,8,144,1152]{3,2,1,0:T(8,128)(2,1)} %pad_maximum_fusion.blocks), custom_call_target="tpu_custom_call" | custom-call | tf_op jit(solution)/shard_map/reduce_1/pallas_call | solution.py:778
  629.3 6.2 fusion.1
  643.2 68.0 %reduce_2.1 = bf16[2,2,144,1152]{3,2,1,0:T(8,128)(2,1)S(1)} custom-call(bf16[2,8,144,1152]{3,2,1,0:T(8,128)(2,1)} %pad_maximum_fusion.1.blocks), custom_call_target="tpu_custom_call" | custom-call | tf_op jit(solution)/shard_map/reduce_2/pallas_call | solution.py:778
  733.5 6.3 reshape.185
  742.6 16.6 %multiply_subtract_fusion = (f32[144,6912]{1,0:T(8,128)}, f32[144,6912]{1,0:T(8,128)}, f32[144,6912]{1,0:T(8,128)}) fusion(f32[144,6912]{1,0:T(8,128)} %param.26, f32[144,6912]{1,0:T(8,128)} %param.27, f32[144,6912]{1,0:T(8,128)} %param.28, f32[128,10368]{1,0:T(8,128)} %reshape.185, s32[]{:T(128)S(6)} %select_n.74), kind=kOutput, calls=%fused_computation.46 | convolution fusion | flops 1543753728 | bytes 27557892 | tf_op jit(solution)/shard_map/dot_general | solution.py:70
  (293 shorter events, 154.7 us)
Async XLA Ops:
  7.2 726.3 %all-gather.3.cloned.1.call-start = ((), (), s32[]{:S(2)}) async-start(), calls=%async_computation | async-start | bytes 5474304 | tf_op jit(solution)/shard_map/all_gather | solution.py:980
  236.6 13.1 %copy-start.11 = (bf16[768,1152]{1,0:T(8,128)(2,1)S(1)}, bf16[768,1152]{1,0:T(8,128)(2,1)}, u32[]{:S(2)}) copy-start(bf16[768,1152]{1,0:T(8,128)(2,1)} %param.25) | copy-start | bytes 5308420
  251.9 223.0 %collective-permute-start.5 = (bf16[768,1152]{1,0:T(8,128)(2,1)}, bf16[768,1152]{1,0:T(8,128)(2,1)}, u32[]{:S(2)}, u32[]{:S(2)}) collective-permute-start(bf16[768,1152]{1,0:T(8,128)(2,1)} %get-tuple-element.103), channel_id=1, source_target_pairs={{0,1},{1,0},{2,3},{3,2},{4,5},{5,4},{6,7},{7,6},{8,9},{9,8},{10,11... | collective-permute-start | bytes 5308424 | tf_op jit(solution)/shard_map/ppermute | solution.py:46
  286.2 16.9 %copy-start.69 = (bf16[8,144,1152]{2,1,0:T(8,128)(2,1)S(1)}, bf16[8,144,1152]{2,1,0:T(8,128)(2,1)}, u32[]{:S(2)}) copy-start(bf16[8,144,1152]{2,1,0:T(8,128)(2,1)} %get-tuple-element.48) | copy-start | bytes 7962628
  305.9 12.8 %slice-start = ((s8[21233664]{0:T(1024)(128)(4,1)}), s8[4194304]{0:T(1024)(128)(4,1)S(1)}, s32[]{:S(2)}) async-start(s8[21233664]{0:T(1024)(128)(4,1)} %bitcast.221), calls=%async_computation.1 | async-start | bytes 8388608
  307.6 11.1 %slice-start.1 = ((s8[21233664]{0:T(1024)(128)(4,1)}), s8[4194304]{0:T(1024)(128)(4,1)S(1)}, s32[]{:S(2)}) async-start(s8[21233664]{0:T(1024)(128)(4,1)} %bitcast.221), calls=%async_computation.2 | async-start | bytes 8388608
  307.6 11.1 %slice-start.2 = ((s8[21233664]{0:T(1024)(128)(4,1)}), s8[4194304]{0:T(1024)(128)(4,1)S(1)}, s32[]{:S(2)}) async-start(s8[21233664]{0:T(1024)(128)(4,1)} %bitcast.221), calls=%async_computation.3 | async-start | bytes 8388608
  307.6 11.1 %slice-start.3 = ((s8[21233664]{0:T(1024)(128)(4,1)}), s8[4194304]{0:T(1024)(128)(4,1)S(1)}, s32[]{:S(2)}) async-start(s8[21233664]{0:T(1024)(128)(4,1)} %bitcast.221), calls=%async_computation.4 | async-start | bytes 8388608
  392.7 11.1 %copy-start.53 = (f32[768]{0:T(1024)}, f32[768]{0:T(1024)S(1)}, u32[]{:S(2)}) copy-start(f32[768]{0:T(1024)S(1)} %add_rsqrt_fusion) | copy-start | bytes 9220
  433.1 44.3 %collective-permute-start.4 = (bf16[1152,768]{1,0:T(8,128)(2,1)}, bf16[1152,768]{1,0:T(8,128)(2,1)}, u32[]{:S(2)}, u32[]{:S(2)}) collective-permute-start(bf16[1152,768]{1,0:T(8,128)(2,1)} %bitcast.47), channel_id=1, source_target_pairs={{0,1},{1,0},{2,3},{3,2},{4,5},{5,4},{6,7},{7,6},{8,9},{9,8},{10,11... | collective-permute-start | bytes 5308424 | tf_op jit(solution)/shard_map/ppermute | solution.py:46
  433.6 48.7 %collective-permute-start.6 = (bf16[1152,768]{1,0:T(8,128)(2,1)}, bf16[1152,768]{1,0:T(8,128)(2,1)}, u32[]{:S(2)}, u32[]{:S(2)}) collective-permute-start(bf16[1152,768]{1,0:T(8,128)(2,1)} %bitcast.50), channel_id=1, source_target_pairs={{0,1},{1,0},{2,3},{3,2},{4,5},{5,4},{6,7},{7,6},{8,9},{9,8},{10,11... | collective-permute-start | bytes 5308424 | tf_op jit(solution)/shard_map/ppermute | solution.py:46
  433.6 54.0 %collective-permute-start.8 = (bf16[768,1152]{1,0:T(8,128)(2,1)}, bf16[768,1152]{1,0:T(8,128)(2,1)}, u32[]{:S(2)}, u32[]{:S(2)}) collective-permute-start(bf16[768,1152]{1,0:T(8,128)(2,1)} %get-tuple-element.107), channel_id=1, source_target_pairs={{0,1},{1,0},{2,3},{3,2},{4,5},{5,4},{6,7},{7,6},{8,9},{9,8},{10,11... | collective-permute-start | bytes 5308424 | tf_op jit(solution)/shard_map/ppermute | solution.py:46
  434.1 53.7 %collective-permute-start.7 = (bf16[768,1152]{1,0:T(8,128)(2,1)}, bf16[768,1152]{1,0:T(8,128)(2,1)}, u32[]{:S(2)}, u32[]{:S(2)}) collective-permute-start(bf16[768,1152]{1,0:T(8,128)(2,1)} %get-tuple-element.65), channel_id=1, source_target_pairs={{0,1},{1,0},{2,3},{3,2},{4,5},{5,4},{6,7},{7,6},{8,9},{9,8},{10,11... | collective-permute-start | bytes 5308424 | tf_op jit(solution)/shard_map/ppermute | solution.py:46
  474.9 154.4 %collective-permute-start = (bf16[768,1152]{1,0:T(8,128)(2,1)}, bf16[768,1152]{1,0:T(8,128)(2,1)}, u32[]{:S(2)}, u32[]{:S(2)}) collective-permute-start(bf16[768,1152]{1,0:T(8,128)(2,1)} %get-tuple-element.62), channel_id=1, source_target_pairs={{0,1},{1,0},{2,3},{3,2},{4,5},{5,4},{6,7},{7,6},{8,9},{9,8},{10,11... | collective-permute-start | bytes 5308424 | tf_op jit(solution)/shard_map/ppermute | solution.py:46
  477.5 15.3 %collective-permute-start.9 = (bf16[768,1152]{1,0:T(8,128)(2,1)S(1)}, bf16[768,1152]{1,0:T(8,128)(2,1)S(1)}, u32[]{:S(2)}, u32[]{:S(2)}) collective-permute-start(bf16[768,1152]{1,0:T(8,128)(2,1)S(1)} %copy-done.72), channel_id=1, source_target_pairs={{0,1},{1,0},{2,3},{3,2},{4,5},{5,4},{6,7},{7,6},{8,9},{9,8},{10,11... | collective-permute-start | bytes 5308424 | tf_op jit(solution)/shard_map/ppermute | solution.py:46
  477.6 10.7 %slice-start.7 = ((s8[5308416]{0:T(1024)(128)(4,1)}), s8[4194304]{0:T(1024)(128)(4,1)S(1)}, s32[]{:S(2)}) async-start(s8[5308416]{0:T(1024)(128)(4,1)} %bitcast.247), calls=%async_computation.8 | async-start | bytes 8388608
  482.3 153.2 %collective-permute-start.1 = (bf16[768,1152]{1,0:T(8,128)(2,1)S(1)}, bf16[768,1152]{1,0:T(8,128)(2,1)}, u32[]{:S(2)}, u32[]{:S(2)}) collective-permute-start(bf16[768,1152]{1,0:T(8,128)(2,1)S(1)} %copy-done.71), channel_id=1, source_target_pairs={{0,1},{1,0},{2,3},{3,2},{4,5},{5,4},{6,7},{7,6},{8,9},{9,8},{10,11... | collective-permute-start | bytes 5308424 | tf_op jit(solution)/shard_map/ppermute | solution.py:46
  482.8 10.0 %slice-start.9 = ((s8[5308416]{0:T(1024)(128)(4,1)}), s8[4194304]{0:T(1024)(128)(4,1)S(1)}, s32[]{:S(2)}) async-start(s8[5308416]{0:T(1024)(128)(4,1)} %bitcast.249), calls=%async_computation.10 | async-start | bytes 8388608
  487.7 147.8 %collective-permute-start.2 = (bf16[768,1152]{1,0:T(8,128)(2,1)S(1)}, bf16[768,1152]{1,0:T(8,128)(2,1)}, u32[]{:S(2)}, u32[]{:S(2)}) collective-permute-start(bf16[768,1152]{1,0:T(8,128)(2,1)S(1)} %broadcast_select_fusion.2), channel_id=1, source_target_pairs={{0,1},{1,0},{2,3},{3,2},{4,5},{5,4},{6,7},{7,6},{8,9},{9,8},{10,11... | collective-permute-start | bytes 5308424 | tf_op jit(solution)/shard_map/ppermute | solution.py:46
  487.9 141.4 %collective-permute-start.3 = (bf16[768,1152]{1,0:T(8,128)(2,1)S(1)}, bf16[768,1152]{1,0:T(8,128)(2,1)}, u32[]{:S(2)}, u32[]{:S(2)}) collective-permute-start(bf16[768,1152]{1,0:T(8,128)(2,1)S(1)} %broadcast_select_fusion.1), channel_id=1, source_target_pairs={{0,1},{1,0},{2,3},{3,2},{4,5},{5,4},{6,7},{7,6},{8,9},{9,8},{10,11... | collective-permute-start | bytes 5308424 | tf_op jit(solution)/shard_map/ppermute | solution.py:46
  742.5 16.7 %copy-start.55 = (f32[2016]{0:T(1024)S(1)}, f32[2016]{0:T(1024)}, u32[]{:S(2)}) copy-start(f32[2016]{0:T(1024)} %param.41) | copy-start | bytes 24196
  742.6 16.7 %copy-start.60 = (f32[2016]{0:T(1024)S(1)}, f32[2016]{0:T(1024)}, u32[]{:S(2)}) copy-start(f32[2016]{0:T(1024)} %param.42) | copy-start | bytes 24196
  742.6 16.6 %copy-start.61 = (f32[2016]{0:T(1024)S(1)}, f32[2016]{0:T(1024)}, u32[]{:S(2)}) copy-start(f32[2016]{0:T(1024)} %param.43) | copy-start | bytes 24196
  742.6 17.4 %copy-start.38 = (bf16[768,1152]{1,0:T(8,128)(2,1)S(1)}, bf16[768,1152]{1,0:T(8,128)(2,1)}, u32[]{:S(2)}) copy-start(bf16[768,1152]{1,0:T(8,128)(2,1)} %get-tuple-element.154) | copy-start | bytes 5308420
  (75 other events, 327.2 us)
Sparse Core Ops, SparseCore 0:
  416.7 67.4 all-gather.2

commit v4 on v3

--- a/solution.py
+++ b/solution.py
@@ -97,17 +97,26 @@
         return 0
     lax.fori_loop(0,out.shape[0],one,0)
 
+def home_rows(starts, i, flat, n):
+    row = lax.broadcasted_iota(jnp.int32, (SPAN, 1), 0) + i * SPAN
+    home = row
+    for s in range(1, n):
+        home = home + jnp.where(row >= starts[s], SPAN - (starts[s] - starts[s - 1]), 0)
+    pick = jnp.where(lax.broadcasted_iota(jnp.int32, (SPAN, n * SPAN), 1) == home, 1.0, 0.0)
+    return dot(pick.astype(bf16), flat)
+
+
 def unspread(starts, slabs, out):
-    n=slabs.shape[0]; rows=out.shape[0]
-    def one(i,_):
-        row=lax.broadcasted_iota(jnp.int32,(SPAN,1),0)+i*SPAN
-        home=row
-        for s in range(1,n):
-            home=home+jnp.where(row>=starts[s],SPAN-(starts[s]-starts[s-1]),0)
-        pick=(lax.broadcasted_iota(jnp.int32,(SPAN,n*SPAN),1)==home).astype(bf16)
-        out[pl.ds(pl.multiple_of(i*SPAN,SPAN),SPAN),:]=dot(pick,slabs[...].reshape(n*SPAN,slabs.shape[2])).astype(bf16)
-        return 0
-    lax.fori_loop(0,rows//SPAN,one,0)
+    n, _, width = slabs.shape
+
+    def one(i, carry):
+        place = pl.ds(pl.multiple_of(i * SPAN, SPAN), SPAN)
+        flat = slabs[...].reshape(n * SPAN, width)
+        out[place, :] = home_rows(starts, i, flat, n).astype(bf16)
+        return carry
+
+    lax.fori_loop(0, out.shape[0] // SPAN, one, 0)
+
 
 def attend_slab(starts, s, qs, ks, vs, os, heads):
     length = starts[s + 1] - starts[s]
@@ -131,27 +140,53 @@
     lax.fori_loop(0, qs.shape[0], seg, 0)
     unspread(starts, os, out)
 
+def back_slab(starts, s, qs, ks, vs, ups, dqs, dks, dvs, heads):
+    scale = HEAD_DIM**-0.5
+    length = starts[s + 1] - starts[s]
+    outside = jnp.where(lax.broadcasted_iota(jnp.int32, (SPAN, 1), 0) < length, 0.0, -1e30)
+    for h in heads:
+        cols = slice(h * HEAD_DIM, (h + 1) * HEAD_DIM)
+        query, key, value, upstream = (part[s, :, cols] for part in (qs, ks, vs, ups))
+        score = back_dot(key, query) + outside
+        power = jnp.exp2((score - jnp.max(score, axis=0, keepdims=True)) * EXP_SCALE)
+        soft = power * (1.0 / jnp.sum(power, axis=0, keepdims=True))
+        back_soft = back_dot(value, upstream)
+        mean = jnp.sum(back_soft * soft, axis=0, keepdims=True)
+        back_score = (soft * (back_soft - mean)).astype(bf16)
+        dvs[s, :, cols] = dot(soft.astype(bf16), upstream).astype(bf16)
+        dks[s, :, cols] = (dot(back_score, query) * scale).astype(bf16)
+        dqs[s, :, cols] = (outer(back_score, key) * scale).astype(bf16)
+
+
+class Slab:
+    def __init__(self, ref, slot, rows):
+        self.ref, self.slot, self.rows = ref, slot, rows
+
+    def __getitem__(self, index):
+        return self.ref[self.slot, self.rows, index[2]]
+
+    def __setitem__(self, index, value):
+        self.ref[self.slot, self.rows, index[2]] = value
+
+
+def back_slab_flat(starts, s, rows, qs, ks, vs, space, heads):
+    dqs, dks, dvs, ups = (Slab(space, slot, rows) for slot in range(4))
+    back_slab(starts, s, qs, ks, vs, ups, dqs, dks, dvs, heads)
+
+
 def back_kernel(starts, qs, ks, vs, up, dq, dk, dv, ups, dqs, dks, dvs):
-    spread(starts,up,ups)
-    n=qs.shape[0]; scale=HEAD_DIM**-0.5
-    def seg(s,_):
-        length=starts[s+1]-starts[s]
-        outside=jnp.where(lax.broadcasted_iota(jnp.int32,(SPAN,1),0)<length,0.0,-1e30)
-        for h in range(qs.shape[2]//HEAD_DIM):
-            cols=slice(h*HEAD_DIM,(h+1)*HEAD_DIM)
-            query,key,value,upstream=qs[s,:,cols],ks[s,:,cols],vs[s,:,cols],ups[s,:,cols]
-            score=back_dot(key,query)+outside
-            power=jnp.exp2((score-jnp.max(score,axis=0,keepdims=True))*EXP_SCALE)
-            soft=power*(1.0/jnp.sum(power,axis=0,keepdims=True))
-            back_soft=back_dot(value,upstream)
-            mean=jnp.sum(back_soft*soft,axis=0,keepdims=True)
-            back_score=(soft*(back_soft-mean)).astype(bf16)
-            dvs[s,:,cols]=dot(soft.astype(bf16),upstream).astype(bf16)
-            dks[s,:,cols]=(dot(back_score,query)*scale).astype(bf16)
-            dqs[s,:,cols]=(outer(back_score,key)*scale).astype(bf16)
-        return 0
-    lax.fori_loop(0,n,seg,0)
-    for slabs,out in ((dqs,dq),(dks,dk),(dvs,dv)): unspread(starts,slabs,out)
+    spread(starts, up, ups)
+
+    def seg(s, carry):
+        back_slab(
+            starts, s, qs, ks, vs, ups, dqs, dks, dvs, range(qs.shape[2] // HEAD_DIM)
+        )
+        return carry
+
+    lax.fori_loop(0, qs.shape[0], seg, 0)
+    for slabs, out in ((dqs, dq), (dks, dk), (dvs, dv)):
+        unspread(starts, slabs, out)
+
 
 VM = pl.BlockSpec(memory_space=pltpu.VMEM)
 SM = pl.BlockSpec(memory_space=pltpu.SMEM)
@@ -215,19 +250,19 @@
 
 
 def forward_kernel(
-    own, cond, bias, w_mod, starts, seg_ids, tokens, *refs
+    att_low, proj_low, exp_low, con_low, cond, bias, w_mod, starts, seg_ids, tokens, *refs
 ):
-    w_out, rest = refs[:8], refs[8:]
-    w_con_out, modulation, h1_out, slab_out, att_out, proj_out, mid_out, h2_out = rest[:8]
-    before_out, act_out, ff_out, y_out = rest[8:12]
-    w, w_con, conds, bias_in, bias_all, parts, x_parts, z_parts = rest[12:20]
-    slabs, padded, wide, hidden = rest[20:24]
-    small_s, small_r, part_s, part_r = rest[24:28]
-    z_s, z_r, x_s, x_r, y_s, y_r, c_s, c_r, load_sem, out_sem, save_sem = rest[28:]
+    w_out, con_out, slab_out, before_out = refs[:8], refs[8:12], refs[12:15], refs[15:19]
+    modulation, pair_out, proj_out, mid_out, h2_out, act_out, ff_out, y_out = refs[19:27]
+    rest = refs[27:]
+    w, w_con, conds, bias_in, bias_all, parts, x_parts, z_parts = rest[:8]
+    slabs, padded, wide, hidden, turned = rest[8:13]
+    small_s, small_r, part_s, part_r = rest[13:17]
+    z_s, z_r, x_s, x_r, y_s, y_r, c_s, c_r, load_sem, out_sem, save_sem = rest[17:]
     row, seg = lax.axis_index("rows"), lax.axis_index("seg")
     x, z = row % 2, row // 2
     y, c = seg // 2, seg % 2
-    n, width = own.shape[1:]
+    n, width = proj_low.shape
     count = tokens.shape[0]
     units = ((0, 2), (1, 3), (4, 5), (6, 7), (8, 9), (10, 11))
     piece = n // 3
@@ -243,14 +278,33 @@
             return w.at[block_of(u), r, rows]
         return w_con.at[r, block_of(u) - 8, rows]
 
+    def columns(number):
+        return pl.ds(pl.multiple_of(number * width, width), width)
+
+    mine = pl.ds(part, 2 * piece)
+    own = (
+        att_low.at[mine, columns(2 * c)],
+        None,
+        exp_low.at[mine, columns(c)],
+        exp_low.at[mine, columns(2 + c)],
+        con_low.at[pl.ds(pl.multiple_of(c * n + part, 16), 2 * piece)],
+        con_low.at[pl.ds(pl.multiple_of((2 + c) * n + part, 16), 2 * piece)],
+    )
     loads = []
     for u in range(6):
-        copy = pltpu.make_async_copy(
-            own.at[block_of(u), pl.ds(part, 2 * piece)],
-            slot(u, row, pl.ds(part, 2 * piece)),
-            load_sem.at[u],
-        )
-        copy.start()
+        dst = slot(u, row, mine)
+        if u != 1:
+            copy = pltpu.make_async_copy(own[u], dst, load_sem.at[u])
+            copy.start()
+        else:
+            two = (att_low.at[mine, columns(1)], proj_low.at[mine])
+            for core in range(2):
+
+                @pl.when(c == core)
+                def _():
+                    pltpu.make_async_copy(two[core], dst, load_sem.at[u]).start()
+
+            copy = pltpu.make_async_copy(two[1], dst, load_sem.at[u])
         loads.append(copy)
     z_peers = [(lax.rem(z + k, 4) * 2 + x, seg) for k in (1, 2, 3)]
     x_peer, y_peer, c_peer = (row + 1 - 2 * x, seg), (row, seg + 2 - 4 * y), (row, seg + 1 - 2 * c)
@@ -381,7 +435,8 @@
                     for b in units[u]:
                         outs.append(save(w.at[b], w_out[b], out_sem.at[b]))
                 elif u == 5:
-                    outs.append(save(w_con, w_con_out, out_sem.at[8]))
+                    for q in range(4):
+                        outs.append(save(w_con.at[pl.ds(2 * q, 2)], con_out[q], out_sem.at[8 + q]))
 
 
     def of_segment(rows, number):
@@ -403,6 +458,18 @@
     def matrix(b):
         return w[b].reshape(8 * n, width)
 
+    def turn(source, out, sem):
+        if ("turned", None) in kept:
+            finish("turned")
+
+        def body(i, carry):
+            rows = pl.ds(pl.multiple_of(i * SPAN, SPAN), SPAN)
+            turned[:, rows] = source[rows, :].T
+            return carry
+
+        lax.fori_loop(0, count // SPAN, body, 0)
+        keep("turned", None, turned, out, sem)
+
     def norm_one():
         def body(rows):
             normed = layer_rows(tokens[rows, :].astype(f32))
@@ -411,7 +478,7 @@
             ).astype(bf16)
 
         tiles(128, body)
-        keep("h1", None, padded, h1_out, 0)
+        turn(padded, pair_out.at[0], 0)
 
     def spread_hidden():
         def one(s, carry):
@@ -429,7 +496,7 @@
             return carry
 
         lax.fori_loop(0, 4, one, 0)
-        keep("slab", which, slabs.at[which], slab_out.at[which], 1 + which)
+        keep("slab", which, slabs.at[which], slab_out[which], 1 + which)
 
     def attend_heads(first, last):
         def one(s, carry):
@@ -441,9 +508,8 @@
         lax.fori_loop(0, 4, one, 0)
 
     def gather_back():
-        finish("h1")
         unspread(starts, slabs.at[3], padded)
-        keep("attended", None, padded, att_out, 4)
+        turn(padded, pair_out.at[1], 4)
 
     def add_projected():
         def body(rows):
@@ -464,10 +530,11 @@
             ).astype(bf16)
 
         tiles(128, body)
-        keep("h2", None, hidden, h2_out, 7)
+        turn(hidden, h2_out, 7)
 
     def expand_block(j):
         finish("wide")
+        finish("turned")
         if j < 3:
             finish("slab", j)
 
@@ -475,16 +542,17 @@
             rows = pl.ds(pl.multiple_of(i * SPAN, SPAN), SPAN)
             before = dot(hidden[rows, :], matrix(4 + j)) + bias_row(3 + j)
             wide[1, rows, :] = before
-            slabs[j, i] = gelu(before).astype(bf16)
+            low = gelu(before).astype(bf16)
+            slabs[j, i] = low
+            turned[:, rows] = low.T
             return carry
 
         lax.fori_loop(0, count // SPAN, body, 0)
-        keep("wide", None, wide.at[1], before_out.at[j], 8 + j)
-        keep("act", j, slabs.at[j, pl.ds(0, 3)], act_out.at[:, :, pl.ds(j * width, width)], 12 + j)
+        keep("wide", None, wide.at[1], before_out[j], 8 + j)
+        keep("turned", None, turned, act_out.at[j], 12 + j)
 
     def contract():
         finish("wide")
-        finish("attended")
 
         def body(i, carry):
             rows = pl.ds(pl.multiple_of(i * SPAN, SPAN), SPAN)
@@ -523,10 +591,7 @@
     width = projection.shape[1]
     n = attention.shape[0]
     count = tokens.shape[0]
-    blocks = [attention[:, j * width : (j + 1) * width] for j in range(3)] + [projection]
-    blocks += [expand[:, j * width : (j + 1) * width] for j in range(4)]
-    blocks += [contract[j * n : (j + 1) * n] for j in range(4)]
-    own = jnp.stack([block.astype(bf16) for block in blocks])
+    low = [part.astype(bf16) for part in own_parts]
     n_seg = cond_silu.shape[0]
     cond = cond_silu.astype(f32).reshape(n_seg, 8, n).transpose(1, 0, 2)
     cond = jnp.pad(jnp.concatenate([cond, cond], axis=1), ((0, 0), (0, 0), (0, 256 - n)))
@@ -543,22 +608,21 @@
     outs = pl.pallas_call(
         forward_kernel,
         out_shape=(shape(bf16, 8, n, width),) * 8
+        + (shape(bf16, 2, 4, n, width),) * 4
+        + (shape(bf16, 4, SPAN, width),) * 3
+        + (shape(f32, count, width),) * 4
         + (
-            shape(bf16, 8, 4, n, width),
             shape(f32, 8, 3 * width),
-            shape(bf16, count, width),
-            shape(bf16, 3, 4, SPAN, width),
-            shape(bf16, count, width),
+            shape(bf16, 2, width, count),
             shape(f32, count, width),
             shape(f32, count, width),
-            shape(bf16, count, width),
-            shape(f32, 4, count, width),
-            shape(bf16, count // SPAN, SPAN, 4 * width),
+            shape(bf16, width, count),
+            shape(bf16, 4, width, count),
             shape(f32, count, width),
             shape(bf16, count, width),
         ),
-        in_specs=[ANY, VM, VM, VM, SM, VM, VM],
-        out_specs=(ANY,) * 9 + (VM,) + (ANY,) * 10,
+        in_specs=[ANY] * 4 + [VM, VM, VM, SM, VM, VM],
+        out_specs=(ANY,) * 19 + (VM,) + (ANY,) * 7,
         scratch_shapes=[
             pltpu.VMEM((8, 8, n, width), bf16),
             pltpu.VMEM((8, 4, n, width), bf16),
@@ -572,6 +636,7 @@
             pltpu.VMEM((count, width), bf16),
             pltpu.VMEM((2, count, width), f32),
             pltpu.VMEM((count, width), bf16),
+            pltpu.VMEM((width, count), bf16),
             sems((14,)),
             sems((14,)),
             sems((4,)),
@@ -579,28 +644,23 @@
         ]
         + [sems((6, 3))] * 2
         + [sems((6, 4))] * 6
-        + [sems((6,)), sems((9,)), sems((18,))],
+        + [sems((6,)), sems((12,)), sems((18,))],
         compiler_params=pltpu.CompilerParams(
             collective_id=0, has_side_effects=True, vmem_limit_bytes=60 << 20
         ),
         name="forward",
-    )(own, cond, bias, mod_low, starts, segments[:, None], tokens)
+    )(*low, cond, bias, mod_low, starts, segments[:, None], tokens)
     w = [block.reshape(8 * n, width) for block in outs[:8]]
-    modulation = jnp.concatenate([outs[9][:n_seg], outs[9][n_seg:]], axis=1)
-    weights = (tuple(w[:3]), w[3], tuple(w[4:]), outs[8].reshape(32 * n, width))
-    h1, slabs, attended, projected, middle, h2, before, act, feedforward, output = outs[10:]
-    saved = (
-        modulation,
-        h1,
-        (slabs[0], slabs[1], slabs[2]),
-        attended,
-        projected,
-        middle,
-        h2,
-        [before[j] for j in range(4)],
-        act.reshape(count, 4 * width),
-        feedforward,
-    )
+    con = [block.reshape(8 * n, width) for block in outs[8:12]]
+    modulation = jnp.concatenate([outs[19][:n_seg], outs[19][n_seg:]], axis=1)
+    weights = (tuple(w[:3]), w[3], tuple(w[4:]), con)
+    pair, projected, middle, h2, act, feedforward, output = outs[20:]
+    lefts = (
+        pair.reshape(2, 8, n, count),
+        h2.reshape(8, n, count),
+        act.reshape(8, 4, n, count),
+    )
+    saved = (modulation, outs[12:15], projected, middle, outs[15:19], feedforward, lefts)
     return output, saved, weights
 
 
@@ -642,225 +702,385 @@
     activated = jnp.concatenate([gelu(part).astype(bf16) for part in before], axis=1)
     feedforward = dot(activated, w_con) + bias[7]
     output = (middle + gate_two * feedforward).astype(bf16)
-    saved = (
-        modulation,
-        hidden_one,
-        slabs,
-        attended,
-        projected,
-        middle,
-        hidden_two,
-        before,
-        activated,
-        feedforward,
-    )
+    w_con = [w_con[j * width : (j + 1) * width] for j in range(4)]
+    lefts = (hidden_one, attended, hidden_two, activated)
+    saved = (modulation, slabs, projected, middle, before, feedforward, lefts)
     return output, saved, (w_att, w_proj, w_exp, w_con)
 
 
-def reduce_kernel(
-    blocks, out, d, y_in, x_in, z_in, total, y2_in, grad, load, y_s, y_r, x_s, x_r, z_s, z_r, y2_s, y2_r, c_s, c_r, store
-):
-    row, seg = lax.axis_index("rows"), lax.axis_index("seg")
-    x, z = row % 2, row // 2
-    y, c = seg // 2, seg % 2
-    units, _, n, width = blocks.shape
-    piece = n // 3
-    part = pl.multiple_of(y * piece, piece)
-    mine = pl.multiple_of(y * 2 * piece, piece)
-    theirs = pl.multiple_of((1 - y) * 2 * piece, piece)
-    level = [lax.rem(z + k, 4) for k in range(4)]
-    z_peers = [(level[k] * 2 + x, seg) for k in range(4)]
-    x_peer, y_peer, c_peer = (row + 1 - 2 * x, seg), (row, seg + 2 - 4 * y), (row, seg + 1 - 2 * c)
-    loads = []
-    for u in range(units):
-        copy = pltpu.make_async_copy(blocks.at[u], d.at[u], load.at[u])
+class Reduce:
+    def __init__(self, out, refs, units):
+        self.out = out
+        self.d, self.y_in, self.x_in, self.z_in, self.total, self.y2_in, self.grad = refs[:7]
+        self.y_s, self.y_r, self.x_s, self.x_r, self.z_s, self.z_r = refs[7:13]
+        self.y2_s, self.y2_r, self.c_s, self.c_r, self.store = refs[13:]
+        row, seg = lax.axis_index("rows"), lax.axis_index("seg")
+        self.row, self.x, self.z = row, row % 2, row // 2
+        self.y, self.c = seg // 2, seg % 2
+        self.units = units
+        self.slots, _, n, self.width = self.d.shape
+        self.piece = piece = n // 3
+        self.part = pl.multiple_of(self.y * piece, piece)
+        self.mine = pl.multiple_of(self.y * 2 * piece, piece)
+        self.theirs = pl.multiple_of((1 - self.y) * 2 * piece, piece)
+        self.level = [lax.rem(self.z + k, 4) for k in range(4)]
+        self.z_peers = [(self.level[k] * 2 + self.x, seg) for k in range(4)]
+        self.x_peer = (row + 1 - 2 * self.x, seg)
+        self.y_peer = (row, seg + 2 - 4 * self.y)
+        self.c_peer = (row, seg + 1 - 2 * self.c)
+        self.sent, self.outs = {u: [] for u in range(units)}, []
+        self.steps = [(u, k) for u in range(self.units) for k in (1, 3, 2, 0)]
+        self.count = len(self.steps) + 8
+
+    def greet(self):
+        greet(self.z_peers[1:] + [self.x_peer, self.y_peer, self.c_peer])
+
+    def go(self, u, copy):
         copy.start()
-        loads.append(copy)
-    greet(z_peers[1:] + [x_peer, y_peer, c_peer])
-    sent = []
-
-    def add(*terms):
+        self.sent[u].append(copy)
+
+    def drain(self, u):
+        for copy in self.sent.pop(u, ()):
+            copy.wait_send()
+
+    def add(self, *terms):
         result = terms[0].astype(f32)
         for term in terms[1:]:
             result = result + term.astype(f32)
         return result.astype(bf16)
 
-    def to_y(u, k):
-        src = d.at[u, pl.ds(level[k] * 2, 2), pl.ds(theirs, piece)]
-        return remote(src, y_in.at[u, k], y_s.at[u, k], y_r.at[u, k], y_peer)
-
-    def to_x(u, k):
-        src = d.at[u, level[k] * 2 + 1 - x, pl.ds(part, 2 * piece)]
-        return remote(src, x_in.at[u, k], x_s.at[u, k], x_r.at[u, k], x_peer)
-
-    def to_z(u, k):
-        src = d.at[u, level[k] * 2 + x, pl.ds(part, 2 * piece)]
-        return remote(src, z_in.at[u, k - 1], z_s.at[u, k - 1], z_r.at[u, k - 1], z_peers[k])
-
-    def to_y_again(u):
-        return remote(total.at[u], y2_in.at[u], y2_s.at[u], y2_r.at[u], y_peer)
-
-    def to_core(u):
-        ref = grad.at[u, c]
-        return remote(ref, ref, c_s.at[u], c_r.at[u], c_peer)
-
-    def go(copy):
+
+    def to_y(self, u, k):
+        i = u % self.slots
+        src = self.d.at[i, pl.ds(self.level[k] * 2, 2), pl.ds(self.theirs, self.piece)]
+        return remote(src, self.y_in.at[i, k], self.y_s.at[u, k], self.y_r.at[u, k], self.y_peer)
+
+    def to_x(self, u, k):
+        i = u % self.slots
+        src = self.d.at[i, self.level[k] * 2 + 1 - self.x, pl.ds(self.part, 2 * self.piece)]
+        return remote(src, self.x_in.at[i, k], self.x_s.at[u, k], self.x_r.at[u, k], self.x_peer)
+
+    def to_z(self, u, k):
+        i = u % self.slots
+        src = self.d.at[i, self.level[k] * 2 + self.x, pl.ds(self.part, 2 * self.piece)]
+        return remote(
+            src, self.z_in.at[i, k - 1], self.z_s.at[u, k - 1], self.z_r.at[u, k - 1], self.z_peers[k]
+        )
+
+    def to_y_again(self, u):
+        i = u % self.slots
+        return remote(
+            self.total.at[i], self.y2_in.at[i], self.y2_s.at[u], self.y2_r.at[u], self.y_peer
+        )
+
+    def to_core(self, u):
+        ref = self.grad.at[u, self.c]
+        return remote(ref, ref, self.c_s.at[u], self.c_r.at[u], self.c_peer)
+
+    def begin(self, u):
+        for k in (1, 3, 2, 0):
+            self.go(u, self.to_y(u, k))
+
+    def step(self, j):
+        d, piece = self.d, self.piece
+        mine, part = pl.ds(self.mine, piece), pl.ds(self.part, 2 * piece)
+        if j < len(self.steps):
+            u, k = self.steps[j]
+            i = u % self.slots
+            self.to_y(u, k).wait_recv()
+            for side in range(2):
+                r = self.level[k] * 2 + side
+                d[i, r, mine] = self.add(d[i, r, mine], self.y_in[i, k, side])
+            self.go(u, self.to_x(u, k))
+        if 0 <= j - 1 < len(self.steps):
+            u, k = self.steps[j - 1]
+            i = u % self.slots
+            self.to_x(u, k).wait_recv()
+            r = self.level[k] * 2 + self.x
+            d[i, r, part] = self.add(d[i, r, part], self.x_in[i, k])
+            if k:
+                self.go(u, self.to_z(u, k))
+        if j >= 5 and (j - 5) % 4 == 0 and (j - 5) // 4 < self.units:
+            u = (j - 5) // 4
+            i = u % self.slots
+            for k in (1, 3, 2):
+                self.to_z(u, k).wait_recv()
+            z_in = self.z_in
+            self.total[i] = self.add(d[i, self.row, part], z_in[i, 0], z_in[i, 1], z_in[i, 2])
+            self.go(u, self.to_y_again(u))
+        if j >= 6 and (j - 6) % 4 == 0 and (j - 6) // 4 < self.units:
+            u = (j - 6) // 4
+            i = u % self.slots
+            self.to_y_again(u).wait_recv()
+            total, y2_in, grad, c = self.total, self.y2_in, self.grad, self.c
+            here = pl.ds(pl.multiple_of(self.y * piece, piece), piece)
+            there = pl.ds(pl.multiple_of((1 - self.y) * piece, piece), piece)
+            grad[u, c, mine] = total[i, here]
+            grad[u, c, pl.ds(self.theirs, piece)] = y2_in[i, there]
+            grad[u, c, pl.ds(piece, piece)] = self.add(total[i, there], y2_in[i, here])
+            self.go(u, self.to_core(u))
+        if j >= 7 and (j - 7) % 4 == 0 and (j - 7) // 4 < self.units:
+            u = (j - 7) // 4
+            self.to_core(u).wait_recv()
+            copy = pltpu.make_async_copy(self.grad.at[u], self.out.at[u], self.store.at[u])
+            copy.start()
+            self.outs.append(copy)
+
+    def finish(self):
+        for u in range(self.units):
+            self.drain(u)
+        for copy in self.outs:
+            copy.wait()
+
+    @staticmethod
+    def scratch(units, slots, n, width):
+        sems = pltpu.SemaphoreType.DMA
+
+        def space(*shape):
+            return pltpu.VMEM(shape + (width,), bf16)
+
+        return (
+            [
+                space(slots, 8, n),
+                space(slots, 4, 2, n // 3),
+                space(slots, 4, 2 * n // 3),
+                space(slots, 3, 2 * n // 3),
+                space(slots, 2 * n // 3),
+                space(slots, 2 * n // 3),
+                space(units, 2, n),
+            ]
+            + [sems((units, 4))] * 4
+            + [sems((units, 3))] * 2
+            + [sems((units,))] * 5
+        )
+
+
+def multiply_pair(out, lefts, rights):
+    n, width = out.shape[1:]
+
+    def one(i, carry):
+        rows = pl.ds(2 * i, 2)
+        total = 0.0
+        for left, right in zip(lefts, rights):
+            total = total + dot(left[rows].reshape(2 * n, left.shape[2]), right[...])
+        out[rows] = total.astype(bf16).reshape(2, n, width)
+        return carry
+
+    lax.fori_loop(0, 4, one, 0)
+
+
+def reduce_kernel(
+    act, feed, hidden, b0, b1, b2, b3, pair, project, starts, qs, ks, vs, up, out, qv, dk, left, right,
+    near, far_s, far_r, save_sem, free, *refs
+):
+    red = Reduce(out, refs, 6)
+    c, count = red.c, up.shape[0]
+    rows = pl.ds(0, count)
+
+    def near_copy(index, src, dst):
+        return pltpu.make_async_copy(src, dst, near.at[index])
+
+    def far_copy(index, src, dst):
+        return remote(src, dst, far_s.at[index], far_r.at[index], red.c_peer)
+
+    def lefts(i):
+        return left.at[2 * i], left.at[2 * i + 1]
+
+    def rights(i):
+        return right.at[2 * i, rows], right.at[2 * i + 1, rows]
+
+    fixed = [
+        (act.at[:, c], act.at[:, 1 - c], lefts(0)),
+        (feed, feed, rights(0)),
+        (act.at[:, 2 + c], act.at[:, 3 - c], lefts(1)),
+        (hidden, hidden, lefts(2)),
+    ]
+    pulls = [
+        ((near_copy(i, here, dst[0]),) * 2, (far_copy(i, there, dst[1]),) * 2)
+        for i, (here, there, dst) in enumerate(fixed)
+    ]
+    for i, two in ((4, (b0, b1)), (5, (b2, b3))):
+        dst = rights(i - 3)
+        pulls.append(
+            (
+                tuple(near_copy(i, two[core], dst[0]) for core in range(2)),
+                tuple(far_copy(i, two[1 - core], dst[1]) for core in range(2)),
+            )
+        )
+    late_far = right.at[0, rows], right.at[1, rows]
+    pulls.append(((near_copy(6, pair.at[c], left.at[0]),) * 2, (far_copy(6, pair.at[1 - c], left.at[1]),) * 2))
+    pulls.append(((near_copy(7, pair.at[0], left.at[2]),) * 2, (far_copy(7, pair.at[0], left.at[3]),) * 2))
+    pulls.append(
+        (
+            (None, near_copy(8, project, right.at[2, rows])),
+            (far_copy(8, project, late_far[0]), far_copy(8, right.at[3, rows], late_far[0])),
+        )
+    )
+    pulls.append(
+        ((None, None), (far_copy(9, right.at[5 - c, rows], late_far[1]),) * 2)
+    )
+
+    def start(index, side):
+        two = pulls[index][side]
+        if two[0] is two[1]:
+            if two[0] is not None:
+                two[0].start()
+            return
+        for core in range(2):
+            if two[core] is not None:
+
+                @pl.when(c == core)
+                def _():
+                    two[core].start()
+
+    def arrive(index):
+        two, far = pulls[index]
+        if two[0] is None and two[1] is not None:
+
+            @pl.when(c == 1)
+            def _():
+                two[1].wait()
+        elif two[0] is not None:
+            two[0].wait()
+        far[0].wait()
+
+    def block(u):
+        for index in ((0, 1), (2,), (3, 4), (5,))[u]:
+            arrive(index)
+        for index in ((2, 3, 4), (5,), (), ())[u]:
+            start(index, 1)
+        multiply_pair(red.d.at[u], lefts(min(u, 2)), rights(max(u - 1, 0)))
+        red.begin(u)
+
+    def late_pulls():
+        pl.semaphore_signal(
+            free, inc=1, device_id=red.c_peer, device_id_type=pl.DeviceIdType.MESH
+        )
+        for index in (6, 7, 8):
+            start(index, 0)
+        pl.semaphore_wait(free, 1)
+        for index in (6, 8, 7, 9):
+            start(index, 1)
+
+    def late_block(u):
+        for index in ((6, 8), (7, 9))[u - 4]:
+            arrive(index)
+        red.drain(u - 4)
+        own = right.at[3 - c, rows] if u == 4 else right.at[4 + c, rows]
+        multiply_pair(red.d.at[u - 4], lefts(u - 4), (own, late_far[u - 4]))
+        red.begin(u)
+
+    def spread_up():
+        def one(s, carry):
+            place = pl.ds(pl.multiple_of(s * SPAN, SPAN), SPAN)
+            right[3, place, :] = spread_rows(starts, up, s).astype(bf16)
+            return carry
+
+        lax.fori_loop(0, 4, one, 0)
+
+    def heads(first, last):
+        def one(s, carry):
+            place = pl.ds(pl.multiple_of(s * SPAN, SPAN), SPAN)
+            back_slab_flat(starts, s, place, qs, ks, vs, right, range(first, last))
+            return carry
+
+        lax.fori_loop(0, 4, one, 0)
+
+    kept = []
+
+    def collect(which, slot, dst):
+        def one(i, carry):
+            place = pl.ds(pl.multiple_of(i * SPAN, SPAN), SPAN)
+            right[slot, place, :] = home_rows(starts, i, right[which], 4).astype(bf16)
+            return carry
+
+        lax.fori_loop(0, count // SPAN, one, 0)
+        copy = pltpu.make_async_copy(right.at[slot, rows], dst, save_sem.at[which])
         copy.start()
-        sent.append(copy)
-
-    steps = [(u, k) for u in range(units) for k in (1, 3, 2, 0)]
-    ahead = 5
-    outs = []
-
-    def first(j):
-        u, k = steps[j]
-        if k == 1:
-            loads[u].wait()
-        go(to_y(u, k))
-
-    for j in range(ahead):
-        first(j)
-    for j in range(len(steps) + 8):
-        if j + ahead < len(steps):
-            first(j + ahead)
-        if j < len(steps):
-            u, k = steps[j]
-            to_y(u, k).wait_recv()
-            for side in range(2):
-                r = level[k] * 2 + side
-                d[u, r, pl.ds(mine, piece)] = add(d[u, r, pl.ds(mine, piece)], y_in[u, k, side])
-            go(to_x(u, k))
-        if 0 <= j - 1 < len(steps):
-            u, k = steps[j - 1]
-            to_x(u, k).wait_recv()
-            r = level[k] * 2 + x
-            d[u, r, pl.ds(part, 2 * piece)] = add(d[u, r, pl.ds(part, 2 * piece)], x_in[u, k])
-            if k:
-                go(to_z(u, k))
-        if j >= 3 and (j - 3) % 4 == 2 and (j - 3) // 4 < units:
-            u = (j - 3) // 4
-            for k in (1, 3, 2):
-                to_z(u, k).wait_recv()
-            total[u] = add(d[u, row, pl.ds(part, 2 * piece)], z_in[u, 0], z_in[u, 1], z_in[u, 2])
-            go(to_y_again(u))
-        if j >= 4 and (j - 4) % 4 == 2 and (j - 4) // 4 < units:
-            u = (j - 4) // 4
-            to_y_again(u).wait_recv()
-            here, there = y * piece, (1 - y) * piece
-            here, there = pl.multiple_of(here, piece), pl.multiple_of(there, piece)
-            grad[u, c, pl.ds(mine, piece)] = total[u, pl.ds(here, piece)]
-            grad[u, c, pl.ds(theirs, piece)] = y2_in[u, pl.ds(there, piece)]
-            grad[u, c, pl.ds(piece, piece)] = add(
-                total[u, pl.ds(there, piece)], y2_in[u, pl.ds(here, piece)]
-            )
-            go(to_core(u))
-        if j >= 5 and (j - 5) % 4 == 2 and (j - 5) // 4 < units:
-            u = (j - 5) // 4
-            to_core(u).wait_recv()
-            copy = pltpu.make_async_copy(grad.at[u], out.at[u], store.at[u])
-            copy.start()
-            outs.append(copy)
-    for copy in sent:
-        copy.wait_send()
-    for copy in outs:
+        kept.append(copy)
+
+    for index in (0, 1, 2, 3, 4, 5):
+        start(index, 0)
+    red.greet()
+    for index in (0, 1):
+        start(index, 1)
+    plan = [partial(block, 0), partial(block, 1), 0, partial(block, 2), 1, partial(block, 3), 2]
+    plan += [spread_up, 3]
+    for first in range(0, 16, 2):
+        plan += [partial(heads, first, first + 2), 4 + first // 2]
+    plan += [partial(collect, 0, 4, qv.at[0]), partial(collect, 2, 5, qv.at[1]), 12]
+    plan += [partial(collect, 1, 3, dk), late_pulls, 13, 14, partial(late_block, 4), 15]
+    plan += [partial(late_block, 5)] + list(range(16, red.count))
+    for item in plan:
+        if isinstance(item, int):
+            red.step(item)
+        else:
+            item()
+    red.finish()
+    for copy in kept:
         copy.wait()
 
 
-def reduce_units(blocks, number):
-    units = len(blocks)
-    rows, width = blocks[0].shape
-    n = rows // 8
+def reduce_all(lefts, feed, befores, project, starts, slabs, up):
+    pair, hidden, act = lefts
+    n = act.shape[2]
+    count, width = feed.shape
     sems = pltpu.SemaphoreType.DMA
-
-    def space(*shape):
-        return pltpu.VMEM(shape + (width,), bf16)
-
     return pl.pallas_call(
         reduce_kernel,
-        out_shape=jax.ShapeDtypeStruct((units, 2, n, width), bf16),
-        in_specs=[ANY],
-        out_specs=ANY,
+        out_shape=(
+            jax.ShapeDtypeStruct((6, 2, n, width), bf16),
+            jax.ShapeDtypeStruct((2, count, width), bf16),
+            jax.ShapeDtypeStruct((count, width), bf16),
+        ),
+        in_specs=[ANY] * 9 + [SM] + [VM] * 4,
+        out_specs=(ANY,) * 3,
         scratch_shapes=[
-            space(units, 8, n),
-            space(units, 4, 2, n // 3),
-            space(units, 4, 2 * n // 3),
-            space(units, 3, 2 * n // 3),
-            space(units, 2 * n // 3),
-            space(units, 2 * n // 3),
-            space(units, 2, n),
-            sems((units,)),
+            pltpu.VMEM((6, 8, n, count), bf16),
+            pltpu.VMEM((6, 4 * SPAN, width), bf16),
+            sems((9,)),
+            sems((10,)),
+            sems((10,)),
+            sems((3,)),
+            pltpu.SemaphoreType.REGULAR,
         ]
-        + [sems((units, 4))] * 4
-        + [sems((units, 3))] * 2
-        + [sems((units,))] * 5,
+        + Reduce.scratch(6, 4, n, width),
         compiler_params=pltpu.CompilerParams(
-            collective_id=number, has_side_effects=True, vmem_limit_bytes=48 << 20
+            collective_id=1, has_side_effects=True, vmem_limit_bytes=60 << 20
         ),
-        name=f"reduce_{number}",
-    )(jnp.stack(blocks).reshape(units, 8, n, width))
-
-
-def reduce_fast(early, hidden_one, attended, hidden_two, activated, back_feed, back_before):
-    x, y, z, c = place()
-    width = hidden_one.shape[1]
-
-    def pick(first, second, which):
-        return jnp.where(which == 0, first, second)
-
-    act = activated.T.reshape(8, 4, width // 8, activated.shape[0])
-    feed_far = over_core(back_feed)
-    blocks = []
-    for unit in range(2):
-        mine, there = (
-            lax.dynamic_index_in_dim(act, 2 * unit + which, 1, False).reshape(width, -1)
-            for which in (c, 1 - c)
-        )
-        far = over_core(there)
-        blocks.append((dot(mine, back_feed) + dot(far, feed_far)).astype(bf16))
-    two_far = over_core(hidden_two)
-    for unit in range(2):
-        first, second = (
-            back_before[:, (2 * unit + j) * width : (2 * unit + j + 1) * width] for j in range(2)
-        )
-        far = over_core(pick(second, first, c))
-        blocks.append(
-            (outer(hidden_two, pick(first, second, c)) + outer(two_far, far)).astype(bf16)
-        )
-    big = reduce_units(blocks, 1).astype(f32)
-    one_far, att_far = over_core(hidden_one), over_core(attended)
-
-    def late(back_query, back_key, back_value, back_project):
-        far = over_core(pick(back_project, back_key, c))
-        left, left_far = pick(hidden_one, attended, c), pick(one_far, att_far, c)
-        first = (outer(left, pick(back_key, back_project, c)) + outer(left_far, far)).astype(bf16)
-        far = over_core(pick(back_value, back_query, c))
-        second = (
-            outer(hidden_one, pick(back_query, back_value, c)) + outer(one_far, far)
-        ).astype(bf16)
-        small = reduce_units([first, second], 2).astype(f32)
-        con = big[0:2].reshape(-1, width)
-        exp = jnp.concatenate([big[2, 0], big[2, 1], big[3, 0], big[3, 1]], axis=1)
-        att = jnp.concatenate([small[1, 0], small[0, 0], small[1, 1]], axis=1)
-        return att, small[0, 1], exp, con
-
-    return late
-
-
-def reduce_plain(early, hidden_one, attended, hidden_two, activated, back_feed, back_before):
+        name="reduce",
+    )(act, feed, hidden, *befores, pair, project, starts, *slabs, up)
+
+
+def reduce_fast(lefts, feed, befores, starts, slabs, up, back_project):
+    width = feed.shape[1]
+    sums, qv, back_key = reduce_all(lefts, feed, befores, back_project, starts, slabs, up)
+
+    def late():
+        con = sums[0:2].reshape(-1, width)
+        exp = jnp.concatenate([sums[2, 0], sums[2, 1], sums[3, 0], sums[3, 1]], axis=1)
+        att = jnp.concatenate([sums[5, 0], sums[4, 0], sums[5, 1]], axis=1)
+        return tuple(part.astype(f32) for part in (att, sums[4, 1], exp, con))
+
+    return (qv[0], back_key, qv[1]), late
+
+
+def reduce_plain(lefts, feed, befores, starts, slabs, up, back_project):
+    hidden_one, attended, hidden_two, activated = lefts
+    back_query, back_key, back_value = attend_back(starts, *slabs, up)
+
     def total(left, right):
         part = lax.psum_scatter(
             outer(left, right).astype(bf16), "rows", scatter_dimension=0, tiled=True
         )
         return lax.psum(part.astype(f32), "seg")
 
-    con = total(activated, back_feed)
-    exp = total(hidden_two, back_before)
-
-    def late(back_query, back_key, back_value, back_project):
+    def late():
         att = total(hidden_one, jnp.concatenate([back_query, back_key, back_value], axis=1))
-        return att, total(attended, back_project), exp, con
-
-    return late
+        exp = total(hidden_two, jnp.concatenate(befores, axis=1))
+        return att, total(attended, back_project), exp, total(activated, feed)
+
+    return (back_query, back_key, back_value), late
 
 
 def on_device(
@@ -912,18 +1132,7 @@
         segments,
         tokens,
     )
-    (
-        modulation,
-        hidden_one,
-        slabs,
-        attended,
-        projected,
-        middle,
-        hidden_two,
-        before,
-        activated,
-        feedforward,
-    ) = saved
+    modulation, slabs, projected, middle, before, feedforward, lefts = saved
     shift_one, scale_one, gate_one, shift_two, scale_two, gate_two = of_tokens(
         onehot, modulation, width
     )
@@ -934,59 +1143,51 @@
     back_feed = (upstream * gate_two).astype(bf16)
     back_before = []
     for j, part in enumerate(before):
-        back_active = back_dot(back_feed, w_con[j * width : (j + 1) * width])
+        back_active = back_dot(back_feed, w_con[j])
         back_before.append(jax.vjp(gelu, part)[1](back_active)[0].astype(bf16))
-    back_before = jnp.concatenate(back_before, axis=1)
-    reduce = reduce_fast if fast else reduce_plain
-    late = reduce(None, hidden_one, attended, hidden_two, activated, back_feed, back_before)
-    back_hidden_two = sum(
-        back_dot(back_before[:, j * width : (j + 1) * width], w_exp[j]) for j in range(4)
-    )
+    back_hidden_two = sum(back_dot(back_before[j], w_exp[j]) for j in range(4))
     back_middle = upstream + norm_back(back_hidden_two * (1.0 + scale_two), normed_two, inverse_two)
     back_gate_one = back_middle * projected
     back_project = (back_middle * gate_one).astype(bf16)
     back_attend = back_dot(back_project, w_proj).astype(bf16)
-    back_query, back_key, back_value = attend_back(starts, *slabs, back_attend)
-    grad_att, grad_proj, grad_exp, grad_con = late(back_query, back_key, back_value, back_project)
+    reduce = reduce_fast if fast else reduce_plain
+    (back_query, back_key, back_value), late = reduce(
+        lefts, back_feed, back_before, starts, slabs, back_attend, back_project
+    )
     back_hidden_one = (
         back_dot(back_query, w_att[0]) + back_dot(back_key, w_att[1]) + back_dot(back_value, w_att[2])
     )
     back_tokens = back_middle + norm_back(
         back_hidden_one * (1.0 + scale_one), normed_one, inverse_one
     )
-    back_modulation = jnp.concatenate(
-        [
-            outer(onehot, part, highest)
-            for part in (
-                back_hidden_one,
-                back_hidden_one * normed_one,
-                back_gate_one,
-                back_hidden_two,
-                back_hidden_two * normed_two,
-                back_gate_two,
-            )
-        ],
-        axis=1,
-    )
-    columns = jnp.concatenate(
-        [
-            jnp.sum(part.astype(f32), axis=0)
-            for part in (back_query, back_value, back_project, back_before, back_feed)
-        ]
-    )
-    payload = jnp.concatenate(
-        [back_modulation, columns.reshape(n_seg, -1), cond_silu.astype(f32)], axis=1
-    )
-    everyone = lax.all_gather(payload, ("rows", "seg"), axis=0, tiled=True)
-    mod_all = everyone[:, : 6 * width]
+    back_modulation = [
+        outer(onehot, part, highest)
+        for part in (
+            back_hidden_one,
+            back_hidden_one * normed_one,
+            back_gate_one,
+            back_hidden_two,
+            back_hidden_two * normed_two,
+            back_gate_two,
+        )
+    ]
+    columns = [
+        jnp.sum(part.astype(f32), axis=0, keepdims=True)
+        for part in (back_query, back_value, back_project, *back_before, back_feed)
+    ]
+    payload = jnp.concatenate(back_modulation + [cond_silu.astype(f32)] + columns, axis=0)
+    everyone = lax.all_gather(payload, ("rows", "seg"), axis=0)
+    grad_att, grad_proj, grad_exp, grad_con = late()
+    mods = [
+        everyone[:, j * n_seg : (j + 1) * n_seg].reshape(-1, width) for j in range(6)
+    ]
     cond_rows = lax.dynamic_slice_in_dim(
-        everyone, everyone.shape[1] - width + row * shard, shard, axis=1
-    )
-    grad_mod = outer(cond_rows, mod_all, highest)
-    devices = everyone.shape[0] // n_seg
-    rest = jnp.sum(everyone[:, 6 * width : -width].reshape(devices, -1), axis=0)
+        everyone[:, 6 * n_seg : 7 * n_seg].reshape(-1, width), row * shard, shard, axis=1
+    )
+    grad_mod = outer(cond_rows, jnp.concatenate(mods, axis=1), highest)
+    rest = jnp.sum(everyone[:, 7 * n_seg :], axis=0).reshape(-1)
     grad_bias = lax.dynamic_slice_in_dim(
-        jnp.concatenate([rest, jnp.sum(mod_all, axis=0)]),
+        jnp.concatenate([rest] + [jnp.sum(part, axis=0) for part in mods]),
         row * bias_master.shape[0],
         bias_master.shape[0],
     )

time: 778 us -> 703 us (0.904)
  matrix products: 165 us -> 89.2 us
  waiting for transfers between devices: 0.04 us -> 39.9 us
  local copies, waits for them, and re-layouts: 77.6 us -> 40.9 us
    dot_general x15 -> x7, matrix products: 73.2 us -> 21.5 us  [outer(): lax.dot_general(left, right, (((0,), (0,)), ((), ())), precision=precisio...]
    all_gather x1, waiting for transfers between devices: 0.01 us -> 39.8 us  [on_device(): everyone = lax.all_gather(payload, ('rows', 'seg'), axis=0)]
    dot_general x4 -> x0, matrix products: 18.3 us -> none  [dot(): return jnp.dot(left, right, preferred_element_type=f32)]
    unnamed x191 -> x128, local copies, waits for them, and re-layouts: 40.3 us -> 24 us
    another operation x5 -> x0, other arithmetic: 10 us -> none  [the longest x2 8.07 us: reduce_units(): jnp.stack(blocks).reshape(units, 8, n, width)]
    convert_element_type x2 -> x5, other arithmetic: 0.53 us -> 8.32 us  [the longest x4 7 us: forward_fast(): low = [part.astype(bf16) for part in own_parts]]
    pallas_call x3 -> x1, Pallas kernels: 237 us -> 236 us  [reduce_all(): pl.pallas_call(reduce_kernel, out_shape=(jax.ShapeDtypeStruct((6, 2, n, w...]
  transfers between devices with their start and end apart: 11 -> 1, of which waited for: 0 -> 1; matrix products, arithmetic and copies ran while one was open for 30% -> 3% of each run, Pallas kernels for 31% -> 0%
where the time goes in v4:
time: 703 us; the launch traced here: 693 us
  Pallas kernels  448 us (64%)
  matrix products  89.2 us (13%)
  other arithmetic  60.2 us (9%)
  local copies, waits for them, and re-layouts  40.9 us (6%)
  waiting for transfers between devices  39.9 us (6%)
  between operations  15.3 us (2%)
    pallas_call x1, Pallas kernels, reduce_all(): pl.pallas_call(reduce_kernel, out_shape=(jax.ShapeDtypeStruct((6, 2, n, w...  236 us
    pallas_call x1, Pallas kernels, forward_fast(): pl.pallas_call(forward_kernel, out_shape=(shape(bf16, 8, n, width),) * 8...  211 us
    dot_general x12, matrix products, back_dot(): lax.dot_general(left, right, (((1,), (1,)), ((), ())), preferred_element_...  67.6 us
    all_gather x1, waiting for transfers between devices, on_device(): everyone = lax.all_gather(payload, ('rows', 'seg'), axis=0)  39.8 us
    unnamed x128, local copies, waits for them, and re-layouts  24 us
    dot_general x7, matrix products, outer(): lax.dot_general(left, right, (((0,), (0,)), ((), ())), precision=precisio...  21.5 us
    sub x5, other arithmetic, adam_update(): master - learning * (first_hat / (jnp.sqrt(second_hat) + adam_epsilon) +...  18.1 us
  transfers between devices with their start and end apart: 1, of which 1 were waited for; matrix products, arithmetic and copies ran while one was open for 3% of the time, Pallas kernels for 0%

profile of v4, /device:TPU:1, one launch (start us, length us, event | category | flops | bytes accessed | tf_op | source)
XLA Modules:
  0.0 693.0 jit_solution(9975786820329334456)
XLA Ops:
  26.3 211.5 %forward.1 = (bf16[8,144,1152]{2,1,0:T(8,128)(2,1)}, bf16[8,144,1152]{2,1,0:T(8,128)(2,1)}, bf16[8,144,1152]{2,1,0:T(8,128)(2,1)}, bf16[8,144,1152]{2,1,0:T(8,12...) custom-call(bf16[144,3456]{1,0:T(8,128)(2,1)} %convert_element_type., ...), custom_call_target="tpu_custom_call" | custom-call | tf_op jit(solution)/shard_map/forward/pallas_call | solution.py:608
  241.7 6.0 multiply_add_fusion
  248.2 4.1 copy-done.50
  255.0 4.6 convert_reduce_fusion.2
  259.7 7.3 %convert_reduce_fusion.3 = (f32[1152]{0:T(1024)S(1)}, bf16[768,1152]{1,0:T(8,128)(2,1)S(1)}) fusion(f32[768,1152]{1,0:T(8,128)} %get-tuple-element.59, bf16[768,1152]{1,0:T(8,128)(2,1)S(1)} %get-tuple-element.119.feed, bf16[1152,1152]{1,0:T(8,128)(2,1)} %bitcast.110), kind=kOutput, calls=%fused_computation.85 | convolution fusion | flops 2060548992 | bytes 9736704 | tf_op jit(solution)/shard_map/dot_general | solution.py:84
  267.0 6.8 convert_reduce_fusion.4
  273.8 7.3 %convert_reduce_fusion.5 = (f32[1152]{0:T(1024)S(1)}, bf16[768,1152]{1,0:T(8,128)(2,1)S(1)}) fusion(f32[768,1152]{1,0:T(8,128)} %get-tuple-element.52, bf16[768,1152]{1,0:T(8,128)(2,1)S(1)} %get-tuple-element.119.feed, bf16[1152,1152]{1,0:T(8,128)(2,1)} %bitcast.108), kind=kOutput, calls=%fused_computation.87 | convolution fusion | flops 2060548992 | bytes 9736704 | tf_op jit(solution)/shard_map/dot_general | solution.py:84
  281.2 6.9 %fusion.117 = f32[768,1152]{1,0:T(8,128)} fusion(bf16[768,1152]{1,0:T(8,128)(2,1)S(1)} %get-tuple-element.127.b0, bf16[1152,1152]{1,0:T(8,128)(2,1)} %bitcast.107), kind=kOutput, calls=%fused_computation.217 | convolution fusion | flops 2038431744 | bytes 7962624 | tf_op jit(solution)/shard_map/dot_general | solution.py:84
  288.1 5.8 convolution_add_fusion.4
  293.9 5.9 convolution_add_fusion.3
  299.8 6.4 fusion.98
  314.1 3.8 convolution_convert_fusion.up
  318.0 236.1 %reduce.24 = (bf16[6,2,144,1152]{3,2,1,0:T(8,128)(2,1)}, bf16[2,768,1152]{2,1,0:T(8,128)(2,1)}, bf16[768,1152]{1,0:T(8,128)(2,1)}) custom-call(bf16[8,4,144,768]{3,2,1,0:T(8,128)(2,1)} %bitcast.94, bf16[768,1152]{1,0:T(8,128)(2,1)} %copy-done.18, bf16[8,144,768]{2,1,0:T(8,128)(2,1)} %bitcast.97, bf16[768,1152]{1,0:T(8,128)(2,1)} %copy-done.36, ...), custom_call_target="tpu_custom_call" | custom-call | tf_op jit(solution)/shard_map/reduce/pallas_call | solution.py:1029
  557.1 4.6 fusion.58
  564.5 5.5 fusion.99
  577.5 3.2 concatenate.24
  584.2 3.6 multiply_subtract_fusion.4
  587.8 4.1 fusion.10
  592.3 3.8 multiply_subtract_fusion.3
  597.9 5.1 multiply_subtract_fusion.1
  604.1 4.2 multiply_subtract_fusion.2
  608.3 39.8 %all-gather.4.cloned.1.call-done = f32[32,36,1152]{2,1,0:T(8,128)} async-done(((f32[1,36,1152]{2,1,0:T(8,128)}), f32[32,36,1152]{2,1,0:T(8,128)}) %all-gather.4.cloned.1.call-update) | async-done | bytes 5308432 | tf_op jit(solution)/shard_map/all_gather | solution.py:1179
  650.5 5.7 slice_reduce_fusion.5
  673.1 11.4 %multiply_subtract_fusion = (f32[144,6912]{1,0:T(8,128)}, f32[144,6912]{1,0:T(8,128)}, f32[144,6912]{1,0:T(8,128)}) fusion(f32[144,6912]{1,0:T(8,128)S(1)} %copy-done.9, f32[144,6912]{1,0:T(8,128)} %param.27, f32[144,6912]{1,0:T(8,128)} %param.28, f32[128,6912]{1,0:T(8,128)S(1)} %constant_dynamic-update-slice_fusion, f32[128,1152]{1,0:T(8,128)} %reshape.180, ...), kind=kOutput, calls=%fused_computation.33 | convolution fusion | flops 1543753728 | bytes 27557892 | tf_op jit(solution)/shard_map/dot_general | solution.py:70
  (191 shorter events, 74.2 us)
Async XLA Ops:
  7.2 13.7 %copy-start.15 = (f32[144,4608]{1,0:T(8,128)S(1)}, f32[144,4608]{1,0:T(8,128)}, u32[]{:S(2)}) copy-start(f32[144,4608]{1,0:T(8,128)} %param.35) | copy-start | bytes 7962628
  7.2 640.9 %all-gather.4.cloned.1.call-start = ((), (), s32[]{:S(2)}) async-start(), calls=%async_computation | async-start | bytes 6082560 | tf_op jit(solution)/shard_map/all_gather | solution.py:1179
  241.7 6.0 copy-start.10
  247.7 63.4 %copy-start.1 = (f32[768,6912]{1,0:T(8,128)}, f32[768,6912]{1,0:T(8,128)S(1)}, u32[]{:S(2)}) copy-start(f32[768,6912]{1,0:T(8,128)S(1)} %multiply_add_fusion) | copy-start | bytes 63700996
  247.7 7.3 %copy-start.56 = (bf16[2,4,144,1152]{3,2,1,0:T(8,128)(2,1)S(1)}, bf16[2,4,144,1152]{3,2,1,0:T(8,128)(2,1)}, u32[]{:S(2)}) copy-start(bf16[2,4,144,1152]{3,2,1,0:T(8,128)(2,1)} %get-tuple-element.63) | copy-start | bytes 7962628
  248.2 25.6 %copy-start.18 = (bf16[768,1152]{1,0:T(8,128)(2,1)}, bf16[768,1152]{1,0:T(8,128)(2,1)S(1)}, u32[]{:S(2)}) copy-start(bf16[768,1152]{1,0:T(8,128)(2,1)S(1)} %get-tuple-element.119.feed) | copy-start | bytes 5308420
  259.6 40.2 %copy-start.19 = (bf16[768,1152]{1,0:T(8,128)(2,1)}, bf16[768,1152]{1,0:T(8,128)(2,1)S(1)}, u32[]{:S(2)}) copy-start(bf16[768,1152]{1,0:T(8,128)(2,1)S(1)} %get-tuple-element.121.b3) | copy-start | bytes 5308420
  259.6 7.4 %copy-start.49 = (f32[768,1152]{1,0:T(8,128)S(1)}, f32[768,1152]{1,0:T(8,128)}, u32[]{:S(2)}) copy-start(f32[768,1152]{1,0:T(8,128)} %get-tuple-element.56) | copy-start | bytes 10616836
  267.0 26.9 %copy-start.34 = (bf16[768,1152]{1,0:T(8,128)(2,1)}, bf16[768,1152]{1,0:T(8,128)(2,1)S(1)}, u32[]{:S(2)}) copy-start(bf16[768,1152]{1,0:T(8,128)(2,1)S(1)} %get-tuple-element.123.b2) | copy-start | bytes 5308420
  273.8 14.3 %copy-start.35 = (bf16[768,1152]{1,0:T(8,128)(2,1)}, bf16[768,1152]{1,0:T(8,128)(2,1)S(1)}, u32[]{:S(2)}) copy-start(bf16[768,1152]{1,0:T(8,128)(2,1)S(1)} %get-tuple-element.125.b1) | copy-start | bytes 5308420
  281.1 7.0 %copy-start.36 = (bf16[768,1152]{1,0:T(8,128)(2,1)}, bf16[768,1152]{1,0:T(8,128)(2,1)S(1)}, u32[]{:S(2)}) copy-start(bf16[768,1152]{1,0:T(8,128)(2,1)S(1)} %get-tuple-element.127.b0) | copy-start | bytes 5308420
  281.1 7.0 %copy-start.55 = (bf16[8,144,1152]{2,1,0:T(8,128)(2,1)S(1)}, bf16[8,144,1152]{2,1,0:T(8,128)(2,1)}, u32[]{:S(2)}) copy-start(bf16[8,144,1152]{2,1,0:T(8,128)(2,1)} %get-tuple-element.58) | copy-start | bytes 7962628
  288.1 5.8 copy-start.54
  582.2 5.5 copy-start.5
  582.2 5.5 copy-start.7
  592.3 5.5 copy-start.25
  597.9 6.2 copy-start.27
  660.0 11.5 %copy-start.30 = (f32[128,1152]{1,0:T(8,128)S(1)}, f32[128,1152]{1,0:T(8,128)}, u32[]{:S(2)}) copy-start(f32[128,1152]{1,0:T(8,128)} %reshape.185) | copy-start | bytes 1769476
  661.0 10.5 %copy-start.29 = (f32[128,1152]{1,0:T(8,128)S(1)}, f32[128,1152]{1,0:T(8,128)}, u32[]{:S(2)}) copy-start(f32[128,1152]{1,0:T(8,128)} %reshape.186) | copy-start | bytes 1769476
  662.1 9.6 %copy-start.42 = (f32[2016]{0:T(1024)S(1)}, f32[2016]{0:T(1024)}, u32[]{:S(2)}) copy-start(f32[2016]{0:T(1024)} %param.41) | copy-start | bytes 24196
  662.1 9.6 %copy-start.47 = (f32[2016]{0:T(1024)S(1)}, f32[2016]{0:T(1024)}, u32[]{:S(2)}) copy-start(f32[2016]{0:T(1024)} %param.42) | copy-start | bytes 24196
  662.1 9.6 %copy-start.48 = (f32[2016]{0:T(1024)S(1)}, f32[2016]{0:T(1024)}, u32[]{:S(2)}) copy-start(f32[2016]{0:T(1024)} %param.43) | copy-start | bytes 24196
  662.1 11.0 %copy-start.9 = (f32[144,6912]{1,0:T(8,128)S(1)}, f32[144,6912]{1,0:T(8,128)}, u32[]{:S(2)}) copy-start(f32[144,6912]{1,0:T(8,128)} %param.26) | copy-start | bytes 11943940
  673.1 11.4 %copy-start.33 = (bf16[768,1152]{1,0:T(8,128)(2,1)S(1)}, bf16[768,1152]{1,0:T(8,128)(2,1)}, u32[]{:S(2)}) copy-start(bf16[768,1152]{1,0:T(8,128)(2,1)} %get-tuple-element.171) | copy-start | bytes 5308420
  (35 other events, 106.2 us)
Sparse Core Ops, SparseCore 0:
  580.9 67.1 all-gather.3

commit v5 on v4

--- a/solution.py
+++ b/solution.py
@@ -412,15 +412,17 @@
     def step(j):
         if j < len(steps):
             u, k = steps[j]
-            if k == 0:
-                for later in [0, 1] if u == 0 else [u + 1]:
-                    if later < 6:
-                        loads[later].wait()
-                        for hop in (1, 3, 2):
-                            go(along_z(later, hop))
-            else:
+            if j == 0:
+                loads[0].wait()
+                for hop in (1, 3, 2):
+                    go(along_z(0, hop))
+            if k:
                 along_z(u, k).wait_recv()
             go(along_x(u, k))
+            if u < 5 and j % 4 < 3:
+                if k == 0:
+                    loads[u + 1].wait()
+                go(along_z(u + 1, (1, 3, 2)[j % 4]))
         if 0 <= j - 1 < len(steps):
             along_x(*steps[j - 1]).wait_recv()
             go(along_y(*steps[j - 1]))
@@ -708,6 +710,16 @@
     return output, saved, (w_att, w_proj, w_exp, w_con)
 
 
+AHEAD = 2
+
+
+def gather_last(value):
+    value = jnp.stack([value] + [over_z(value, k) for k in (1, 2, 3)])
+    for over in (over_x, over_y, over_core):
+        value = jnp.concatenate([value, over(value)])
+    return value
+
+
 class Reduce:
     def __init__(self, out, refs, units):
         self.out = out
@@ -729,6 +741,7 @@
         self.y_peer = (row, seg + 2 - 4 * self.y)
         self.c_peer = (row, seg + 1 - 2 * self.c)
         self.sent, self.outs = {u: [] for u in range(units)}, []
+        self.ready, self.next_y = -1, 0
         self.steps = [(u, k) for u in range(self.units) for k in (1, 3, 2, 0)]
         self.count = len(self.steps) + 8
 
@@ -778,10 +791,16 @@
         return remote(ref, ref, self.c_s.at[u], self.c_r.at[u], self.c_peer)
 
     def begin(self, u):
-        for k in (1, 3, 2, 0):
+        self.ready = u
+
+    def pump(self, limit):
+        while self.next_y < min(limit, len(self.steps)) and self.steps[self.next_y][0] <= self.ready:
+            u, k = self.steps[self.next_y]
             self.go(u, self.to_y(u, k))
+            self.next_y += 1
 
     def step(self, j):
+        self.pump(j + 1 + AHEAD)
         d, piece = self.d, self.piece
         mine, part = pl.ds(self.mine, piece), pl.ds(self.part, 2 * piece)
         if j < len(self.steps):
@@ -951,6 +970,8 @@
             start(index, 1)
         multiply_pair(red.d.at[u], lefts(min(u, 2)), rights(max(u - 1, 0)))
         red.begin(u)
+        if u == 0:
+            red.pump(AHEAD)
 
     def late_pulls():
         pl.semaphore_signal(
@@ -1047,6 +1068,9 @@
         + Reduce.scratch(6, 4, n, width),
         compiler_params=pltpu.CompilerParams(
             collective_id=1, has_side_effects=True, vmem_limit_bytes=60 << 20
+        ),
+        cost_estimate=pl.CostEstimate(
+            flops=180_000_000_000, bytes_accessed=60_000_000, transcendentals=0
         ),
         name="reduce",
     )(act, feed, hidden, *befores, pair, project, starts, *slabs, up)
@@ -1150,6 +1174,22 @@
     back_gate_one = back_middle * projected
     back_project = (back_middle * gate_one).astype(bf16)
     back_attend = back_dot(back_project, w_proj).astype(bf16)
+    def segment_sums(*parts):
+        return [outer(onehot, part, highest) for part in parts]
+
+    def column_sums(*parts):
+        return [jnp.sum(part.astype(f32), axis=0, keepdims=True) for part in parts]
+
+    early = jnp.concatenate(
+        segment_sums(
+            back_gate_one, back_hidden_two, back_hidden_two * normed_two, back_gate_two
+        )
+        + [cond_silu.astype(f32)]
+        + column_sums(back_project, *back_before, back_feed),
+        axis=0,
+    )
+    back_attend, early = lax.optimization_barrier((back_attend, early))
+    early = lax.all_gather(early.astype(bf16), ("rows", "seg"), axis=0)
     reduce = reduce_fast if fast else reduce_plain
     (back_query, back_key, back_value), late = reduce(
         lefts, back_feed, back_before, starts, slabs, back_attend, back_project
@@ -1160,34 +1200,35 @@
     back_tokens = back_middle + norm_back(
         back_hidden_one * (1.0 + scale_one), normed_one, inverse_one
     )
-    back_modulation = [
-        outer(onehot, part, highest)
-        for part in (
-            back_hidden_one,
-            back_hidden_one * normed_one,
-            back_gate_one,
-            back_hidden_two,
-            back_hidden_two * normed_two,
-            back_gate_two,
-        )
+    last = segment_sums(back_hidden_one, back_hidden_one * normed_one)
+    last = last + [cond_silu.astype(f32)] + column_sums(back_query, back_value)
+    last = jnp.concatenate(last, axis=0)
+    last = jnp.pad(last, ((0, -last.shape[0] % 16), (0, 0))).astype(bf16)
+    last, early = lax.optimization_barrier((last, early))
+    if fast:
+        last = gather_last(last)
+    else:
+        last = lax.all_gather(last, ("rows", "seg"), axis=0)
+    grad_att, grad_proj, grad_exp, grad_con = late()
+
+    def part_of(rows, number):
+        return rows[:, number * n_seg : (number + 1) * n_seg].reshape(-1, width)
+
+    def mod_gradient(conds, parts):
+        conds = lax.dynamic_slice_in_dim(conds, row * shard, shard, axis=1)
+        return outer(conds, jnp.concatenate(parts, axis=1))
+
+    mods = [part_of(last, j) for j in range(2)], [part_of(early, j) for j in range(4)]
+    grad_mod = jnp.concatenate(
+        [mod_gradient(part_of(last, 2), mods[0]), mod_gradient(part_of(early, 4), mods[1])], axis=1
+    )
+    totals = [last[:, 3 * n_seg : 3 * n_seg + 2], early[:, 5 * n_seg :]]
+    totals = [jnp.sum(part.astype(f32), axis=0) for part in totals]
+    totals += [
+        jnp.sum(part.astype(f32), axis=0, keepdims=True) for part in mods[0] + mods[1]
     ]
-    columns = [
-        jnp.sum(part.astype(f32), axis=0, keepdims=True)
-        for part in (back_query, back_value, back_project, *back_before, back_feed)
-    ]
-    payload = jnp.concatenate(back_modulation + [cond_silu.astype(f32)] + columns, axis=0)
-    everyone = lax.all_gather(payload, ("rows", "seg"), axis=0)
-    grad_att, grad_proj, grad_exp, grad_con = late()
-    mods = [
-        everyone[:, j * n_seg : (j + 1) * n_seg].reshape(-1, width) for j in range(6)
-    ]
-    cond_rows = lax.dynamic_slice_in_dim(
-        everyone[:, 6 * n_seg : 7 * n_seg].reshape(-1, width), row * shard, shard, axis=1
-    )
-    grad_mod = outer(cond_rows, jnp.concatenate(mods, axis=1), highest)
-    rest = jnp.sum(everyone[:, 7 * n_seg :], axis=0).reshape(-1)
     grad_bias = lax.dynamic_slice_in_dim(
-        jnp.concatenate([rest] + [jnp.sum(part, axis=0) for part in mods]),
+        jnp.concatenate(totals, axis=0).reshape(-1),
         row * bias_master.shape[0],
         bias_master.shape[0],
     )

time: 703 us -> 637 us (0.906)
  Pallas kernels: 448 us -> 401 us
  waiting for transfers between devices: 39.9 us -> 10.2 us
    pallas_call x1, Pallas kernels: 236 us -> 194 us  [reduce_all(): pl.pallas_call(reduce_kernel, out_shape=(jax.ShapeDtypeStruct((6, 2, n, w...]
    all_gather x1, waiting for transfers between devices: 39.8 us -> 0.01 us  [on_device(): early = lax.all_gather(early.astype(bf16), ('rows', 'seg'), axis=0)]
    unnamed x128 -> x124, local copies, waits for them, and re-layouts: 24 us -> 11 us
    ppermute x0 -> x6, waiting for transfers between devices: none -> 10.1 us  [the longest x3 4.92 us: over_z(): return lax.ppermute(v, 'rows', ROW_Z[k])]
    sub x5 -> x6, other arithmetic: 18.1 us -> 27.6 us  [adam_update(): master - learning * (first_hat / (jnp.sqrt(second_hat) + adam_epsilon) +...]
    dot_general x7 -> x8, matrix products: 21.5 us -> 17.1 us  [outer(): lax.dot_general(left, right, (((0,), (0,)), ((), ())), precision=precisio...]
  transfers between devices with their start and end apart: 1 -> 7, of which waited for: 1 -> 4; matrix products, arithmetic and copies ran while one was open for 3% -> 9% of each run, Pallas kernels for 0% -> 31%
where the time goes in v5:
time: 637 us; the launch traced here: 627 us
  Pallas kernels  401 us (63%)
  matrix products  84.5 us (13%)
  other arithmetic  66.5 us (10%)
  local copies, waits for them, and re-layouts  42.9 us (7%)
  between operations  15.2 us (2%)
  waiting for transfers between devices  10.2 us (2%)
    pallas_call x1, Pallas kernels, forward_fast(): pl.pallas_call(forward_kernel, out_shape=(shape(bf16, 8, n, width),) * 8...  207 us
    pallas_call x1, Pallas kernels, reduce_all(): pl.pallas_call(reduce_kernel, out_shape=(jax.ShapeDtypeStruct((6, 2, n, w...  194 us
    dot_general x12, matrix products, back_dot(): lax.dot_general(left, right, (((1,), (1,)), ((), ())), preferred_element_...  67.5 us
    sub x6, other arithmetic, adam_update(): master - learning * (first_hat / (jnp.sqrt(second_hat) + adam_epsilon) +...  27.6 us
    dot_general x8, matrix products, outer(): lax.dot_general(left, right, (((0,), (0,)), ((), ())), precision=precisio...  17.1 us
  transfers between devices with their start and end apart: 7, of which 4 were waited for; matrix products, arithmetic and copies ran while one was open for 9% of the time, Pallas kernels for 31%

profile of v5, /device:TPU:1, one launch (start us, length us, event | category | flops | bytes accessed | tf_op | source)
XLA Modules:
  0.0 626.6 jit_solution(1913266146799165515)
XLA Ops:
  23.9 206.9 %forward.1 = (bf16[8,144,1152]{2,1,0:T(8,128)(2,1)}, bf16[8,144,1152]{2,1,0:T(8,128)(2,1)}, bf16[8,144,1152]{2,1,0:T(8,128)(2,1)}, bf16[8,144,1152]{2,1,0:T(8,12...) custom-call(bf16[144,3456]{1,0:T(8,128)(2,1)} %convert_element_type., ...), custom_call_target="tpu_custom_call" | custom-call | tf_op jit(solution)/shard_map/forward/pallas_call | solution.py:610
  235.5 6.0 multiply_add_fusion
  242.0 3.1 copy-done.55
  245.2 8.9 %convert_reduce_fusion.2 = (bf16[1152]{0:T(1024)(128)(2,1)S(1)}, bf16[768,1152]{1,0:T(8,128)(2,1)}) fusion(f32[768,1152]{1,0:T(8,128)} %get-tuple-element.66, bf16[768,1152]{1,0:T(8,128)(2,1)S(1)} %get-tuple-element.127.feed, bf16[1152,1152]{1,0:T(8,128)(2,1)S(1)} %bitcast.127), kind=kOutput, calls=%fused_computation.85 | convolution fusion | flops 2060548992 | bytes 9734400 | tf_op jit(solution)/shard_map/dot_general | solution.py:84
  254.1 7.2 %convert_reduce_fusion.3 = (bf16[1152]{0:T(1024)(128)(2,1)S(1)}, bf16[768,1152]{1,0:T(8,128)(2,1)}) fusion(f32[768,1152]{1,0:T(8,128)S(1)} %copy-done.46, bf16[768,1152]{1,0:T(8,128)(2,1)S(1)} %get-tuple-element.127.feed, bf16[1152,1152]{1,0:T(8,128)(2,1)} %bitcast.126), kind=kOutput, calls=%fused_computation.86 | convolution fusion | flops 2060548992 | bytes 9734400 | tf_op jit(solution)/shard_map/dot_general | solution.py:84
  261.3 6.9 %convert_reduce_fusion.4 = (bf16[1152]{0:T(1024)(128)(2,1)S(1)}, bf16[768,1152]{1,0:T(8,128)(2,1)}) fusion(f32[768,1152]{1,0:T(8,128)} %get-tuple-element.60, bf16[768,1152]{1,0:T(8,128)(2,1)S(1)} %get-tuple-element.127.feed, bf16[1152,1152]{1,0:T(8,128)(2,1)S(1)} %bitcast.125), kind=kOutput, calls=%fused_computation.87 | convolution fusion | flops 2060548992 | bytes 9734400 | tf_op jit(solution)/shard_map/dot_general | solution.py:84
  268.2 6.3 %convert_reduce_fusion.5 = (bf16[1152]{0:T(1024)(128)(2,1)S(1)}, bf16[768,1152]{1,0:T(8,128)(2,1)S(1)}) fusion(f32[768,1152]{1,0:T(8,128)S(1)} %copy-done.45, bf16[768,1152]{1,0:T(8,128)(2,1)S(1)} %get-tuple-element.127.feed, bf16[1152,1152]{1,0:T(8,128)(2,1)} %bitcast.124), kind=kOutput, calls=%fused_computation.88 | convolution fusion | flops 2060548992 | bytes 9734400 | tf_op jit(solution)/shard_map/dot_general | solution.py:84
  277.3 6.1 convolution_add_fusion.4
  283.4 5.9 convolution_add_fusion.3
  289.3 6.8 %fusion.114 = (f32[768]{0:T(1024)S(1)}, f32[768]{0:T(1024)S(1)}, f32[768,1152]{1,0:T(8,128)S(1)}) fusion(f32[768,6912]{1,0:T(8,128)S(1)} %multiply_add_fusion, f32[768]{0:T(1024)S(1)} %add_rsqrt_fusion.1, f32[768,1152]{1,0:T(8,128)S(1)} %copy-done, f32[768]{0:T(1024)S(1)} %broadcast_multiply_fusion.5, f32[768,1152]{1,0:T(8,128)} %convolution_add_fusion.3, ...), kind=kOutput, calls=%fused_computation.238 | convolution fusion | flops 2045508096 | bytes 18591744 | tf_op jit(solution)/shard_map/dot_general | solution.py:84
  308.9 4.7 fusion.49
  313.6 4.2 convolution_convert_fusion.up
  317.9 5.4 concatenate.46
  324.8 194.5 %reduce.30 = (bf16[6,2,144,1152]{3,2,1,0:T(8,128)(2,1)}, bf16[2,768,1152]{2,1,0:T(8,128)(2,1)}, bf16[768,1152]{1,0:T(8,128)(2,1)}) custom-call(bf16[8,4,144,768]{3,2,1,0:T(8,128)(2,1)} %bitcast.115, bf16[768,1152]{1,0:T(8,128)(2,1)} %copy-done.27, bf16[8,144,768]{2,1,0:T(8,128)(2,1)} %bitcast.128, bf16[768,1152]{1,0:T(8,128)(2,1)} %copy-done.56, ...), custom_call_target="tpu_custom_call" | custom-call | flops 179999997952 | bytes 60000000 | tf_op jit(solution)/shard_map/reduce/pallas_call | solution.py:1050
  519.4 4.3 fusion.61
  527.1 5.4 fusion.115
  538.3 6.1 fusion.10
  544.7 3.7 multiply_subtract_fusion.3
  549.5 3.1 multiply_subtract_fusion.4
  552.7 6.6 %multiply_subtract_fusion.1 = (f32[576,1152]{1,0:T(8,128)}, f32[576,1152]{1,0:T(8,128)}, f32[576,1152]{1,0:T(8,128)}) fusion(f32[576,1152]{1,0:T(8,128)S(1)} %copy-done.9, bf16[2,2,144,1152]{3,2,1,0:T(8,128)(2,1)S(1)} %copy-done.13, f32[576,1152]{1,0:T(8,128)S(1)} %copy-done.19, f32[576,1152]{1,0:T(8,128)} %param.40), kind=kLoop, calls=%fused_computation.104 | loop fusion | flops 10616832 | bytes 17252352 | tf_op jit(solution)/shard_map/sub | solution.py:217
  559.4 4.0 multiply_subtract_fusion.2
  566.4 4.0 collective-permute-done.1
  580.3 3.1 collective-permute-done.4
  609.3 8.8 %multiply_subtract_fusion = (f32[144,6912]{1,0:T(8,128)}, f32[144,6912]{1,0:T(8,128)}, f32[144,6912]{1,0:T(8,128)}) fusion(f32[144,6912]{1,0:T(8,128)} %param.26, f32[144,4608]{1,0:T(8,128)S(1)} %fusion.69, f32[144,2304]{1,0:T(8,128)S(1)} %fusion.79, f32[144,6912]{1,0:T(8,128)} %param.27, f32[144,6912]{1,0:T(8,128)} %param.28), kind=kLoop, calls=%fused_computation.34 | loop fusion | flops 15925248 | bytes 27869184 | tf_op jit(solution)/shard_map/sub | solution.py:217
  (216 shorter events, 89.3 us)
Async XLA Ops:
  7.2 11.4 %copy-start.10 = (f32[144,4608]{1,0:T(8,128)S(1)}, f32[144,4608]{1,0:T(8,128)}, u32[]{:S(2)}) copy-start(f32[144,4608]{1,0:T(8,128)} %param.35) | copy-start | bytes 7962628
  7.2 556.2 %all-gather.4.cloned.1.call-start = ((), (), s32[]{:S(2)}) async-start(), calls=%async_computation | async-start | bytes 2433024 | tf_op jit(solution)/shard_map/all_gather | solution.py:1192
  8.1 300.8 %copy-start.32 = (s32[768]{0:T(1024)}, s32[768]{0:T(1024)S(1)}, u32[]{:S(2)}) copy-start(s32[768]{0:T(1024)S(1)} %reduce.11) | copy-start | bytes 9220
  9.5 308.4 %copy-start.35 = (bf16[4,1152]{1,0:T(4,128)(2,1)}, bf16[4,1152]{1,0:T(4,128)(2,1)S(1)}, u32[]{:S(2)}) copy-start(bf16[4,1152]{1,0:T(4,128)(2,1)S(1)} %fusion.99) | copy-start | bytes 27652
  241.5 64.0 %copy-start.1 = (f32[768,6912]{1,0:T(8,128)}, f32[768,6912]{1,0:T(8,128)S(1)}, u32[]{:S(2)}) copy-start(f32[768,6912]{1,0:T(8,128)S(1)} %multiply_add_fusion) | copy-start | bytes 63700996
  242.0 26.2 %copy-start.27 = (bf16[768,1152]{1,0:T(8,128)(2,1)}, bf16[768,1152]{1,0:T(8,128)(2,1)S(1)}, u32[]{:S(2)}) copy-start(bf16[768,1152]{1,0:T(8,128)(2,1)S(1)} %get-tuple-element.127.feed) | copy-start | bytes 5308420
  245.2 8.9 %copy-start.46 = (f32[768,1152]{1,0:T(8,128)S(1)}, f32[768,1152]{1,0:T(8,128)}, u32[]{:S(2)}) copy-start(f32[768,1152]{1,0:T(8,128)} %get-tuple-element.63) | copy-start | bytes 10616836
  254.1 7.2 %copy-start.54 = (bf16[2,4,144,1152]{3,2,1,0:T(8,128)(2,1)S(1)}, bf16[2,4,144,1152]{3,2,1,0:T(8,128)(2,1)}, u32[]{:S(2)}) copy-start(bf16[2,4,144,1152]{3,2,1,0:T(8,128)(2,1)} %get-tuple-element.61) | copy-start | bytes 7962628
  261.3 6.9 %copy-start.45 = (f32[768,1152]{1,0:T(8,128)S(1)}, f32[768,1152]{1,0:T(8,128)}, u32[]{:S(2)}) copy-start(f32[768,1152]{1,0:T(8,128)} %get-tuple-element.56) | copy-start | bytes 10616836
  313.6 9.7 %copy-start.2 = (bf16[768,1152]{1,0:T(8,128)(2,1)S(1)}, bf16[768,1152]{1,0:T(8,128)(2,1)}, u32[]{:S(2)}) copy-start(bf16[768,1152]{1,0:T(8,128)(2,1)} %tokens.1) | copy-start | bytes 5308420
  324.8 194.5 %copy-start.49 = (bf16[8,144,1152]{2,1,0:T(8,128)(2,1)S(1)}, bf16[8,144,1152]{2,1,0:T(8,128)(2,1)}, u32[]{:S(2)}) copy-start(bf16[8,144,1152]{2,1,0:T(8,128)(2,1)} %get-tuple-element.80) | copy-start | bytes 7962628
  552.7 6.7 %copy-start.11 = (f32[144,4608]{1,0:T(8,128)S(1)}, f32[144,4608]{1,0:T(8,128)}, u32[]{:S(2)}) copy-start(f32[144,4608]{1,0:T(8,128)} %param.35) | copy-start | bytes 7962628
  552.7 6.7 %copy-start.20 = (f32[144,4608]{1,0:T(8,128)S(1)}, f32[144,4608]{1,0:T(8,128)}, u32[]{:S(2)}) copy-start(f32[144,4608]{1,0:T(8,128)} %param.36) | copy-start | bytes 7962628
  552.7 6.7 %copy-start.21 = (f32[144,4608]{1,0:T(8,128)S(1)}, f32[144,4608]{1,0:T(8,128)}, u32[]{:S(2)}) copy-start(f32[144,4608]{1,0:T(8,128)} %param.37) | copy-start | bytes 7962628
  552.7 6.7 %copy-start.28 = (bf16[144,1152]{1,0:T(8,128)(2,1)S(1)}, bf16[144,1152]{1,0:T(8,128)(2,1)}, u32[]{:S(2)}) copy-start(bf16[144,1152]{1,0:T(8,128)(2,1)} %get-tuple-element.139) | copy-start | bytes 995332
  552.7 6.7 %copy-start.29 = (bf16[144,1152]{1,0:T(8,128)(2,1)S(1)}, bf16[144,1152]{1,0:T(8,128)(2,1)}, u32[]{:S(2)}) copy-start(bf16[144,1152]{1,0:T(8,128)(2,1)} %get-tuple-element.140) | copy-start | bytes 995332
  563.4 23.1 %copy-start.14 = (bf16[32,26,1152]{2,1,0:T(8,128)(2,1)S(1)}, bf16[32,26,1152]{2,1,0:T(8,128)(2,1)}, u32[]{:S(2)}) copy-start(bf16[32,26,1152]{2,1,0:T(8,128)(2,1)} %all-gather.4.cloned.1.call-done) | copy-start | bytes 5750788
  563.4 3.1 collective-permute-start.2
  564.5 5.9 collective-permute-start.1
  564.5 5.9 collective-permute-start
  570.4 5.0 collective-permute-start.3
  576.2 7.2 %collective-permute-start.4 = (bf16[8,16,1152]{2,1,0:T(8,128)(2,1)S(1)}, bf16[8,16,1152]{2,1,0:T(8,128)(2,1)S(1)}, u32[]{:S(2)}, u32[]{:S(2)}) collective-permute-start(bf16[8,16,1152]{2,1,0:T(8,128)(2,1)S(1)} %get-tuple-element.158), channel_id=1, source_target_pairs={{0,2},{1,3},{2,0},{3,1},{4,6},{5,7},{6,4},{7,5},{8,10},{9,11},{10,... | collective-permute-start | bytes 884744 | tf_op jit(solution)/shard_map/ppermute | solution.py:42
  584.3 10.4 %collective-permute-start.5 = (bf16[16,16,1152]{2,1,0:T(8,128)(2,1)}, bf16[16,16,1152]{2,1,0:T(8,128)(2,1)}, u32[]{:S(2)}, u32[]{:S(2)}) collective-permute-start(bf16[16,16,1152]{2,1,0:T(8,128)(2,1)} %get-tuple-element.154), channel_id=1, source_target_pairs={{0,1},{1,0},{2,3},{3,2},{4,5},{5,4},{6,7},{7,6},{8,9},{9,8},{10,11... | collective-permute-start | bytes 1769480 | tf_op jit(solution)/shard_map/ppermute | solution.py:46
  609.3 8.8 %copy-start.26 = (bf16[768,1152]{1,0:T(8,128)(2,1)S(1)}, bf16[768,1152]{1,0:T(8,128)(2,1)}, u32[]{:S(2)}) copy-start(bf16[768,1152]{1,0:T(8,128)(2,1)} %get-tuple-element.197) | copy-start | bytes 5308420
  (42 other events, 153.3 us)
Sparse Core Ops, SparseCore 0:
  323.4 62.4 all-gather.3

commit v6 on v5

--- a/solution.py
+++ b/solution.py
@@ -247,6 +247,10 @@
 def layer_rows(values):
     center = values - jnp.mean(values, axis=-1, keepdims=True)
     return center * lax.rsqrt(jnp.mean(center * center, axis=-1, keepdims=True) + norm_epsilon)
+
+
+LEAD_FROM = 4
+LEAD = (2, 1, 0)
 
 
 def forward_kernel(
@@ -409,26 +413,35 @@
         copy.start()
         return copy
 
+    def send_x(j):
+        u, k = steps[j]
+        if j == 0:
+            loads[0].wait()
+            for hop in (1, 3, 2):
+                go(along_z(0, hop))
+        if k:
+            along_z(u, k).wait_recv()
+        go(along_x(u, k))
+        if u < 5 and j % 4 < 3:
+            if k == 0:
+                loads[u + 1].wait()
+            go(along_z(u + 1, (1, 3, 2)[j % 4]))
+
+    def send_y(j):
+        along_x(*steps[j]).wait_recv()
+        go(along_y(*steps[j]))
+
+    def send_across(j):
+        along_y(*steps[j]).wait_recv()
+        go(across(*steps[j]))
+
+    stages = [[send_x, 0], [send_y, 0], [send_across, 0]]
+
     def step(j):
-        if j < len(steps):
-            u, k = steps[j]
-            if j == 0:
-                loads[0].wait()
-                for hop in (1, 3, 2):
-                    go(along_z(0, hop))
-            if k:
-                along_z(u, k).wait_recv()
-            go(along_x(u, k))
-            if u < 5 and j % 4 < 3:
-                if k == 0:
-                    loads[u + 1].wait()
-                go(along_z(u + 1, (1, 3, 2)[j % 4]))
-        if 0 <= j - 1 < len(steps):
-            along_x(*steps[j - 1]).wait_recv()
-            go(along_y(*steps[j - 1]))
-        if 0 <= j - 2 < len(steps):
-            along_y(*steps[j - 2]).wait_recv()
-            go(across(*steps[j - 2]))
+        for i, stage in enumerate(stages):
+            while stage[1] <= min(j - i + (LEAD[i] if j >= LEAD_FROM else 0), len(steps) - 1):
+                stage[0](stage[1])
+                stage[1] += 1
         if 0 <= j - 3 < len(steps):
             u, k = steps[j - 3]
             across(u, k).wait_recv()
@@ -574,9 +587,9 @@
     plan += [partial(project, 0), 8, partial(project, 2), 9, 10, partial(project, 1), 11]
     for first in range(0, 16, 2):
         plan += [partial(attend_heads, first, first + 2)] + ([12 + first // 4] if first % 4 else [])
-    plan += [gather_back, 16, add_projected, norm_two, 17]
-    plan += [partial(expand_block, 0), 18, partial(expand_block, 1), 19]
-    plan += [partial(expand_block, 2), 20, partial(expand_block, 3), 21, 22, 23, 24, 25, 26]
+    plan += [gather_back, 16, add_projected, 17, norm_two, 18]
+    plan += [partial(expand_block, 0), 19, partial(expand_block, 1), 20]
+    plan += [partial(expand_block, 2), 21, partial(expand_block, 3), 22, 23, 24, 25, 26]
     for item in plan + [contract]:
         if isinstance(item, int):
             step(item)
@@ -667,8 +680,10 @@
 
 
 def of_tokens(onehot, modulation, width):
-    rows = sum(onehot[:, s : s + 1] * modulation[s] for s in range(onehot.shape[1]))
-    return [rows[:, j * width : (j + 1) * width] for j in range(6)]
+    parts = [modulation[:, j * width : (j + 1) * width] for j in range(6)]
+    return [
+        sum(onehot[:, s : s + 1] * part[s] for s in range(onehot.shape[1])) for part in parts
+    ]
 
 
 def forward_plain(own_parts, cond_silu, bias_low, mod_low, starts, segments, tokens):
@@ -713,11 +728,14 @@
 AHEAD = 2
 
 
-def gather_last(value):
+def gather_last(value, beside):
     value = jnp.stack([value] + [over_z(value, k) for k in (1, 2, 3)])
-    for over in (over_x, over_y, over_core):
+    beside = list(beside)
+    for i, over in enumerate((over_x, over_y, over_core)):
+        if i < 2:
+            value, beside[i] = lax.optimization_barrier((value, beside[i]))
         value = jnp.concatenate([value, over(value)])
-    return value
+    return value, beside
 
 
 class Reduce:
@@ -1205,11 +1223,11 @@
     last = jnp.concatenate(last, axis=0)
     last = jnp.pad(last, ((0, -last.shape[0] % 16), (0, 0))).astype(bf16)
     last, early = lax.optimization_barrier((last, early))
+    grad_att, grad_proj, grad_exp, grad_con = late()
     if fast:
-        last = gather_last(last)
+        last, (grad_con, grad_exp) = gather_last(last, (grad_con, grad_exp))
     else:
         last = lax.all_gather(last, ("rows", "seg"), axis=0)
-    grad_att, grad_proj, grad_exp, grad_con = late()
 
     def part_of(rows, number):
         return rows[:, number * n_seg : (number + 1) * n_seg].reshape(-1, width)

time: 637 us -> 582 us (0.914)
  matrix products: 84.5 us -> 62.1 us
  Pallas kernels: 401 us -> 386 us
  local copies, waits for them, and re-layouts: 42.9 us -> 30.3 us
  waiting for transfers between devices: 10.2 us -> 2.29 us
    dot_general x12, matrix products: 67.5 us -> 48.9 us  [back_dot(): lax.dot_general(left, right, (((1,), (1,)), ((), ())), preferred_element_...]
    pallas_call x1, Pallas kernels: 207 us -> 189 us  [forward_fast(): pl.pallas_call(forward_kernel, out_shape=(shape(bf16, 8, n, width),) * 8...]
  transfers between devices with their start and end apart: 7 -> 7, of which waited for: 4 -> 1; matrix products, arithmetic and copies ran while one was open for 9% -> 11% of each run, Pallas kernels for 31% -> 34%
where the time goes in v6:
time: 582 us; the launch traced here: 572 us
  Pallas kernels  386 us (66%)
  other arithmetic  68.6 us (12%)
  matrix products  62.1 us (11%)
  local copies, waits for them, and re-layouts  30.3 us (5%)
  between operations  15.7 us (3%)
  starting transfers between devices  6.79 us (1%)
    pallas_call x1, Pallas kernels, reduce_all(): pl.pallas_call(reduce_kernel, out_shape=(jax.ShapeDtypeStruct((6, 2, n, w...  197 us
    pallas_call x1, Pallas kernels, forward_fast(): pl.pallas_call(forward_kernel, out_shape=(shape(bf16, 8, n, width),) * 8...  189 us
    dot_general x12, matrix products, back_dot(): lax.dot_general(left, right, (((1,), (1,)), ((), ())), preferred_element_...  48.9 us
    sub x6, other arithmetic, adam_update(): master - learning * (first_hat / (jnp.sqrt(second_hat) + adam_epsilon) +...  31.1 us
    dot_general x8, matrix products, outer(): lax.dot_general(left, right, (((0,), (0,)), ((), ())), precision=precisio...  13.2 us
  transfers between devices with their start and end apart: 7, of which 1 were waited for; matrix products, arithmetic and copies ran while one was open for 11% of the time, Pallas kernels for 34%

profile of v6, /device:TPU:1, one launch (start us, length us, event | category | flops | bytes accessed | tf_op | source)
XLA Modules:
  0.0 571.8 jit_solution(11243259139009658878)
XLA Ops:
  9.4 3.8 convert_element_type.166.w_mod
  19.9 189.2 %forward.1 = (bf16[8,144,1152]{2,1,0:T(8,128)(2,1)}, bf16[8,144,1152]{2,1,0:T(8,128)(2,1)}, bf16[8,144,1152]{2,1,0:T(8,128)(2,1)}, bf16[8,144,1152]{2,1,0:T(8,12...) custom-call(bf16[144,3456]{1,0:T(8,128)(2,1)} %convert_element_type., ...), custom_call_target="tpu_custom_call" | custom-call | tf_op jit(solution)/shard_map/forward/pallas_call | solution.py:623
  211.9 2.9 reduce_sum.226
  218.0 7.4 %convert_reduce_fusion.2 = (bf16[1152]{0:T(1024)(128)(2,1)S(1)}, bf16[768,1152]{1,0:T(8,128)(2,1)S(1)}) fusion(f32[768,1152]{1,0:T(8,128)S(1)} %copy-done.73, bf16[768,1152]{1,0:T(8,128)(2,1)S(1)} %get-tuple-element.148.feed, bf16[1152,1152]{1,0:T(8,128)(2,1)} %bitcast.108), kind=kOutput, calls=%fused_computation.77 | convolution fusion | flops 2060548992 | bytes 9734400 | tf_op jit(solution)/shard_map/dot_general | solution.py:84
  225.4 4.4 convert_reduce_fusion.3
  229.9 4.4 convert_reduce_fusion.4
  234.4 4.6 convert_reduce_fusion.5
  244.6 2.7 convolution_add_fusion.3
  247.4 3.5 fusion.102
  255.3 5.0 convert_reduce_fusion.6
  266.0 3.8 convolution_convert_fusion.up
  274.0 196.7 %reduce.54 = (bf16[6,2,144,1152]{3,2,1,0:T(8,128)(2,1)}, bf16[2,768,1152]{2,1,0:T(8,128)(2,1)}, bf16[768,1152]{1,0:T(8,128)(2,1)}) custom-call(bf16[8,4,144,768]{3,2,1,0:T(8,128)(2,1)} %bitcast.95, bf16[768,1152]{1,0:T(8,128)(2,1)} %copy-done.25, bf16[8,144,768]{2,1,0:T(8,128)(2,1)} %bitcast.109, bf16[768,1152]{1,0:T(8,128)(2,1)} %copy-done.85, ...), custom_call_target="tpu_custom_call" | custom-call | flops 179999997952 | bytes 60000000 | tf_op jit(solution)/shard_map/reduce/pallas_call | solution.py:1068
  470.7 4.3 fusion.56
  475.2 2.8 convolution_add_fusion.1
  478.5 5.5 fusion.103
  491.8 3.2 maximum_convert_fusion
  495.0 3.2 multiply_subtract_fusion.4
  501.6 3.7 multiply_subtract_fusion.3
  505.3 2.9 collective-permute-start.1
  508.8 3.0 convert_reduce_fusion.8
  528.9 7.5 %multiply_subtract_fusion.1 = (f32[576,1152]{1,0:T(8,128)}, f32[576,1152]{1,0:T(8,128)}, f32[576,1152]{1,0:T(8,128)}) fusion(f32[576,1152]{1,0:T(8,128)S(1)} %copy-done.7, f32[576,1152]{1,0:T(8,128)S(1)} %copy-done.10, f32[576,1152]{1,0:T(8,128)} %param.39, f32[576,1152]{1,0:T(8,128)} %param.40), kind=kLoop, calls=%fused_computation.95 | loop fusion | flops 9953280 | bytes 18579456 | tf_op jit(solution)/shard_map/sub | solution.py:217
  537.8 6.5 %multiply_subtract_fusion.2 = (f32[144,4608]{1,0:T(8,128)}, f32[144,4608]{1,0:T(8,128)}, f32[144,4608]{1,0:T(8,128)}) fusion(f32[144,4608]{1,0:T(8,128)S(1)} %copy-done.9, f32[144,4608]{1,0:T(8,128)S(1)} %copy-done.11, f32[144,4608]{1,0:T(8,128)S(1)} %copy-done.19, f32[144,4608]{1,0:T(8,128)} %param.37), kind=kLoop, calls=%fused_computation.97 | loop fusion | flops 9953280 | bytes 18579456 | tf_op jit(solution)/shard_map/sub | solution.py:217
  546.4 2.8 concatenate.50
  554.5 8.8 %multiply_subtract_fusion = (f32[144,6912]{1,0:T(8,128)}, f32[144,6912]{1,0:T(8,128)}, f32[144,6912]{1,0:T(8,128)}) fusion(f32[144,6912]{1,0:T(8,128)} %param.26, f32[144,4608]{1,0:T(8,128)S(1)} %fusion.64, f32[144,2304]{1,0:T(8,128)S(1)} %fusion.74, f32[144,6912]{1,0:T(8,128)} %param.27, f32[144,6912]{1,0:T(8,128)} %param.28), kind=kLoop, calls=%fused_computation.31 | loop fusion | flops 15925248 | bytes 27869184 | tf_op jit(solution)/shard_map/sub | solution.py:217
  (276 shorter events, 73.4 us)
Async XLA Ops:
  7.2 498.1 %all-gather.4.cloned.1.call-start = ((), (), s32[]{:S(2)}) async-start(), calls=%async_computation | async-start | bytes 2433024 | tf_op jit(solution)/shard_map/all_gather | solution.py:1210
  8.1 253.8 %copy-start.28 = (s32[768]{0:T(1024)}, s32[768]{0:T(1024)S(1)}, u32[]{:S(2)}) copy-start(s32[768]{0:T(1024)S(1)} %reduce.11) | copy-start | bytes 9220
  209.2 6.5 %copy-start = (f32[768,1152]{1,0:T(8,128)S(1)}, f32[768,1152]{1,0:T(8,128)}, u32[]{:S(2)}) copy-start(f32[768,1152]{1,0:T(8,128)} %get-tuple-element.59) | copy-start | bytes 10616836
  217.9 16.4 %copy-start.25 = (bf16[768,1152]{1,0:T(8,128)(2,1)}, bf16[768,1152]{1,0:T(8,128)(2,1)S(1)}, u32[]{:S(2)}) copy-start(bf16[768,1152]{1,0:T(8,128)(2,1)S(1)} %get-tuple-element.148.feed) | copy-start | bytes 5308420
  218.0 7.4 %copy-start.72 = (f32[768,1152]{1,0:T(8,128)S(1)}, f32[768,1152]{1,0:T(8,128)}, u32[]{:S(2)}) copy-start(f32[768,1152]{1,0:T(8,128)} %get-tuple-element.67) | copy-start | bytes 10616836
  218.0 7.4 %copy-start.84 = (bf16[2,4,144,1152]{3,2,1,0:T(8,128)(2,1)S(1)}, bf16[2,4,144,1152]{3,2,1,0:T(8,128)(2,1)}, u32[]{:S(2)}) copy-start(bf16[2,4,144,1152]{3,2,1,0:T(8,128)(2,1)} %get-tuple-element.68) | copy-start | bytes 7962628
  225.4 21.9 %copy-start.89 = (bf16[768,1152]{1,0:T(8,128)(2,1)}, bf16[768,1152]{1,0:T(8,128)(2,1)S(1)}, u32[]{:S(2)}) copy-start(bf16[768,1152]{1,0:T(8,128)(2,1)S(1)} %get-tuple-element.150.b3) | copy-start | bytes 5308420
  229.9 14.6 %copy-start.86 = (bf16[768,1152]{1,0:T(8,128)(2,1)}, bf16[768,1152]{1,0:T(8,128)(2,1)S(1)}, u32[]{:S(2)}) copy-start(bf16[768,1152]{1,0:T(8,128)(2,1)S(1)} %get-tuple-element.152.b2) | copy-start | bytes 5308420
  234.4 7.4 %copy-start.87 = (bf16[768,1152]{1,0:T(8,128)(2,1)}, bf16[768,1152]{1,0:T(8,128)(2,1)S(1)}, u32[]{:S(2)}) copy-start(bf16[768,1152]{1,0:T(8,128)(2,1)S(1)} %get-tuple-element.154.b1) | copy-start | bytes 5308420
  255.2 14.6 %copy-start.30 = (bf16[4,1152]{1,0:T(4,128)(2,1)}, bf16[4,1152]{1,0:T(4,128)(2,1)S(1)}, u32[]{:S(2)}) copy-start(bf16[4,1152]{1,0:T(4,128)(2,1)S(1)} %fusion.87) | copy-start | bytes 27652
  274.0 196.7 %copy-start.76 = (bf16[8,144,1152]{2,1,0:T(8,128)(2,1)S(1)}, bf16[8,144,1152]{2,1,0:T(8,128)(2,1)}, u32[]{:S(2)}) copy-start(bf16[8,144,1152]{2,1,0:T(8,128)(2,1)} %get-tuple-element.84) | copy-start | bytes 7962628
  491.8 6.4 %copy-start.18 = (f32[768,1152]{1,0:T(8,128)S(1)}, f32[768,1152]{1,0:T(8,128)}, u32[]{:S(2)}) copy-start(f32[768,1152]{1,0:T(8,128)} %get-tuple-element.146) | copy-start | bytes 10616836
  505.3 16.3 %collective-permute-start = (bf16[16,1152]{1,0:T(8,128)(2,1)}, bf16[16,1152]{1,0:T(8,128)(2,1)}, u32[]{:S(2)}, u32[]{:S(2)}) collective-permute-start(bf16[16,1152]{1,0:T(8,128)(2,1)} %pad.13), channel_id=1, source_target_pairs={{0,8},{4,12},{8,16},{12,20},{16,24},{20,28},{24,0},{28,4},{1,9},{5... | collective-permute-start | bytes 110600 | tf_op jit(solution)/shard_map/ppermute | solution.py:38
  505.3 16.3 %collective-permute-start.1 = (bf16[16,1152]{1,0:T(8,128)(2,1)}, bf16[16,1152]{1,0:T(8,128)(2,1)}, u32[]{:S(2)}, u32[]{:S(2)}) collective-permute-start(bf16[16,1152]{1,0:T(8,128)(2,1)} %pad.13), channel_id=1, source_target_pairs={{0,16},{4,20},{8,24},{12,28},{16,0},{20,4},{24,8},{28,12},{1,17},{... | collective-permute-start | bytes 110600 | tf_op jit(solution)/shard_map/ppermute | solution.py:38
  508.2 13.3 %collective-permute-start.2 = (bf16[16,1152]{1,0:T(8,128)(2,1)}, bf16[16,1152]{1,0:T(8,128)(2,1)}, u32[]{:S(2)}, u32[]{:S(2)}) collective-permute-start(bf16[16,1152]{1,0:T(8,128)(2,1)} %pad.13), channel_id=1, source_target_pairs={{0,24},{4,28},{8,0},{12,4},{16,8},{20,12},{24,16},{28,20},{1,25},{... | collective-permute-start | bytes 110600 | tf_op jit(solution)/shard_map/ppermute | solution.py:38
  516.0 12.9 %copy-start.7 = (f32[576,1152]{1,0:T(8,128)S(1)}, f32[576,1152]{1,0:T(8,128)}, u32[]{:S(2)}) copy-start(f32[576,1152]{1,0:T(8,128)} %param.38) | copy-start | bytes 7962628
  516.0 12.9 %copy-start.10 = (f32[576,1152]{1,0:T(8,128)S(1)}, f32[576,1152]{1,0:T(8,128)}, u32[]{:S(2)}) copy-start(f32[576,1152]{1,0:T(8,128)} %bitcast_convert_fusion) | copy-start | bytes 7962628
  522.4 5.6 collective-permute-start.3
  528.1 9.7 %copy-start.9 = (f32[144,4608]{1,0:T(8,128)S(1)}, f32[144,4608]{1,0:T(8,128)}, u32[]{:S(2)}) copy-start(f32[144,4608]{1,0:T(8,128)} %param.35) | copy-start | bytes 7962628
  528.1 9.7 %copy-start.11 = (f32[144,4608]{1,0:T(8,128)S(1)}, f32[144,4608]{1,0:T(8,128)}, u32[]{:S(2)}) copy-start(f32[144,4608]{1,0:T(8,128)} %maximum_convert_fusion) | copy-start | bytes 7962628
  528.1 9.7 %copy-start.19 = (f32[144,4608]{1,0:T(8,128)S(1)}, f32[144,4608]{1,0:T(8,128)}, u32[]{:S(2)}) copy-start(f32[144,4608]{1,0:T(8,128)} %param.36) | copy-start | bytes 7962628
  528.1 8.4 %collective-permute-start.4 = (bf16[8,16,1152]{2,1,0:T(8,128)(2,1)S(1)}, bf16[8,16,1152]{2,1,0:T(8,128)(2,1)S(1)}, u32[]{:S(2)}, u32[]{:S(2)}) collective-permute-start(bf16[8,16,1152]{2,1,0:T(8,128)(2,1)S(1)} %pad_maximum_fusion.3), channel_id=1, source_target_pairs={{0,2},{1,3},{2,0},{3,1},{4,6},{5,7},{6,4},{7,5},{8,10},{9,11},{10,... | collective-permute-start | bytes 884744 | tf_op jit(solution)/shard_map/ppermute | solution.py:42
  536.6 7.7 %collective-permute-start.5 = (bf16[16,16,1152]{2,1,0:T(8,128)(2,1)S(1)}, bf16[16,16,1152]{2,1,0:T(8,128)(2,1)S(1)}, u32[]{:S(2)}, u32[]{:S(2)}) collective-permute-start(bf16[16,16,1152]{2,1,0:T(8,128)(2,1)S(1)} %pad_maximum_fusion.2), channel_id=1, source_target_pairs={{0,1},{1,0},{2,3},{3,2},{4,5},{5,4},{6,7},{7,6},{8,9},{9,8},{10,11... | collective-permute-start | bytes 1769480 | tf_op jit(solution)/shard_map/ppermute | solution.py:46
  554.5 8.8 %copy-start.24 = (bf16[768,1152]{1,0:T(8,128)(2,1)S(1)}, bf16[768,1152]{1,0:T(8,128)(2,1)}, u32[]{:S(2)}) copy-start(bf16[768,1152]{1,0:T(8,128)(2,1)} %get-tuple-element.199) | copy-start | bytes 5308420
  (73 other events, 232.3 us)
Sparse Core Ops, SparseCore 0:
  272.5 65.2 all-gather.3
